TPU v7x, 512 devices: a whole 4x4x16 slice. The times are simulated.
512 devices in a mesh: stream: 16 (over z), vert: 8 (over y, core), span: 4 (over x).
Axes of the slice: x: 4, y: 4, z: 16, core: 2. Of those that a mesh axis runs over, the one named last changes fastest.
Arguments:
- forcing: float32 [128, 128, 512], P('stream', 'vert', 'span'), may hold values from -6 to 6
- geometry: float32 [4, 16, 16, 64], P(None, 'stream', 'vert', 'span'), may hold values from 0.02 to 0.2
- wall_elem: int32 [512, 64], P(('stream', 'vert', 'span')), may hold values from 0 to 31
- wall_face: int32 [512, 64], P(('stream', 'vert', 'span')), may hold values from 0 to 5
- wall_store: int32 [512, 64], P(('stream', 'vert', 'span')), may hold values from 0 to 4, as said below
- wall_weight: float32 [512, 4096], P(('stream', 'vert', 'span')), may hold values from 0.00034526698 to 0.0013810679
- wall_arm: float32 [512, 3, 4096], P(('stream', 'vert', 'span')), may hold values from -6 to 6
- store_motion: float32 [6, 4], replicated, may hold values from -6 to 6
- store_inverse: float32 [4, 4], replicated, may hold values from 1 to 4
Outputs:
- pressure: float32 [128, 128, 512], P('stream', 'vert', 'span')
- mesh_velocity: float32 [512, 3, 4096], P(('stream', 'vert', 'span'))
Inputs may be any that keep to these rules, and one draw needn't show every extreme that they name: `wall_store`: on each device the live slots come first; some device has all 64 slots live and some has none.
All inputs are finite; a program needn't handle non-finite values.
Results may differ from a plain program's by a relative error of at most 0.0003.
Values sent between devices are 32-bit elements; how exact they have to be, the bound alone decides.
No kernel may reach another device: no remote copies, remote signals or barrier semaphores. Data moves between devices by JAX's collectives and lax.ppermute only.
A program may use at most 64 MiB of HBM per device.

v0:
```python
import jax
import jax.numpy as jnp
import numpy as np
from jax import lax
from jax.sharding import PartitionSpec as P

ITERS = 2


precise = lax.Precision.HIGHEST
gll_inner = [
    -0.8717401485096066,
    -0.5917001814331423,
    -0.2092992179024789,
    0.2092992179024789,
    0.5917001814331423,
    0.8717401485096066,
]


def extended(block, sides, width):
    for axis, dim in sides:
        count = lax.axis_size(axis)
        forward = [(i, i + 1) for i in range(count - 1)]
        backward = [(target, source) for source, target in forward]
        low = lax.ppermute(
            lax.slice_in_dim(block, block.shape[dim] - width, None, axis=dim), axis, forward
        )
        high = lax.ppermute(lax.slice_in_dim(block, 0, width, axis=dim), axis, backward)
        block = jnp.concatenate([low, block, high], axis=dim)
    return block


def legendre_seven(points):
    before = points * 0.0 + 1.0
    current = points * 1.0
    for order in range(1, 7):
        following = ((2 * order + 1) * points * current - order * before) / (order + 1)
        before = current
        current = following
    return current


def gll_tables():
    degree = 7
    points = np.array([-1.0] + gll_inner + [1.0])
    legendre_at = legendre_seven(points)
    weights = 2.0 / (degree * (degree + 1) * legendre_at**2)
    derivative = np.zeros((8, 8))
    for i in range(8):
        for j in range(8):
            if i != j:
                derivative[i, j] = legendre_at[i] / (legendre_at[j] * (points[i] - points[j]))
    derivative[0, 0] = -degree * (degree + 1) / 4.0
    derivative[7, 7] = degree * (degree + 1) / 4.0
    return (jnp.asarray(derivative, dtype=jnp.float32), jnp.asarray(weights, dtype=jnp.float32))


def apply_local(field, geometry, derivative, weights):
    ex, ey, ez = (geometry.shape[1], geometry.shape[2], geometry.shape[3])
    blocks = field.reshape(ex, 8, ey, 8, ez, 8)
    cube = weights[:, None, None] * weights[None, :, None] * weights[None, None, :]
    cube = cube[None, :, None, :, None, :]

    def scaled(node_values, factor):
        return node_values * (factor[:, None, :, None, :, None] * cube)

    grad_a = jnp.einsum("pi,aibjck->apbjck", derivative, blocks, precision=precise)
    grad_b = jnp.einsum("pj,aibjck->aibpck", derivative, blocks, precision=precise)
    grad_c = jnp.einsum("pk,aibjck->aibjcp", derivative, blocks, precision=precise)
    total = jnp.einsum(
        "pi,apbjck->aibjck", derivative, scaled(grad_a, geometry[0]), precision=precise
    )
    total = total + jnp.einsum(
        "pj,aibpck->aibjck", derivative, scaled(grad_b, geometry[1]), precision=precise
    )
    total = total + jnp.einsum(
        "pk,aibjcp->aibjck", derivative, scaled(grad_c, geometry[2]), precision=precise
    )
    total = total + scaled(blocks, 50.0 * geometry[3])
    return total.reshape(field.shape)


def add_along(padded, axis):
    size = padded.shape[axis] - 2
    before = lax.slice_in_dim(padded, 0, size, axis=axis)
    centre = lax.slice_in_dim(padded, 1, size + 1, axis=axis)
    after = lax.slice_in_dim(padded, 2, size + 2, axis=axis)
    position = lax.broadcasted_iota(jnp.int32, centre.shape, axis) % 8
    return centre + jnp.where(position == 0, before, 0.0) + jnp.where(position == 7, after, 0.0)


def assemble(field):
    field = add_along(extended(field, (("stream", 0),), 1), 0)
    field = add_along(extended(field, (("vert", 1),), 1), 1)
    return add_along(extended(field, (("span", 2),), 1), 2)


def face_values(field, elems, faces, ey, ez):

    def one_block(elem):
        corner_x = elem // (ey * ez) * 8
        vertical_corner = elem // ez % ey * 8
        spanwise_corner = elem % ez * 8
        return lax.dynamic_slice(field, (corner_x, vertical_corner, spanwise_corner), (8, 8, 8))

    blocks = jax.vmap(one_block)(elems)
    count = elems.shape[0]
    sides = jnp.stack(
        [
            blocks[:, 0],
            blocks[:, 7],
            blocks[:, :, 0],
            blocks[:, :, 7],
            blocks[:, :, :, 0],
            blocks[:, :, :, 7],
        ],
        axis=1,
    )
    sides = sides.reshape(count, 6, 64)
    pick = (jnp.arange(6, dtype=jnp.int32)[None, :] == faces[:, None]).astype(field.dtype)
    return jnp.sum(sides * pick[:, :, None], axis=1).reshape(count * 64)


def cross(left, right):
    return jnp.stack(
        [
            left[1] * right[2] - left[2] * right[1],
            left[2] * right[0] - left[0] * right[2],
            left[0] * right[1] - left[1] * right[0],
        ]
    )


def store_onehot(stores, count_stores, dtype):
    store_rows = jnp.repeat(stores, 64)
    return (jnp.arange(count_stores, dtype=jnp.int32)[:, None] == store_rows[None, :]).astype(dtype)


def wall_loads(node_values, faces, stores, weights, arms, count_stores):
    face_rows = jnp.repeat(faces, 64)
    sign = (2 * (face_rows % 2) - 1).astype(node_values.dtype)
    direction = face_rows // 2
    push = -node_values * weights * sign
    traction = jnp.stack([jnp.where(direction == comp, push, 0.0) for comp in range(3)])
    loads = jnp.concatenate([traction, cross(arms, traction)], axis=0)
    onehot = store_onehot(stores, count_stores, node_values.dtype)
    return jnp.einsum("lr,sr->ls", loads, onehot, precision=precise)


def rigid_motion(totals, motion, inverse, stores, arms):
    onehot = store_onehot(stores, motion.shape[1], totals.dtype)
    linear = motion[0:3] + inverse[0:1] * totals[0:3]
    angular = motion[3:6] + inverse[1:4] * totals[3:6]
    linear_rows = jnp.einsum("cs,sr->cr", linear, onehot, precision=precise)
    angular_rows = jnp.einsum("cs,sr->cr", angular, onehot, precision=precise)
    return linear_rows + cross(angular_rows, arms)


def per_device(
    forcing,
    geometry,
    wall_elem,
    wall_face,
    wall_store,
    wall_weight,
    wall_arm,
    store_motion,
    store_inverse,
):
    derivative, weights = gll_tables()
    inverse_mult = 1.0 / assemble(jnp.ones_like(forcing))
    right = assemble(forcing)

    def squares(residual):
        return lax.psum(jnp.sum(residual * residual * inverse_mult), ("stream", "vert", "span"))

    pressure = jnp.zeros_like(forcing)
    residual = right
    direction = right
    norm_now = squares(residual)
    for step in range(ITERS):
        image = assemble(apply_local(direction, geometry, derivative, weights))
        curve = lax.psum(jnp.sum(direction * image * inverse_mult), ("stream", "vert", "span"))
        alpha = norm_now / curve
        pressure = pressure + alpha * direction
        residual = residual - alpha * image
        if step + 1 < ITERS:
            norm_next = squares(residual)
            direction = residual + norm_next / norm_now * direction
            norm_now = norm_next
    node_values = face_values(
        pressure, wall_elem[0], wall_face[0], geometry.shape[2], geometry.shape[3]
    )
    partial_value = wall_loads(
        node_values, wall_face[0], wall_store[0], wall_weight[0], wall_arm[0], store_motion.shape[1]
    )
    totals = lax.psum(partial_value, ("stream", "vert", "span"))
    mesh_velocity = rigid_motion(totals, store_motion, store_inverse, wall_store[0], wall_arm[0])
    return (pressure, mesh_velocity[None])


def solution(mesh):
    return jax.shard_map(
        per_device,
        mesh=mesh,
        in_specs=(
            P("stream", "vert", "span"),
            P(None, "stream", "vert", "span"),
            P(("stream", "vert", "span"), None),
            P(("stream", "vert", "span"), None),
            P(("stream", "vert", "span"), None),
            P(("stream", "vert", "span"), None),
            P(("stream", "vert", "span"), None, None),
            P(),
            P(),
        ),
        out_specs=(P("stream", "vert", "span"), P(("stream", "vert", "span"), None, None)),
        check_vma=False,
    )
```

profile of v0, /device:TPU:1, one launch (start us, length us, event | category | flops | bytes accessed | tf_op | source)
XLA Modules:
  0.0 676.4 jit_solution(2011171923673687992)
XLA Ops:
  1.2 4.9 collective-permute-start.6
  8.2 4.0 collective-permute-start
  17.6 5.8 collective-permute-start.2
  23.4 3.0 collective-permute-start.3
  26.4 1.9 collective-permute-done.3
  28.5 3.1 collective-permute-start.4
  33.0 3.6 collective-permute-done.5
  39.5 7.4 %convolution_multiply_fusion.1 = f32[8,2,8,16,8]{3,4,2,1,0:T(8,128)S(1)} fusion(f32[8,2,8,16,8]{4,3,2,1,0:T(8,128)S(1)} %reshape.597, f32[8,8,1,1,1]{1,0,4,3,2:T(8,128)S(1)} %copy-done.2, f32[8,8,8]{2,1,0:T(8,128)S(1)} %copy.77, f32[2,16]{1,0:T(2,128)S(1)} %get-tuple-element.67), kind=kOutput, calls=%fused_computation.7 | convolution fusion | flops 1605632 | bytes 133504 | tf_op jit(solution)/shard_map/pk,aibjck->aibjcp/dot_general | solution.py:70
  51.8 4.0 collective-permute-start.12
  58.2 4.0 collective-permute-done.13
  63.1 4.6 collective-permute-start.14
  67.7 1.9 collective-permute-start.15
  69.6 3.6 collective-permute-start.8
  73.3 1.9 collective-permute-start.9
  75.2 3.0 collective-permute-done.9
  78.4 3.1 collective-permute-start.10
  82.9 4.0 collective-permute-start.16
  88.2 3.8 collective-permute-done.17
  92.9 108.3 %all-reduce.2 = (f32[]{:T(128)}, f32[]{:T(128)}) all-reduce(f32[]{:T(128)} %get-tuple-element.17, f32[]{:T(128)} %get-tuple-element.16), channel_id=1, replica_groups=mesh['stream'=16,'vert'=8,'span'=4] {'stream','vert','span'}, use_global_device_ids=true, to_apply=%region_1.2 | all-reduce | flops 2 | bytes 16 | tf_op jit(solution)/shard_map/psum | solution.py:176
  203.8 98.6 %psum.37 = f32[]{:T(128)} all-reduce(f32[]{:T(128)} %multiply_reduce_fusion.1), channel_id=1, replica_groups=mesh['stream'=16,'vert'=8,'span'=4] {'stream','vert','span'}, use_global_device_ids=true, to_apply=%region_5.6 | all-reduce | flops 1 | bytes 8 | tf_op jit(solution)/shard_map/psum | solution.py:176
  304.8 7.4 %convolution_multiply_fusion = f32[8,2,8,16,8]{3,4,2,1,0:T(8,128)S(1)} fusion(f32[8,2,8,16,8]{4,3,2,1,0:T(8,128)S(1)} %reshape.602, f32[8,8,1,1,1]{1,0,4,3,2:T(8,128)S(1)} %copy-done.2, f32[8,8,8]{2,1,0:T(8,128)S(1)} %copy.77, f32[2,16]{1,0:T(2,128)S(1)} %copy-done.13), kind=kOutput, calls=%fused_computation.4 | convolution fusion | flops 1605632 | bytes 133504 | tf_op jit(solution)/shard_map/pk,aibjck->aibjcp/dot_general | solution.py:70
  318.1 3.7 collective-permute-start.18
  324.9 1.5 collective-permute-done.19
  326.5 4.6 collective-permute-start.20
  331.1 1.9 collective-permute-start.21
  333.1 3.0 collective-permute-done.21
  337.5 1.5 collective-permute-start.23
  339.3 3.6 collective-permute-done.23
  343.8 101.1 %psum.38 = f32[]{:T(128)} all-reduce(f32[]{:T(128)} %fusion.48), channel_id=1, replica_groups=mesh['stream'=16,'vert'=8,'span'=4] {'stream','vert','span'}, use_global_device_ids=true, to_apply=%region_7.8 | all-reduce | flops 1 | bytes 8 | tf_op jit(solution)/shard_map/psum | solution.py:184
  446.4 125.5 %while.1 = (s32[]{:T(128)}, f32[8,16,128]{2,1,0:T(8,128)S(1)}, s32[64,3]{0,1:T(4,128)S(1)}, f32[64,8,8,8]{3,2,1,0:T(8,128)S(1)}, s32[]{:T(128)}) while((s32[]{:T(128)}, f32[8,16,128]{2,1,0:T(8,128)S(1)}, s32[64,3]{0,1:T(4,128)S(1)}, f32[64,8,8,8]{3,2,1,0:T(8,128)S(1)}, s32[]{:T(128)}) %tuple.56), condition=%wide.while_cond, body=%wide.while_body.sunk | while | flops 2 | bytes 65653 | solution.py:105
  447.0 1.3 bitcast_dynamic-update-slice_fusion.2
  449.0 1.3 bitcast_dynamic-update-slice_fusion.2
  450.9 1.3 bitcast_dynamic-update-slice_fusion.2
  454.9 1.3 bitcast_dynamic-update-slice_fusion.2
  456.8 1.3 bitcast_dynamic-update-slice_fusion.2
  460.7 1.3 bitcast_dynamic-update-slice_fusion.2
  462.7 1.3 bitcast_dynamic-update-slice_fusion.2
  464.7 1.3 bitcast_dynamic-update-slice_fusion.2
  466.6 1.3 bitcast_dynamic-update-slice_fusion.2
  468.6 1.3 bitcast_dynamic-update-slice_fusion.2
  470.5 1.3 bitcast_dynamic-update-slice_fusion.2
  472.5 1.3 bitcast_dynamic-update-slice_fusion.2
  474.5 1.3 bitcast_dynamic-update-slice_fusion.2
  476.4 1.3 bitcast_dynamic-update-slice_fusion.2
  478.4 1.3 bitcast_dynamic-update-slice_fusion.2
  480.3 1.3 bitcast_dynamic-update-slice_fusion.2
  482.3 1.3 bitcast_dynamic-update-slice_fusion.2
  484.3 1.3 bitcast_dynamic-update-slice_fusion.2
  486.2 1.3 bitcast_dynamic-update-slice_fusion.2
  488.2 1.3 bitcast_dynamic-update-slice_fusion.2
  492.1 1.3 bitcast_dynamic-update-slice_fusion.2
  494.1 1.3 bitcast_dynamic-update-slice_fusion.2
  498.0 1.3 bitcast_dynamic-update-slice_fusion.2
  500.0 1.3 bitcast_dynamic-update-slice_fusion.2
  501.9 1.3 bitcast_dynamic-update-slice_fusion.2
  503.9 1.3 bitcast_dynamic-update-slice_fusion.2
  505.8 1.3 bitcast_dynamic-update-slice_fusion.2
  507.8 1.3 bitcast_dynamic-update-slice_fusion.2
  509.8 1.3 bitcast_dynamic-update-slice_fusion.2
  511.7 1.3 bitcast_dynamic-update-slice_fusion.2
  513.7 1.3 bitcast_dynamic-update-slice_fusion.2
  515.6 1.3 bitcast_dynamic-update-slice_fusion.2
  517.6 1.3 bitcast_dynamic-update-slice_fusion.2
  576.5 98.5 %psum.39 = f32[6,4]{0,1:T(4,128)S(1)} all-reduce(f32[6,4]{0,1:T(4,128)S(1)} %fusion.70), channel_id=1, replica_groups=mesh['stream'=16,'vert'=8,'span'=4] {'stream','vert','span'}, use_global_device_ids=true, to_apply=%region_9.10 | all-reduce | flops 24 | bytes 192 | tf_op jit(solution)/shard_map/psum | solution.py:198
  (361 shorter events, 126.1 us)
Async XLA Ops:
  1.2 57.0 %collective-permute-start.6 = (f32[1,16,128]{2,1,0:T(8,128)}, f32[1,16,128]{2,1,0:T(8,128)}, u32[]{:S(2)}, u32[]{:S(2)}) collective-permute-start(f32[1,16,128]{2,1,0:T(8,128)} %broadcast.652), channel_id=1, source_target_pairs={{0,32},{32,64},{64,96},{96,128},{128,160},{160,192},{192,224},{224... | collective-permute-start | bytes 24584 | tf_op jit(solution)/shard_map/ppermute | solution.py:26
  6.2 52.0 %collective-permute-start.7 = (f32[1,16,128]{2,1,0:T(8,128)}, f32[1,16,128]{2,1,0:T(8,128)}, u32[]{:S(2)}, u32[]{:S(2)}) collective-permute-start(f32[1,16,128]{2,1,0:T(8,128)} %broadcast.652), channel_id=1, source_target_pairs={{32,0},{64,32},{96,64},{128,96},{160,128},{192,160},{224,192},{256... | collective-permute-start | bytes 24584 | tf_op jit(solution)/shard_map/ppermute | solution.py:29
  8.2 8.2 %collective-permute-start = (f32[1,16,128]{2,1,0:T(8,128)S(1)}, f32[1,16,128]{2,1,0:T(8,128)S(1)}, u32[]{:S(2)}, u32[]{:S(2)}) collective-permute-start(f32[1,16,128]{2,1,0:T(8,128)S(1)} %get-tuple-element.62), channel_id=1, source_target_pairs={{0,32},{32,64},{64,96},{96,128},{128,160},{160,192},{192,224},{224... | collective-permute-start | bytes 24584 | tf_op jit(solution)/shard_map/ppermute | solution.py:26
  12.2 4.4 collective-permute-start.1
  13.5 14.8 %copy-start.23 = (s32[8]{0:T(128)}, s32[8]{0:T(128)S(1)}, u32[]{:S(2)}) copy-start(s32[8]{0:T(128)S(1)} %get-tuple-element.75) | copy-start | bytes 100
  13.5 14.8 %copy-start.26 = (s32[8]{0:T(128)}, s32[8]{0:T(128)S(1)}, u32[]{:S(2)}) copy-start(s32[8]{0:T(128)S(1)} %get-tuple-element.76) | copy-start | bytes 100
  13.5 14.8 %copy-start.29 = (pred[8]{0:T(512)(128)(4,1)}, pred[8]{0:T(512)(128)(4,1)S(1)}, u32[]{:S(2)}) copy-start(pred[8]{0:T(512)(128)(4,1)S(1)} %compare_and_fusion.2) | copy-start | bytes 28
  13.5 14.8 %copy-start.14 = (s32[16]{0:T(128)}, s32[16]{0:T(128)S(1)}, u32[]{:S(2)}) copy-start(s32[16]{0:T(128)S(1)} %get-tuple-element.77) | copy-start | bytes 196
  13.5 14.8 %copy-start.17 = (s32[16]{0:T(128)}, s32[16]{0:T(128)S(1)}, u32[]{:S(2)}) copy-start(s32[16]{0:T(128)S(1)} %get-tuple-element.78) | copy-start | bytes 196
  13.6 14.8 %copy-start.20 = (pred[16]{0:T(512)(128)(4,1)}, pred[16]{0:T(512)(128)(4,1)S(1)}, u32[]{:S(2)}) copy-start(pred[16]{0:T(512)(128)(4,1)S(1)} %compare_and_fusion.1) | copy-start | bytes 52
  16.4 23.1 %copy-start.12 = (f32[2,16]{1,0:T(2,128)}, f32[2,16]{1,0:T(2,128)S(1)}, u32[]{:S(2)}) copy-start(f32[2,16]{1,0:T(2,128)S(1)} %get-tuple-element.67) | copy-start | bytes 388
  16.4 33.9 %copy-start.6 = (f32[2,16]{1,0:T(2,128)}, f32[2,16]{1,0:T(2,128)S(1)}, u32[]{:S(2)}) copy-start(f32[2,16]{1,0:T(2,128)S(1)} %get-tuple-element.64) | copy-start | bytes 388
  17.6 8.7 %collective-permute-start.2 = (f32[8,1,128]{2,1,0:T(1,128)S(1)}, f32[8,1,128]{2,1,0:T(1,128)S(1)}, u32[]{:S(2)}, u32[]{:S(2)}) collective-permute-start(f32[8,1,128]{2,1,0:T(1,128)S(1)} %get-tuple-element.60), channel_id=1, source_target_pairs={{0,4},{4,8},{8,12},{12,16},{16,20},{20,24},{24,28},{1,5},{5,9},{9,... | collective-permute-start | bytes 12296 | tf_op jit(solution)/shard_map/ppermute | solution.py:26
  23.4 4.9 collective-permute-start.3
  28.5 4.5 collective-permute-start.4
  31.6 5.0 collective-permute-start.5
  37.3 2.1 copy-start.2
  39.4 8.1 %copy-start = (f32[8,2,8,16,8]{3,2,4,1,0:T(8,128)S(1)}, f32[8,2,8,16,8]{3,2,4,1,0:T(8,128)}, u32[]{:S(2)}) copy-start(f32[8,2,8,16,8]{3,2,4,1,0:T(8,128)} %copy.71) | copy-start | bytes 196612
  39.4 8.6 %copy-start.10 = (f32[2,16]{1,0:T(2,128)S(1)}, f32[2,16]{1,0:T(2,128)}, u32[]{:S(2)}) copy-start(f32[2,16]{1,0:T(2,128)} %get-tuple-element.65) | copy-start | bytes 388
  48.1 1.6 copy-start.8
  51.4 10.8 %copy-start.24 = (s32[8]{0:T(128)S(1)}, s32[8]{0:T(128)}, u32[]{:S(2)}) copy-start(s32[8]{0:T(128)} %copy-done.23) | copy-start | bytes 100
  51.4 10.8 %copy-start.27 = (s32[8]{0:T(128)S(1)}, s32[8]{0:T(128)}, u32[]{:S(2)}) copy-start(s32[8]{0:T(128)} %copy-done.26) | copy-start | bytes 100
  51.4 10.8 %copy-start.30 = (pred[8]{0:T(512)(128)(4,1)S(1)}, pred[8]{0:T(512)(128)(4,1)}, u32[]{:S(2)}) copy-start(pred[8]{0:T(512)(128)(4,1)} %copy-done.29) | copy-start | bytes 28
  51.5 26.7 %copy-start.15 = (s32[16]{0:T(128)S(1)}, s32[16]{0:T(128)}, u32[]{:S(2)}) copy-start(s32[16]{0:T(128)} %copy-done.14) | copy-start | bytes 196
  51.5 26.7 %copy-start.18 = (s32[16]{0:T(128)S(1)}, s32[16]{0:T(128)}, u32[]{:S(2)}) copy-start(s32[16]{0:T(128)} %copy-done.17) | copy-start | bytes 196
  51.5 26.7 %copy-start.21 = (pred[16]{0:T(512)(128)(4,1)S(1)}, pred[16]{0:T(512)(128)(4,1)}, u32[]{:S(2)}) copy-start(pred[16]{0:T(512)(128)(4,1)} %copy-done.20) | copy-start | bytes 52
  51.8 6.4 collective-permute-start.12
  56.0 147.2 %copy-start.32 = (s32[1,64]{1,0:T(1,128)S(1)}, s32[1,64]{1,0:T(1,128)}, u32[]{:S(2)}) copy-start(s32[1,64]{1,0:T(1,128)} %param.14) | copy-start | bytes 772
  56.0 6.2 collective-permute-start.13
  63.1 12.1 %collective-permute-start.14 = (f32[8,1,128]{2,1,0:T(1,128)S(1)}, f32[8,1,128]{2,1,0:T(1,128)S(1)}, u32[]{:S(2)}, u32[]{:S(2)}) collective-permute-start(f32[8,1,128]{2,1,0:T(1,128)S(1)} %get-tuple-element.52), channel_id=1, source_target_pairs={{0,4},{4,8},{8,12},{12,16},{16,20},{20,24},{24,28},{1,5},{5,9},{9,... | collective-permute-start | bytes 12296 | tf_op jit(solution)/shard_map/ppermute | solution.py:26
  67.7 7.5 %collective-permute-start.15 = (f32[8,1,128]{2,1,0:T(1,128)S(1)}, f32[8,1,128]{2,1,0:T(1,128)S(1)}, u32[]{:S(2)}, u32[]{:S(2)}) collective-permute-start(f32[8,1,128]{2,1,0:T(1,128)S(1)} %get-tuple-element.53), channel_id=1, source_target_pairs={{4,0},{8,4},{12,8},{16,12},{20,16},{24,20},{28,24},{5,1},{9,5},{13... | collective-permute-start | bytes 12296 | tf_op jit(solution)/shard_map/ppermute | solution.py:29
  69.6 5.6 collective-permute-start.8
  73.3 4.9 collective-permute-start.9
  78.4 9.8 %collective-permute-start.10 = (f32[8,16,1]{2,1,0:T(8,128)S(1)}, f32[8,16,1]{2,1,0:T(8,128)S(1)}, u32[]{:S(2)}, u32[]{:S(2)}) collective-permute-start(f32[8,16,1]{2,1,0:T(8,128)S(1)} %get-tuple-element.54), channel_id=1, source_target_pairs={{0,1},{1,2},{2,3},{4,5},{5,6},{6,7},{8,9},{9,10},{10,11},{12,13},{... | collective-permute-start | bytes 1544 | tf_op jit(solution)/shard_map/ppermute | solution.py:26
  81.5 6.7 collective-permute-start.11
  82.9 221.9 %copy-start.13 = (f32[2,16]{1,0:T(2,128)S(1)}, f32[2,16]{1,0:T(2,128)}, u32[]{:S(2)}) copy-start(f32[2,16]{1,0:T(2,128)} %copy-done.12) | copy-start | bytes 388
  82.9 5.3 collective-permute-start.16
  86.9 5.2 collective-permute-start.17
  312.2 1.5 copy-start.11
  313.2 2.4 copy-start.9
  315.0 1.6 copy-start.7
  317.7 8.7 %copy-start.25 = (s32[8]{0:T(128)S(1)}, s32[8]{0:T(128)}, u32[]{:S(2)}) copy-start(s32[8]{0:T(128)} %copy-done.23) | copy-start | bytes 100
  317.7 8.7 %copy-start.28 = (s32[8]{0:T(128)S(1)}, s32[8]{0:T(128)}, u32[]{:S(2)}) copy-start(s32[8]{0:T(128)} %copy-done.26) | copy-start | bytes 100
  317.7 8.7 %copy-start.31 = (pred[8]{0:T(512)(128)(4,1)S(1)}, pred[8]{0:T(512)(128)(4,1)}, u32[]{:S(2)}) copy-start(pred[8]{0:T(512)(128)(4,1)} %copy-done.29) | copy-start | bytes 28
  317.7 15.3 %copy-start.37 = (s32[1,64]{1,0:T(1,128)S(1)}, s32[1,64]{1,0:T(1,128)}, u32[]{:S(2)}) copy-start(s32[1,64]{1,0:T(1,128)} %param.13) | copy-start | bytes 772
  317.7 18.3 %copy-start.16 = (s32[16]{0:T(128)S(1)}, s32[16]{0:T(128)}, u32[]{:S(2)}) copy-start(s32[16]{0:T(128)} %copy-done.14) | copy-start | bytes 196
  317.7 18.3 %copy-start.19 = (s32[16]{0:T(128)S(1)}, s32[16]{0:T(128)}, u32[]{:S(2)}) copy-start(s32[16]{0:T(128)} %copy-done.17) | copy-start | bytes 196
  317.8 18.3 %copy-start.22 = (pred[16]{0:T(512)(128)(4,1)S(1)}, pred[16]{0:T(512)(128)(4,1)}, u32[]{:S(2)}) copy-start(pred[16]{0:T(512)(128)(4,1)} %copy-done.20) | copy-start | bytes 52
  317.8 21.3 %copy-start.35 = (f32[4,4]{1,0:T(4,128)S(1)}, f32[4,4]{1,0:T(4,128)}, u32[]{:S(2)}) copy-start(f32[4,4]{1,0:T(4,128)} %param.19) | copy-start | bytes 196
  317.8 21.3 %copy-start.33 = (s32[1,64]{1,0:T(1,128)S(1)}, s32[1,64]{1,0:T(1,128)}, u32[]{:S(2)}) copy-start(s32[1,64]{1,0:T(1,128)} %param.14) | copy-start | bytes 772
  318.0 25.7 %copy-start.36 = (s32[1,64]{1,0:T(1,128)S(1)}, s32[1,64]{1,0:T(1,128)}, u32[]{:S(2)}) copy-start(s32[1,64]{1,0:T(1,128)} %param.15) | copy-start | bytes 772
  318.1 6.8 %collective-permute-start.18 = (f32[1,16,128]{2,1,0:T(8,128)S(1)}, f32[1,16,128]{2,1,0:T(8,128)S(1)}, u32[]{:S(2)}, u32[]{:S(2)}) collective-permute-start(f32[1,16,128]{2,1,0:T(8,128)S(1)} %slice.300), channel_id=1, source_target_pairs={{0,32},{32,64},{64,96},{96,128},{128,160},{160,192},{192,224},{224... | collective-permute-start | bytes 24584 | tf_op jit(solution)/shard_map/ppermute | solution.py:26
  322.0 4.4 collective-permute-start.19
  326.5 6.6 collective-permute-start.20
  331.1 4.9 collective-permute-start.21
  336.2 3.0 collective-permute-start.22
  337.5 5.3 collective-permute-start.23
  571.8 2.4 copy-start.1
  572.9 2.6 copy-start.4
  574.2 1.5 copy-start.3
  574.2 1.5 copy-start.5
  574.2 100.8 %copy-start.34 = (f32[6,4]{0,1:T(4,128)S(1)}, f32[6,4]{0,1:T(4,128)}, u32[]{:S(2)}) copy-start(f32[6,4]{0,1:T(4,128)} %param.18) | copy-start | bytes 292
where the time goes:
time: 679 us; the launch traced here: 676 us
  blocking collectives  407 us (60%)
  local copies, waits for them, and re-layouts  141 us (21%)
  starting transfers between devices  65.9 us (10%)
  waiting for transfers between devices  24.6 us (4%)
  matrix products  23.2 us (3%)
  other arithmetic  9.36 us (1%)
    psum x2, blocking collectives, squares(): lax.psum(jnp.sum(residual * residual * inverse_mult), ('stream', 'vert',...  207 us
    gather x192, local copies, waits for them, and re-layouts  125 us
    psum x1, blocking collectives, per_device(): lax.psum(jnp.sum(direction * image * inverse_mult), ('stream', 'vert', 's...  101 us
    psum x1, blocking collectives, per_device(): totals = lax.psum(partial_value, ('stream', 'vert', 'span'))  98.5 us
    ppermute x12, starting transfers between devices, extended(): lax.ppermute(lax.slice_in_dim(block, block.shape[dim] - width, None, axis...  46.7 us
    ppermute x12, waiting for transfers between devices, extended(): lax.ppermute(lax.slice_in_dim(block, 0, width, axis=dim), axis, backward)  24.6 us
    ppermute x12, starting transfers between devices, extended(): lax.ppermute(lax.slice_in_dim(block, 0, width, axis=dim), axis, backward)  19.3 us
    dot_general x2, matrix products, apply_local(): jnp.einsum('pk,aibjck->aibjcp', derivative, blocks, precision=precise)  14.8 us
  transfers between devices with their start and end apart: 24, of which 9 were waited for; matrix products, arithmetic and copies ran while one was open for 3% of the time, Pallas kernels for 0%

commit v1 on v0

v1 whole, which is shorter than its diff:
```python
import functools

import jax
import jax.numpy as jnp
import numpy as np
from jax import lax
from jax.experimental import pallas as pl
from jax.experimental.pallas import tpu as pltpu
from jax.sharding import PartitionSpec as P

F32 = jnp.float32
AXES = ("stream", "vert", "span")
SHARDS = P(AXES, None)
gll_inner = [
    -0.8717401485096066,
    -0.5917001814331423,
    -0.2092992179024789,
    0.2092992179024789,
    0.5917001814331423,
    0.8717401485096066,
]
MOMENTS = (((1, 2, 1.0), (2, 1, -1.0)), ((0, 2, -1.0), (2, 0, 1.0)), ((0, 1, 1.0), (1, 0, -1.0)))


def legendre_seven(points):
    before = points * 0.0 + 1.0
    current = points * 1.0
    for order in range(1, 7):
        following = ((2 * order + 1) * points * current - order * before) / (order + 1)
        before = current
        current = following
    return current


def gll_tables():
    degree = 7
    points = np.array([-1.0] + gll_inner + [1.0])
    legendre_at = legendre_seven(points)
    weights = 2.0 / (degree * (degree + 1) * legendre_at**2)
    derivative = np.zeros((8, 8))
    for i in range(8):
        for j in range(8):
            if i != j:
                derivative[i, j] = legendre_at[i] / (legendre_at[j] * (points[i] - points[j]))
    derivative[0, 0] = -degree * (degree + 1) / 4.0
    derivative[7, 7] = degree * (degree + 1) / 4.0
    return derivative, weights


DERIV, WEIGHTS = gll_tables()
STIFF = DERIV.T @ np.diag(WEIGHTS) @ DERIV


def constants():
    def f32(a):
        return np.asarray(a, np.float32)

    lane_k = f32(np.kron(np.eye(16), STIFF))
    lane_i = f32(np.kron(np.eye(2), np.kron(STIFF, np.eye(8))))
    rows = f32(np.kron(np.eye(32), STIFF))
    wj = np.tile(WEIGHTS[:, None], (1, 128))
    wk = np.tile(np.tile(WEIGHTS, 16)[None], (8, 1))
    wi = np.tile(np.tile(np.repeat(WEIGHTS, 8), 2)[None], (8, 1))
    return lane_k, lane_i, rows, f32(np.concatenate([wj, wk, wi], axis=0))


def dot(a, b):
    return lax.dot_general(
        a,
        b,
        (((1,), (0,)), ((), ())),
        precision=lax.Precision.HIGHEST,
        preferred_element_type=F32,
    )


def lane_sums(rows):
    return lax.dot_general(
        jnp.ones((8, 128), F32),
        rows,
        (((1,), (1,)), ((), ())),
        precision=lax.Precision.HIGHEST,
        preferred_element_type=F32,
    )


def row_ids():
    return lax.broadcasted_iota(jnp.int32, (8, 128), 0)


def lane_ids(rows=8):
    return lax.broadcasted_iota(jnp.int32, (rows, 128), 1)


def join_rows(below, above):
    row = row_ids()
    new_below = below + jnp.where(row == 7, pltpu.roll(above, 7, 0), 0.0)
    new_above = above + jnp.where(row == 0, pltpu.roll(below, 1, 0), 0.0)
    return new_below, new_above


def join_lanes(tile):
    lane = lane_ids()
    k = lane % 8
    left = jnp.where((k == 0) & (lane > 0), pltpu.roll(tile, 1, 1), 0.0)
    right = jnp.where((k == 7) & (lane < 127), pltpu.roll(tile, 127, 1), 0.0)
    return tile + left + right


def call(body, outs, cost=2000, **kwargs):
    vmem = pl.BlockSpec(memory_space=pltpu.VMEM)

    def run(*args, smem=0):
        specs = [pl.BlockSpec(memory_space=pltpu.SMEM)] * smem + [vmem] * (len(args) - smem)
        return pl.pallas_call(
            body,
            out_shape=[jax.ShapeDtypeStruct(s, F32) for s in outs],
            in_specs=specs,
            out_specs=[vmem] * len(outs),
            compiler_params=pltpu.CompilerParams(vmem_limit_bytes=16 * 2**20),
            cost_estimate=pl.CostEstimate(flops=cost * 1000, bytes_accessed=200000, transcendentals=0),
            **kwargs,
        )(*args)

    return run


def stream_added(f_ref, low_ref, high_ref, geo_ref, x_ref, up_ref, down_ref):
    for i in range(8):
        a = f_ref[i, 0:8, :]
        b = f_ref[i, 8:16, :]
        if i == 0:
            a = a + low_ref[0:8, :]
            b = b + low_ref[8:16, :]
        if i == 7:
            a = a + high_ref[0:8, :]
            b = b + high_ref[8:16, :]
        a, b = join_rows(a, b)
        x_ref[i, 0:8, :] = a
        x_ref[i, 8:16, :] = b
        down_ref[8 * i : 8 * i + 8, :] = a
        up_ref[8 * i : 8 * i + 8, :] = b
    down_ref[64:72, :] = geo_ref[...]
    up_ref[64:72, :] = geo_ref[...]


def vert_added(x_ref, low_ref, high_ref, geo_ref, v_ref, g_ref, right_ref, left_ref):
    v = lax.axis_index("vert")
    has_low = jnp.where(v > 0, 1.0, 0.0)
    has_high = jnp.where(v < 7, 1.0, 0.0)
    lane = lane_ids()
    right = [jnp.zeros((8, 128), F32) for _ in range(4)]
    left = [jnp.zeros((8, 128), F32) for _ in range(4)]
    for i in range(8):
        rows = slice(8 * i, 8 * i + 8)
        low, a = join_rows(low_ref[rows, :] * has_low, x_ref[i, 0:8, :])
        b, high = join_rows(x_ref[i, 8:16, :], high_ref[rows, :] * has_high)
        for t, tile in enumerate((low, a, b, high)):
            tile = join_lanes(tile)
            v_ref[i, 8 * t : 8 * t + 8, :] = tile
            to_right = pltpu.roll(tile, (8 * i - 120) % 128, 1)
            to_left = pltpu.roll(tile, 64 + 8 * i, 1)
            right[t] = jnp.where(lane // 8 == i, to_right, right[t])
            left[t] = jnp.where(lane // 8 == 8 + i, to_left, left[t])
    for t in range(4):
        right_ref[8 * t : 8 * t + 8, :] = right[t]
        left_ref[8 * t : 8 * t + 8, :] = left[t]
    geo = geo_ref[...]
    geo_low = low_ref[64:72, :] * has_low
    geo_high = high_ref[64:72, :] * has_high
    rows = []
    for d in range(4):
        rows.append(geo_low[2 * d + 1 : 2 * d + 2, :])
        rows.append(geo[2 * d : 2 * d + 2, :])
        rows.append(geo_high[2 * d : 2 * d + 1, :])
    extended = jnp.concatenate(rows, axis=0)
    g_ref[...] = extended
    wide = lane_ids(16)
    last = jnp.broadcast_to(extended[:, 127:128], (16, 128))
    first = jnp.broadcast_to(extended[:, 0:1], (16, 128))
    right_ref[32:48, :] = jnp.where(wide < 64, last, 0.0)
    left_ref[32:48, :] = jnp.where(wide >= 64, first, 0.0)


def node_rows(geo, d, t):
    return jnp.broadcast_to(geo[4 * d + t : 4 * d + t + 1, :], (8, 128))


def span_added(
    v_ref, g_ref, right_ref, left_ref, low_ref, high_ref, kk_ref, ki_ref, kr_ref, w_ref,
    v0_ref, local_ref, part_ref, top_ref, bottom_ref, maps_ref, field,
):
    lane = lane_ids()
    wj, wk, wi = w_ref[0:8, :], w_ref[8:16, :], w_ref[16:24, :]
    got = [low_ref[8 * t : 8 * t + 8, :] + high_ref[8 * t : 8 * t + 8, :] for t in range(4)]
    halo = []
    for t in range(4):
        rows = slice(8 * t, 8 * t + 8)
        from_own_first = pltpu.roll(left_ref[rows, :], 71, 1)
        from_own_last = pltpu.roll(right_ref[rows, :], 57, 1)
        tile = got[t] + jnp.where((lane < 64) & (lane % 8 == 7), from_own_first, 0.0)
        halo.append(tile + jnp.where((lane >= 64) & (lane % 8 == 0), from_own_last, 0.0))
    own = [[None] * 4 for _ in range(8)]
    for i in range(8):
        for t in range(4):
            first = pltpu.roll(got[t], (-(8 * i + 7)) % 128, 1)
            last = pltpu.roll(got[t], (63 - 8 * i) % 128, 1)
            tile = v_ref[i, 8 * t : 8 * t + 8, :]
            tile = tile + jnp.where(lane == 0, first, 0.0) + jnp.where(lane == 127, last, 0.0)
            own[i][t] = tile
            field[32 * i + 8 * t : 32 * i + 8 * t + 8, :] = tile
        v0_ref[i, 0:8, :] = own[i][1]
        v0_ref[i, 8:16, :] = own[i][2]
    for t in range(4):
        field[256 + 8 * t : 264 + 8 * t, :] = halo[t]
    along_k = dot(field[...], kk_ref[...])
    along_j = dot(kr_ref[...], field[0:256, :])
    halo_j = dot(kr_ref[0:32, 0:32], field[256:288, :])
    halo_i = dot(field[256:288, :], ki_ref[...])

    geo = g_ref[...]
    geo_halo = low_ref[32:48, :] + high_ref[32:48, :]
    out = [[None] * 4 for _ in range(8)]
    out_halo = []
    for t in range(4):
        g0, g1, g2, g3 = [node_rows(geo, d, t) for d in range(4)]
        f0, f1, f2, f3 = g0 * wj * wk, g1 * wk, g2 * wj, 50.0 * g3 * wj * wk
        if t in (1, 2):
            for d, f in enumerate((f0, f1, f2, f3)):
                maps_ref[d, 8 * t - 8 : 8 * t, :] = f
        for i in range(8):
            along_i = own[0][t] * float(STIFF[i, 0])
            for q in range(1, 8):
                along_i = along_i + own[q][t] * float(STIFF[i, q])
            at = slice(32 * i + 8 * t, 32 * i + 8 * t + 8)
            inner = f1 * along_j[at, :] + f2 * along_k[at, :] + f3 * own[i][t]
            out[i][t] = f0 * along_i + float(WEIGHTS[i]) * inner
        h0, h1, h2, h3 = [node_rows(geo_halo, d, t) for d in range(4)]
        at = slice(8 * t, 8 * t + 8)
        total = h0 * wj * wk * halo_i[at, :] + h1 * wi * wk * halo_j[at, :]
        total = total + h2 * wi * wj * along_k[256 + 8 * t : 264 + 8 * t, :]
        out_halo.append(total + 50.0 * h3 * wi * wj * wk * halo[t])

    row = row_ids()

    def middle(tiles):
        low, a, b, high = tiles
        new_a = a + jnp.where(row == 0, pltpu.roll(low, 1, 0), 0.0) + jnp.where(row == 7, pltpu.roll(b, 7, 0), 0.0)
        new_b = b + jnp.where(row == 0, pltpu.roll(a, 1, 0), 0.0) + jnp.where(row == 7, pltpu.roll(high, 7, 0), 0.0)
        return new_a, new_b

    beside = middle(out_halo)
    for i in range(8):
        local_ref[i, 0:8, :] = out[i][1]
        local_ref[i, 8:16, :] = out[i][2]
        for b, tile in enumerate(middle(out[i])):
            tile = join_lanes(tile)
            first = pltpu.roll(beside[b], (-(8 * i + 7)) % 128, 1)
            last = pltpu.roll(beside[b], (63 - 8 * i) % 128, 1)
            tile = tile + jnp.where(lane == 0, first, 0.0) + jnp.where(lane == 127, last, 0.0)
            part_ref[i, 8 * b : 8 * b + 8, :] = tile
            if i == 7:
                top_ref[8 * b : 8 * b + 8, :] = tile
            if i == 0:
                bottom_ref[8 * b : 8 * b + 8, :] = tile


def share_maps():
    s, v, w = [lax.axis_index(a) for a in AXES]
    row, lane = row_ids(), lane_ids()
    k = lane % 8
    shared = ((k == 0) & ((lane > 0) | (w > 0))) | ((k == 7) & ((lane < 127) | (w < 3)))
    span = jnp.where(shared, 0.5, 1.0)
    first = ((row == 0) & (v > 0)) | (row == 7)
    second = (row == 0) | ((row == 7) & (v < 7))
    tiles = (jnp.where(first, 0.5, 1.0) * span, jnp.where(second, 0.5, 1.0) * span)
    low = jnp.where(s > 0, 0.5, 1.0)
    high = jnp.where(s < 15, 0.5, 1.0)
    return tiles, [low] + [1.0] * 6 + [high]


def face_tiles(tiles):
    lane, row = lane_ids(), row_ids()
    out = []
    for side in range(2):
        out += [tiles[7 * side][0], tiles[7 * side][1]]
    for side in range(2):
        for b in range(2):
            tile = jnp.zeros((8, 128), F32)
            for i in range(8):
                tile = jnp.where(row == i, pltpu.roll(tiles[i][b], (i - 7 * side) % 8, 0), tile)
            out.append(tile)
    for side in range(2):
        for b in range(2):
            tile = jnp.zeros((8, 128), F32)
            for i in range(8):
                tile = jnp.where(lane % 8 == i, pltpu.roll(tiles[i][b], (i - 7 * side) % 128, 1), tile)
            out.append(tile)
    return out


def load_rows(faces, omega_ref):
    sums = [[None] * 4 for _ in range(6)]
    for d in range(3):
        targets = [(d, 1.0)] + [(3 + c, sign) for c, _, sign in MOMENTS[d]]
        for q, (component, sign) in enumerate(targets):
            for store in range(4):
                total = None
                for face in (2 * d, 2 * d + 1):
                    for b in range(2):
                        term = omega_ref[((2 * face + b) * 5 + store) * 3 + q] * faces[2 * face + b]
                        total = term if total is None else total + term
                total = total * sign
                before = sums[component][store]
                sums[component][store] = total if before is None else before + total
    return [jnp.sum(sums[c][s], axis=0, keepdims=True) for c in range(6) for s in range(4)]


def zero_rows(n):
    return [jnp.zeros((n, 128), F32)]


def sublane_sum(tile):
    return jnp.sum(tile, axis=0, keepdims=True)


def before_image(v0_ref, local_ref, part_ref, omega_ref, pre_ref):
    share, layers = share_maps()
    norm = energy = top = bottom = jnp.zeros((8, 128), F32)
    tiles = [[v0_ref[i, 0:8, :], v0_ref[i, 8:16, :]] for i in range(8)]
    for i in range(8):
        for b in range(2):
            x = tiles[i][b]
            square = x * x * share[b]
            norm = norm + square * layers[i]
            energy = energy + x * local_ref[i, 8 * b : 8 * b + 8, :]
            if 0 < i < 7:
                bottom = bottom + square
                top = top + x * part_ref[i, 8 * b : 8 * b + 8, :] * share[b]
    rows = [sublane_sum(norm), sublane_sum(energy)] + zero_rows(6)
    rows += load_rows(face_tiles(tiles), omega_ref)
    rows += [sublane_sum(top), sublane_sum(bottom)] + zero_rows(94)
    sums = lane_sums(jnp.concatenate(rows, axis=0))
    lane = lane_ids()
    over, under = sums[:, 32:33], sums[:, 33:34]
    usable = under > 1e-30
    quotient = jnp.where(usable, over / jnp.where(usable, under, 1.0), 0.0)
    quotient = jnp.broadcast_to(jnp.clip(quotient, 0.0, 1e6), (8, 128))
    pre_ref[...] = jnp.where(lane == 2, quotient, jnp.where(lane < 32, sums, 0.0))


def image_sums(
    v0_ref, local_ref, part_ref, low_ref, high_ref, maps_ref, omega_ref, pre_ref, kk_ref, kr_ref,
    v1_ref, out_ref, field,
):
    share, layers = share_maps()
    quotient = jnp.broadcast_to(pre_ref[:, 2:3], (8, 128))
    v1 = [[None] * 2 for _ in range(8)]
    u = [[None] * 2 for _ in range(8)]
    norm = cross_norm = energy = cross_energy = jnp.zeros((8, 128), F32)
    for i in range(8):
        for b in range(2):
            rows = slice(8 * b, 8 * b + 8)
            tile = part_ref[i, rows, :]
            if i == 0:
                tile = tile + low_ref[rows, :]
            if i == 7:
                tile = tile + high_ref[rows, :]
            v1[i][b] = tile
            v1_ref[i, rows, :] = tile
            x = v0_ref[i, rows, :]
            y = tile - quotient * x
            u[i][b] = y
            field[16 * i + 8 * b : 16 * i + 8 * b + 8, :] = y
            weighted = y * share[b] * layers[i]
            norm = norm + y * weighted
            cross_norm = cross_norm + x * weighted
            cross_energy = cross_energy + y * local_ref[i, rows, :]
    along_k = dot(field[...], kk_ref[...])
    along_j = dot(kr_ref[0:128, 0:128], field[...])
    for b in range(2):
        rows = slice(8 * b, 8 * b + 8)
        f0, f1, f2, f3 = [maps_ref[d, rows, :] for d in range(4)]
        for i in range(8):
            along_i = u[0][b] * float(STIFF[i, 0])
            for q in range(1, 8):
                along_i = along_i + u[q][b] * float(STIFF[i, q])
            at = slice(16 * i + 8 * b, 16 * i + 8 * b + 8)
            inner = f1 * along_j[at, :] + f2 * along_k[at, :] + f3 * u[i][b]
            energy = energy + u[i][b] * (f0 * along_i + float(WEIGHTS[i]) * inner)
    rows = zero_rows(3) + [sublane_sum(a) for a in (norm, cross_norm, energy, cross_energy)] + zero_rows(25)
    rows += load_rows(face_tiles(v1), omega_ref) + zero_rows(72)
    sums = lane_sums(jnp.concatenate(rows, axis=0)) + pre_ref[...]
    out_ref[...] = jnp.broadcast_to(sums[0:1, :][None], (32, 1, 128))


def merged(parts, last):
    m, q, s, uu, g, ulu, t = [parts[:, n : n + 1] for n in range(7)]

    def add(a):
        return jnp.sum(a, axis=0, keepdims=True)

    m_all, q_all = add(m), add(q)
    if last:
        common = q_all / m_all
    else:
        usable = m_all > 0.0
        common = jnp.where(usable, add(m * s) / jnp.where(usable, m_all, 1.0), 0.0)
    e = s - common
    uu_all = add(uu + e * (2.0 * g + e * m))
    g_all = add(g + e * m)
    ulu_all = add(ulu + e * (2.0 * t + e * q))
    t_all = add(t + e * q)
    return m_all, q_all, common, uu_all, g_all, ulu_all, t_all, add(parts)


def group_sums(parts_ref, out_ref):
    parts = parts_ref[...].reshape(parts_ref.shape[0], 128)
    values = merged(parts, False)
    row = values[7]
    lane = lane_ids(1)
    for n in range(7):
        row = jnp.where(lane == n, values[n], row)
    out_ref[...] = jnp.broadcast_to(row[None], out_ref.shape)


def finish(parts_ref, v0_ref, v1_ref, arm_ref, store_ref, motion_ref, p_ref, velocity_ref):
    parts = parts_ref[...].reshape(parts_ref.shape[0], 128)
    m, q, _, uu, _, ulu, _, sums = merged(parts, True)
    alpha = m / q
    beta = alpha * alpha * uu / m
    new = alpha * alpha * uu
    curve = alpha * alpha * ulu - beta * beta * q
    alpha_next = new / curve
    c0 = alpha + alpha_next * (1.0 + beta)
    c1 = -alpha_next * alpha
    for i in range(8):
        p_ref[i] = c0 * v0_ref[i] + c1 * v1_ref[i]
    loads = c0 * sums + c1 * pltpu.roll(sums, 104, 1)
    state = motion_ref[0:1, :] + motion_ref[1:2, :] * loads
    stores = store_ref[...]
    zero = jnp.zeros((32, 128), F32)
    maps = []
    for c in range(6):
        total = zero
        for store in range(4):
            at = 8 + 4 * c + store
            total = jnp.where(stores == store, state[:, at : at + 1], total)
        maps.append(total)
    arms = [arm_ref[c] for c in range(3)]
    for c in range(3):
        a, b = (c + 1) % 3, (c + 2) % 3
        value = maps[c] + (maps[3 + a] * arms[b] - maps[3 + b] * arms[a])
        for r in range(32):
            velocity_ref[0, c : c + 1, 128 * r : 128 * r + 128] = value[r : r + 1, :]


def wall_weights(elem_ref, face_ref, store_ref, node_ref, spread_ref, omega_ref, spread):
    spread[...] = dot(node_ref[...], spread_ref[...])
    omega_ref[...] = jnp.zeros(omega_ref.shape, F32)
    lane = lane_ids() // 8

    def add(n, carry):
        elem, face, store = elem_ref[0, n], face_ref[0, n], store_ref[0, n]
        tile = (2 * face + elem // 16) * 5 + store
        here = lane == elem % 16
        for q in range(3):
            at = pl.multiple_of((q * 64 + n) * 8, 8)
            omega_ref[tile * 3 + q] += jnp.where(here, spread[pl.ds(at, 8), :], 0.0)
        return carry

    lax.fori_loop(0, 64, add, 0)


def shifted(x, axis, step, ring=False):
    count = lax.axis_size(axis)
    pairs = [(i, (i + step) % count) for i in range(count) if ring or 0 <= i + step < count]
    return lax.ppermute(x, axis, pairs)


def per_device(
    forcing, geometry, wall_elem, wall_face, wall_store, wall_weight, wall_arm, store_motion, store_inverse
):
    lane_k, lane_i, rows, node_w = [jnp.asarray(a) for a in constants()]
    field = (8, 16, 128)

    low = shifted(forcing[7], "stream", 1)
    high = shifted(forcing[0], "stream", -1)

    geo = jnp.repeat(geometry.reshape(8, 16), 8, axis=1)
    face = wall_face[0]
    sign = (1 - 2 * (face % 2)).astype(F32)[:, None]
    weight = wall_weight[0].reshape(64, 64) * sign
    arms = wall_arm[0].reshape(3, 64, 64)
    direction = (face // 2)[:, None]
    first = jnp.where(direction == 2, arms[1], arms[2])
    second = jnp.where(direction == 0, arms[1], arms[0])
    nodes = jnp.stack([weight, weight * first, weight * second]).reshape(3, 64, 8, 8)
    nodes = jnp.where((direction == 2)[None, :, :, None], jnp.swapaxes(nodes, 2, 3), nodes)
    spread = jnp.asarray(np.kron(np.ones((1, 16)), np.eye(8)).astype(np.float32))
    omega = call(wall_weights, [(180, 8, 128)], cost=4000, scratch_shapes=[pltpu.VMEM((1536, 128), F32)])(
        wall_elem, wall_face, wall_store, nodes.reshape(1536, 8), spread, smem=3
    )[0]
    arm_rows = wall_arm[0].reshape(3, 32, 128)
    store_rows = jnp.repeat(wall_store[0], 64).reshape(32, 128)
    zeros8, zeros96 = jnp.zeros((8,), F32), jnp.zeros((96,), F32)
    scale = jnp.concatenate([store_inverse[0:1]] * 3 + [store_inverse[1:4]], axis=0)
    motion = jnp.stack(
        [
            jnp.concatenate([zeros8, store_motion.reshape(24), zeros96]),
            jnp.concatenate([zeros8, scale.reshape(24), zeros96]),
        ]
    )

    x, up, down = call(stream_added, [field, (72, 128), (72, 128)])(forcing, low, high, geo)
    low = shifted(up, "vert", 1, ring=True)
    high = shifted(down, "vert", -1, ring=True)
    wide, geo_wide, right, left = call(vert_added, [(8, 32, 128), (16, 128), (48, 128), (48, 128)])(
        x, low, high, geo
    )
    low = shifted(right, "span", 1)
    high = shifted(left, "span", -1)
    v0, local, part, top, bottom, maps = call(
        span_added,
        [field, field, field, (16, 128), (16, 128), (4, 16, 128)],
        scratch_shapes=[pltpu.VMEM((288, 128), F32)],
    )(wide, geo_wide, right, left, low, high, lane_k, lane_i, rows, node_w)
    low = shifted(top, "stream", 1)
    high = shifted(bottom, "stream", -1)
    pre = call(before_image, [(8, 128)])(v0, local, part, omega)[0]
    v1, sums = call(image_sums, [field, (32, 1, 128)], scratch_shapes=[pltpu.VMEM((128, 128), F32)])(
        v0, local, part, low, high, maps, omega, pre, lane_k, rows
    )
    sums = lax.all_to_all(sums, ("vert", "span"), 0, 0)
    sums = call(group_sums, [(16, 1, 128)])(sums)[0]
    sums = lax.all_to_all(sums, "stream", 0, 0)
    pressure, velocity = call(finish, [field, (1, 3, 4096)])(sums, v0, v1, arm_rows, store_rows, motion)
    return pressure, velocity


def solution(mesh):
    return jax.shard_map(
        per_device,
        mesh=mesh,
        in_specs=(
            P("stream", "vert", "span"),
            P(None, "stream", "vert", "span"),
            SHARDS,
            SHARDS,
            SHARDS,
            SHARDS,
            P(AXES, None, None),
            P(),
            P(),
        ),
        out_specs=(P("stream", "vert", "span"), P(AXES, None, None)),
        check_vma=False,
    )
```

time: 679 us -> 83.6 us (0.12)
  blocking collectives: 407 us -> 0 us
  local copies, waits for them, and re-layouts: 141 us -> 6.82 us
  matrix products: 23.2 us -> 0 us
  starting transfers between devices: 65.9 us -> 45.2 us
  other arithmetic: 9.36 us -> 2.02 us
    psum x4 -> x0, blocking collectives: 407 us -> none  [the longest x2 207 us: squares(): lax.psum(jnp.sum(residual * residual * inverse_mult), ('stream', 'vert',...]
    gather x195 -> x0, local copies, waits for them, and re-layouts: 129 us -> none
    ppermute x24 -> x8, starting transfers between devices: 65.9 us -> 19.7 us  [shifted(): return lax.ppermute(x, axis, pairs)]
    all_to_all x0 -> x2, starting transfers between devices: none -> 25.5 us  [the longest x1 17.6 us: per_device(): sums = lax.all_to_all(sums, 'stream', 0, 0)]
    dot_general x15 -> x0, matrix products: 23.2 us -> none  [the longest x2 14.8 us: apply_local(): jnp.einsum('pk,aibjck->aibjcp', derivative, blocks, precision=precise)]
    ppermute x24 -> x8, waiting for transfers between devices: 24.6 us -> 4.48 us  [shifted(): return lax.ppermute(x, axis, pairs)]
    all_to_all x0 -> x2, waiting for transfers between devices: none -> 16.5 us  [the longest x1 9.73 us: per_device(): sums = lax.all_to_all(sums, 'stream', 0, 0)]
  transfers between devices with their start and end apart: 24 -> 10, of which waited for: 9 -> 5; matrix products, arithmetic and copies ran while one was open for 3% -> 7% of each run, Pallas kernels for 0% -> 3%
where the time goes in v1:
time: 83.6 us; the launch traced here: 82.8 us
  starting transfers between devices  45.2 us (54%)
  waiting for transfers between devices  21 us (25%)
  local copies, waits for them, and re-layouts  6.82 us (8%)
  Pallas kernels  6.77 us (8%)
  other arithmetic  2.02 us (2%)
  between operations  1.02 us (1%)
    ppermute x8, starting transfers between devices, shifted(): return lax.ppermute(x, axis, pairs)  19.7 us
    all_to_all x1, starting transfers between devices, per_device(): sums = lax.all_to_all(sums, 'stream', 0, 0)  17.6 us
    all_to_all x1, waiting for transfers between devices, per_device(): sums = lax.all_to_all(sums, 'stream', 0, 0)  9.73 us
    all_to_all x1, starting transfers between devices, per_device(): sums = lax.all_to_all(sums, ('vert', 'span'), 0, 0)  7.9 us
    pallas_call x8, Pallas kernels, run(): pl.pallas_call(body, out_shape=[jax.ShapeDtypeStruct(s, F32) for s in out...  6.77 us
    all_to_all x1, waiting for transfers between devices, per_device(): sums = lax.all_to_all(sums, ('vert', 'span'), 0, 0)  6.75 us
    ppermute x8, waiting for transfers between devices, shifted(): return lax.ppermute(x, axis, pairs)  4.48 us
    unnamed x31, local copies, waits for them, and re-layouts  3.06 us
  transfers between devices with their start and end apart: 10, of which 5 were waited for; matrix products, arithmetic and copies ran while one was open for 7% of the time, Pallas kernels for 3%

profile of v1, /device:TPU:1, one launch (start us, length us, event | category | flops | bytes accessed | tf_op | source)
XLA Modules:
  0.0 82.8 jit_solution(7995422571125172245)
XLA Ops:
  0.6 0.7 slice_bitcast_fusion
  1.3 4.5 %collective-permute-start = (f32[16,128]{1,0:T(8,128)S(1)}, f32[16,128]{1,0:T(8,128)S(1)}, u32[]{:S(2)}, u32[]{:S(2)}) collective-permute-start(f32[16,128]{1,0:T(8,128)S(1)} %get-tuple-element.48), channel_id=1, source_target_pairs={{0,32},{32,64},{64,96},{96,128},{128,160},{160,192},{192,224},{224... | collective-permute-start | bytes 24584 | tf_op jit(solution)/shard_map/ppermute | solution.py:478
  5.8 1.3 %collective-permute-start.1 = (f32[16,128]{1,0:T(8,128)S(1)}, f32[16,128]{1,0:T(8,128)S(1)}, u32[]{:S(2)}, u32[]{:S(2)}) collective-permute-start(f32[16,128]{1,0:T(8,128)S(1)} %get-tuple-element.47), channel_id=1, source_target_pairs={{32,0},{64,32},{96,64},{128,96},{160,128},{192,160},{224,192},{256... | collective-permute-start | bytes 24584 | tf_op jit(solution)/shard_map/ppermute | solution.py:478
  7.2 0.9 %slice_reduce_fusion.1 = (f32[4096]{0:T(1024)S(1)}, f32[4096]{0:T(1024)S(1)}, f32[4096]{0:T(1024)S(1)}) fusion(f32[1,3,4096]{2,0,1:T(1,128)} %param.20), kind=kLoop, calls=%fused_computation.6 | loop fusion | bytes 98304 | tf_op jit(solution)/shard_map/slice | solution.py:496
  8.1 0.2 squeeze.23
  8.2 0.0 copy-start.10
  8.2 0.2 squeeze.24
  8.4 0.5 broadcast.204
  8.9 0.0 copy-done.10
  9.0 0.7 reduce.18
  9.6 0.2 reshape_squeeze.7
  9.8 0.2 squeeze.25
  10.0 0.2 select_multiply_fusion.1
  10.2 0.0 copy-start.11
  10.2 0.1 select_multiply_fusion
  10.4 0.5 copy-done.11
  10.9 0.1 broadcast_in_dim.37
  11.0 0.1 reshape.232.geo_ref
  11.1 0.0 collective-permute-done.low_ref
  11.1 0.0 collective-permute-done.1.high_ref
  11.1 0.6 copy-done.3
  11.7 2.1 %collective-permute-start.2 = (f32[72,128]{1,0:T(8,128)S(1)}, f32[72,128]{1,0:T(8,128)S(1)}, u32[]{:S(2)}, u32[]{:S(2)}) collective-permute-start(f32[72,128]{1,0:T(8,128)S(1)} %get-tuple-element.18), channel_id=1, source_target_pairs={{0,4},{4,8},{8,12},{12,16},{16,20},{20,24},{24,28},{28,0},{1,5},{5... | collective-permute-start | bytes 110600 | tf_op jit(solution)/shard_map/ppermute | solution.py:478
  13.9 1.7 %collective-permute-start.3 = (f32[72,128]{1,0:T(8,128)S(1)}, f32[72,128]{1,0:T(8,128)S(1)}, u32[]{:S(2)}, u32[]{:S(2)}) collective-permute-start(f32[72,128]{1,0:T(8,128)S(1)} %get-tuple-element.19), channel_id=1, source_target_pairs={{0,28},{4,0},{8,4},{12,8},{16,12},{20,16},{24,20},{28,24},{1,29},{... | collective-permute-start | bytes 110600 | tf_op jit(solution)/shard_map/ppermute | solution.py:478
  15.6 0.1 pad_maximum_fusion
  15.6 0.3 copy.29
  15.9 0.4 collective-permute-done.2.low_ref
  16.3 1.0 %collective-permute-done.3.high_ref = f32[72,128]{1,0:T(8,128)S(1)} collective-permute-done((f32[72,128]{1,0:T(8,128)S(1)}, f32[72,128]{1,0:T(8,128)S(1)}, u32[]{:S(2)}, u32[]{:S(2)}) %collective-permute-start.3) | collective-permute-done | bytes 36896 | tf_op jit(solution)/shard_map/ppermute | solution.py:478
  17.3 0.3 shard_map.150
  17.6 3.1 %collective-permute-start.4 = (f32[48,128]{1,0:T(8,128)S(1)}, f32[48,128]{1,0:T(8,128)S(1)}, u32[]{:S(2)}, u32[]{:S(2)}) collective-permute-start(f32[48,128]{1,0:T(8,128)S(1)} %get-tuple-element.22.right_ref), channel_id=1, source_target_pairs={{0,1},{1,2},{2,3},{4,5},{5,6},{6,7},{8,9},{9,10},{10,11},{12,13},{... | collective-permute-start | bytes 73736 | tf_op jit(solution)/shard_map/ppermute | solution.py:478
  20.7 0.0 copy-start
  20.7 0.0 copy-start.1
  20.7 0.0 copy-start.4
  20.7 1.4 %collective-permute-start.5 = (f32[48,128]{1,0:T(8,128)S(1)}, f32[48,128]{1,0:T(8,128)S(1)}, u32[]{:S(2)}, u32[]{:S(2)}) collective-permute-start(f32[48,128]{1,0:T(8,128)S(1)} %get-tuple-element.23.left_ref), channel_id=1, source_target_pairs={{1,0},{2,1},{3,2},{5,4},{6,5},{7,6},{9,8},{10,9},{11,10},{13,12},{... | collective-permute-start | bytes 73736 | tf_op jit(solution)/shard_map/ppermute | solution.py:478
  22.2 0.0 copy-start.5
  22.2 0.1 bitcast_select_fusion
  22.3 3.1 %collective-permute-done.5.high_ref = f32[48,128]{1,0:T(8,128)S(1)} collective-permute-done((f32[48,128]{1,0:T(8,128)S(1)}, f32[48,128]{1,0:T(8,128)S(1)}, u32[]{:S(2)}, u32[]{:S(2)}) %collective-permute-start.5) | collective-permute-done | bytes 24608 | tf_op jit(solution)/shard_map/ppermute | solution.py:478
  25.5 0.8 shard_map.151
  26.2 0.0 copy-start.13
  26.2 4.3 %collective-permute-start.6 = (f32[16,128]{1,0:T(8,128)S(1)}, f32[16,128]{1,0:T(8,128)S(1)}, u32[]{:S(2)}, u32[]{:S(2)}) collective-permute-start(f32[16,128]{1,0:T(8,128)S(1)} %get-tuple-element.27), channel_id=1, source_target_pairs={{0,32},{32,64},{64,96},{96,128},{128,160},{160,192},{192,224},{224... | collective-permute-start | bytes 24584 | tf_op jit(solution)/shard_map/ppermute | solution.py:478
  30.5 0.0 copy-start.12
  30.5 1.3 %collective-permute-start.7 = (f32[16,128]{1,0:T(8,128)S(1)}, f32[16,128]{1,0:T(8,128)S(1)}, u32[]{:S(2)}, u32[]{:S(2)}) collective-permute-start(f32[16,128]{1,0:T(8,128)S(1)} %get-tuple-element.28), channel_id=1, source_target_pairs={{32,0},{64,32},{96,64},{128,96},{160,128},{192,160},{224,192},{256... | collective-permute-start | bytes 24584 | tf_op jit(solution)/shard_map/ppermute | solution.py:478
  31.9 0.1 copy.30
  32.0 0.1 reshape.234
  32.1 0.1 reshape.235
  32.1 0.6 copy-done.6
  32.7 0.1 copy-done.7
  32.8 0.0 copy-done.9
  32.8 2.3 %shard_map.152.omega_ref = f32[180,8,128]{2,1,0:T(8,128)S(1)} custom-call(s32[1,64]{1,0:T(1,128)S(1)} %copy-done.7, s32[1,64]{1,0:T(1,128)S(1)} %copy-done.8, s32[1,64]{1,0:T(1,128)S(1)} %copy-done.9, f32[1536,8]{1,0:T(8,128)S(1)} %bitcast.29, f32[8,128]{1,0:T(8,128)S(1)} %copy-done.6), custom_call_target="tpu_custom_call" | custom-call | flops 4000000 | bytes 200000 | tf_op jit(solution)/shard_map/pallas_call | solution.py:115
  35.1 0.5 shard_map.153.pre_ref
  35.6 1.2 %shard_map.154 = (f32[8,16,128]{2,1,0:T(8,128)S(1)}, f32[32,1,128]{2,1,0:T(1,128)}) custom-call(f32[8,16,128]{2,1,0:T(8,128)S(1)} %get-tuple-element.24.v0_ref, f32[8,16,128]{2,1,0:T(8,128)S(1)} %get-tuple-element.25.local_ref, f32[8,16,128]{2,1,0:T(8,128)S(1)} %get-tuple-element.26.part_ref, f32[16,128]{1,0:T(8,128)S(1)} %collective-permute-done.6.low_ref, ...), custom_call_target="tpu_custom_call" | custom-call | flops 2000000 | bytes 200000 | tf_op jit(solution)/shard_map/pallas_call | solution.py:115
  36.8 7.9 %all-to-all-start = ((f32[32,1,128]{2,1,0:T(1,128)}), f32[32,1,128]{2,1,0:T(1,128)S(1)}, u32[]{:S(2)}, u32[]{:S(2)}) async-start(f32[32,1,128]{2,1,0:T(1,128)} %get-tuple-element.30), calls=%async_computation | async-start | bytes 32768 | tf_op jit(solution)/shard_map/all_to_all | solution.py:534
  44.7 0.1 fusion
  44.8 6.8 %all-to-all-done.parts_ref = f32[32,1,128]{2,1,0:T(1,128)S(1)} async-done(((f32[32,1,128]{2,1,0:T(1,128)}), f32[32,1,128]{2,1,0:T(1,128)S(1)}, u32[]{:S(2)}, u32[]{:S(2)}) %all-to-all-start) | async-done | bytes 16416 | tf_op jit(solution)/shard_map/all_to_all | solution.py:534
  51.6 0.8 shard_map.155
  52.4 17.6 %all-to-all-start.1 = ((f32[16,1,128]{2,1,0:T(1,128)}), f32[16,1,128]{2,1,0:T(1,128)S(1)}, u32[]{:S(2)}, u32[]{:S(2)}) async-start(f32[16,1,128]{2,1,0:T(1,128)} %shard_map.155), calls=%async_computation.1 | async-start | bytes 16384 | tf_op jit(solution)/shard_map/all_to_all | solution.py:536
  70.0 0.5 broadcast.205
  70.5 0.7 reduce.19
  71.2 0.1 broadcast_in_dim.41
  71.3 0.0 copy-start.2
  71.3 0.1 broadcast_in_dim.42
  71.4 0.1 broadcast_in_dim.43.store_ref
  71.5 9.7 %all-to-all-done.1.parts_ref = f32[16,1,128]{2,1,0:T(1,128)S(1)} async-done(((f32[16,1,128]{2,1,0:T(1,128)}), f32[16,1,128]{2,1,0:T(1,128)S(1)}, u32[]{:S(2)}, u32[]{:S(2)}) %all-to-all-start.1) | async-done | bytes 8224 | tf_op jit(solution)/shard_map/all_to_all | solution.py:536
  81.2 0.9 %shard_map.156 = (f32[8,16,128]{2,1,0:T(8,128)}, f32[1,3,4096]{2,1,0:T(4,128)S(1)}) custom-call(f32[16,1,128]{2,1,0:T(1,128)S(1)} %all-to-all-done.1.parts_ref, f32[8,16,128]{2,1,0:T(8,128)S(1)} %get-tuple-element.24.v0_ref, f32[8,16,128]{2,1,0:T(8,128)S(1)} %get-tuple-element.31.v1_ref, f32[3,32,128]{2,1,0:T(8,128)S(1)} %bitcast.30, ...), custom_call_target="tpu_custom_call" | custom-call | flops 2000000 | bytes 200000 | tf_op jit(solution)/shard_map/pallas_call | solution.py:115
  82.1 0.7 copy.31
  (26 shorter events, 0.1 us)
Async XLA Ops:
  1.3 5.8 %copy-start.8 = (s32[1,64]{1,0:T(1,128)S(1)}, s32[1,64]{1,0:T(1,128)}, u32[]{:S(2)}) copy-start(s32[1,64]{1,0:T(1,128)} %face_ref.1) | copy-start | bytes 772
  1.3 9.7 %collective-permute-start = (f32[16,128]{1,0:T(8,128)S(1)}, f32[16,128]{1,0:T(8,128)S(1)}, u32[]{:S(2)}, u32[]{:S(2)}) collective-permute-start(f32[16,128]{1,0:T(8,128)S(1)} %get-tuple-element.48), channel_id=1, source_target_pairs={{0,32},{32,64},{64,96},{96,128},{128,160},{160,192},{192,224},{224... | collective-permute-start | bytes 24584 | tf_op jit(solution)/shard_map/ppermute | solution.py:478
  5.8 5.2 %collective-permute-start.1 = (f32[16,128]{1,0:T(8,128)S(1)}, f32[16,128]{1,0:T(8,128)S(1)}, u32[]{:S(2)}, u32[]{:S(2)}) collective-permute-start(f32[16,128]{1,0:T(8,128)S(1)} %get-tuple-element.47), channel_id=1, source_target_pairs={{32,0},{64,32},{96,64},{128,96},{160,128},{192,160},{224,192},{256... | collective-permute-start | bytes 24584 | tf_op jit(solution)/shard_map/ppermute | solution.py:478
  8.2 0.7 copy-start.10
  10.2 0.7 copy-start.11
  10.9 0.8 %copy-start.3 = (f32[8,16,128]{2,1,0:T(8,128)S(1)}, f32[8,16,128]{2,1,0:T(8,128)}, u32[]{:S(2)}) copy-start(f32[8,16,128]{2,1,0:T(8,128)} %f_ref.1) | copy-start | bytes 196612
  11.7 4.5 %collective-permute-start.2 = (f32[72,128]{1,0:T(8,128)S(1)}, f32[72,128]{1,0:T(8,128)S(1)}, u32[]{:S(2)}, u32[]{:S(2)}) collective-permute-start(f32[72,128]{1,0:T(8,128)S(1)} %get-tuple-element.18), channel_id=1, source_target_pairs={{0,4},{4,8},{8,12},{12,16},{16,20},{20,24},{24,28},{28,0},{1,5},{5... | collective-permute-start | bytes 110600 | tf_op jit(solution)/shard_map/ppermute | solution.py:478
  13.9 3.4 %collective-permute-start.3 = (f32[72,128]{1,0:T(8,128)S(1)}, f32[72,128]{1,0:T(8,128)S(1)}, u32[]{:S(2)}, u32[]{:S(2)}) collective-permute-start(f32[72,128]{1,0:T(8,128)S(1)} %get-tuple-element.19), channel_id=1, source_target_pairs={{0,28},{4,0},{8,4},{12,8},{16,12},{20,16},{24,20},{28,24},{1,29},{... | collective-permute-start | bytes 110600 | tf_op jit(solution)/shard_map/ppermute | solution.py:478
  17.6 4.8 %collective-permute-start.4 = (f32[48,128]{1,0:T(8,128)S(1)}, f32[48,128]{1,0:T(8,128)S(1)}, u32[]{:S(2)}, u32[]{:S(2)}) collective-permute-start(f32[48,128]{1,0:T(8,128)S(1)} %get-tuple-element.22.right_ref), channel_id=1, source_target_pairs={{0,1},{1,2},{2,3},{4,5},{5,6},{6,7},{8,9},{9,10},{10,11},{12,13},{... | collective-permute-start | bytes 73736 | tf_op jit(solution)/shard_map/ppermute | solution.py:478
  20.7 4.7 %copy-start = (f32[256,256]{1,0:T(8,128)S(1)}, f32[256,256]{1,0:T(8,128)}, u32[]{:S(2)}) copy-start(f32[256,256]{1,0:T(8,128)} %constant.45.clone.kr_ref) | copy-start | bytes 786436
  20.7 4.7 %copy-start.1 = (f32[128,128]{1,0:T(8,128)S(1)}, f32[128,128]{1,0:T(8,128)}, u32[]{:S(2)}) copy-start(f32[128,128]{1,0:T(8,128)} %constant.43.clone.kk_ref) | copy-start | bytes 196612
  20.7 4.7 %copy-start.4 = (f32[128,128]{1,0:T(8,128)S(1)}, f32[128,128]{1,0:T(8,128)}, u32[]{:S(2)}) copy-start(f32[128,128]{1,0:T(8,128)} %constant.44.clone.ki_ref) | copy-start | bytes 196612
  20.7 4.7 %collective-permute-start.5 = (f32[48,128]{1,0:T(8,128)S(1)}, f32[48,128]{1,0:T(8,128)S(1)}, u32[]{:S(2)}, u32[]{:S(2)}) collective-permute-start(f32[48,128]{1,0:T(8,128)S(1)} %get-tuple-element.23.left_ref), channel_id=1, source_target_pairs={{1,0},{2,1},{3,2},{5,4},{6,5},{7,6},{9,8},{10,9},{11,10},{13,12},{... | collective-permute-start | bytes 73736 | tf_op jit(solution)/shard_map/ppermute | solution.py:478
  22.2 3.3 %copy-start.5 = (f32[24,128]{1,0:T(8,128)S(1)}, f32[24,128]{1,0:T(8,128)}, u32[]{:S(2)}) copy-start(f32[24,128]{1,0:T(8,128)} %constant.46.clone.w_ref) | copy-start | bytes 36868
  26.2 5.6 %copy-start.13 = (f32[4,4]{1,0:T(4,128)S(1)}, f32[4,4]{1,0:T(4,128)}, u32[]{:S(2)}) copy-start(f32[4,4]{1,0:T(4,128)} %param.22) | copy-start | bytes 196
  26.2 5.6 %slice-start = ((f32[4,4]{1,0:T(4,128)}), f32[1,4]{1,0:T(1,128)S(1)}, s32[]{:S(2)}) async-start(f32[4,4]{1,0:T(4,128)} %param.22), calls=%async_computation.2 | async-start | bytes 1024 | tf_op jit(solution)/shard_map/slice | solution.py:507
  26.2 9.3 %collective-permute-start.6 = (f32[16,128]{1,0:T(8,128)S(1)}, f32[16,128]{1,0:T(8,128)S(1)}, u32[]{:S(2)}, u32[]{:S(2)}) collective-permute-start(f32[16,128]{1,0:T(8,128)S(1)} %get-tuple-element.27), channel_id=1, source_target_pairs={{0,32},{32,64},{64,96},{96,128},{128,160},{160,192},{192,224},{224... | collective-permute-start | bytes 24584 | tf_op jit(solution)/shard_map/ppermute | solution.py:478
  30.5 1.4 %copy-start.12 = (f32[6,4]{0,1:T(4,128)S(1)}, f32[6,4]{0,1:T(4,128)}, u32[]{:S(2)}) copy-start(f32[6,4]{0,1:T(4,128)} %param.21) | copy-start | bytes 292
  30.5 5.1 %collective-permute-start.7 = (f32[16,128]{1,0:T(8,128)S(1)}, f32[16,128]{1,0:T(8,128)S(1)}, u32[]{:S(2)}, u32[]{:S(2)}) collective-permute-start(f32[16,128]{1,0:T(8,128)S(1)} %get-tuple-element.28), channel_id=1, source_target_pairs={{32,0},{64,32},{96,64},{128,96},{160,128},{192,160},{224,192},{256... | collective-permute-start | bytes 24584 | tf_op jit(solution)/shard_map/ppermute | solution.py:478
  32.1 0.7 copy-start.6
  32.1 0.7 copy-start.7
  32.1 0.7 copy-start.9
  36.8 14.8 %all-to-all-start = ((f32[32,1,128]{2,1,0:T(1,128)}), f32[32,1,128]{2,1,0:T(1,128)S(1)}, u32[]{:S(2)}, u32[]{:S(2)}) async-start(f32[32,1,128]{2,1,0:T(1,128)} %get-tuple-element.30), calls=%async_computation | async-start | bytes 32768 | tf_op jit(solution)/shard_map/all_to_all | solution.py:534
  52.4 28.8 %all-to-all-start.1 = ((f32[16,1,128]{2,1,0:T(1,128)}), f32[16,1,128]{2,1,0:T(1,128)S(1)}, u32[]{:S(2)}, u32[]{:S(2)}) async-start(f32[16,1,128]{2,1,0:T(1,128)} %shard_map.155), calls=%async_computation.1 | async-start | bytes 16384 | tf_op jit(solution)/shard_map/all_to_all | solution.py:536
  71.3 9.9 %copy-start.2 = (f32[1,3,4096]{2,0,1:T(1,128)S(1)}, f32[1,3,4096]{2,0,1:T(1,128)}, u32[]{:S(2)}) copy-start(f32[1,3,4096]{2,0,1:T(1,128)} %param.20) | copy-start | bytes 147460

commit v2 on v1

--- a/solution.py
+++ b/solution.py
@@ -9,6 +9,7 @@
 from jax.sharding import PartitionSpec as P
 
 F32 = jnp.float32
+UU, G2, M, ULU, T2, Q, S = range(7)
 AXES = ("stream", "vert", "span")
 SHARDS = P(AXES, None)
 gll_inner = [
@@ -74,14 +75,11 @@
     )
 
 
-def lane_sums(rows):
-    return lax.dot_general(
-        jnp.ones((8, 128), F32),
-        rows,
-        (((1,), (1,)), ((), ())),
-        precision=lax.Precision.HIGHEST,
-        preferred_element_type=F32,
-    )
+def lane_sums(rows, first):
+    n = rows.shape[0]
+    sums = jnp.sum(rows, axis=1, keepdims=True)
+    place = lax.broadcasted_iota(jnp.int32, (n, 128), 0) + first
+    return jnp.sum(jnp.where(lane_ids(n) == place, sums, 0.0), axis=0, keepdims=True)
 
 
 def row_ids():
@@ -107,16 +105,18 @@
     return tile + left + right
 
 
-def call(body, outs, cost=2000, **kwargs):
-    vmem = pl.BlockSpec(memory_space=pltpu.VMEM)
+def call(body, outs, cost=2000, space=pltpu.VMEM, out_space=pltpu.VMEM, **kwargs):
+    given, taken = pl.BlockSpec(memory_space=space), pl.BlockSpec(memory_space=out_space)
+
+    shapes = [s if isinstance(s[0], tuple) else (s, F32) for s in outs]
 
     def run(*args, smem=0):
-        specs = [pl.BlockSpec(memory_space=pltpu.SMEM)] * smem + [vmem] * (len(args) - smem)
+        specs = [pl.BlockSpec(memory_space=pltpu.SMEM)] * smem + [given] * (len(args) - smem)
         return pl.pallas_call(
             body,
-            out_shape=[jax.ShapeDtypeStruct(s, F32) for s in outs],
+            out_shape=[jax.ShapeDtypeStruct(*s) for s in shapes],
             in_specs=specs,
-            out_specs=[vmem] * len(outs),
+            out_specs=[taken] * len(outs),
             compiler_params=pltpu.CompilerParams(vmem_limit_bytes=16 * 2**20),
             cost_estimate=pl.CostEstimate(flops=cost * 1000, bytes_accessed=200000, transcendentals=0),
             **kwargs,
@@ -126,15 +126,16 @@
 
 
 def stream_added(f_ref, low_ref, high_ref, geo_ref, x_ref, up_ref, down_ref):
+    low, high = in_order(low_ref[...], high_ref[...], "A" in SWAPS)
     for i in range(8):
         a = f_ref[i, 0:8, :]
         b = f_ref[i, 8:16, :]
         if i == 0:
-            a = a + low_ref[0:8, :]
-            b = b + low_ref[8:16, :]
+            a = a + low[0:8, :]
+            b = b + low[8:16, :]
         if i == 7:
-            a = a + high_ref[0:8, :]
-            b = b + high_ref[8:16, :]
+            a = a + high[0:8, :]
+            b = b + high[8:16, :]
         a, b = join_rows(a, b)
         x_ref[i, 0:8, :] = a
         x_ref[i, 8:16, :] = b
@@ -250,6 +251,7 @@
         return new_a, new_b
 
     beside = middle(out_halo)
+    outer = {0: [], 7: []}
     for i in range(8):
         local_ref[i, 0:8, :] = out[i][1]
         local_ref[i, 8:16, :] = out[i][2]
@@ -259,10 +261,10 @@
             last = pltpu.roll(beside[b], (63 - 8 * i) % 128, 1)
             tile = tile + jnp.where(lane == 0, first, 0.0) + jnp.where(lane == 127, last, 0.0)
             part_ref[i, 8 * b : 8 * b + 8, :] = tile
-            if i == 7:
-                top_ref[8 * b : 8 * b + 8, :] = tile
-            if i == 0:
-                bottom_ref[8 * b : 8 * b + 8, :] = tile
+            if i in (0, 7):
+                outer[i].append(tile)
+    top, bottom = [jnp.concatenate(outer[i], axis=0) for i in (7, 0)]
+    bottom_ref[...], top_ref[...] = in_order(bottom, top, "D" in SWAPS)
 
 
 def share_maps():
@@ -296,7 +298,7 @@
             for i in range(8):
                 tile = jnp.where(lane % 8 == i, pltpu.roll(tiles[i][b], (i - 7 * side) % 128, 1), tile)
             out.append(tile)
-    return out
+    return [tile if (n // 2) % 2 == 0 else -tile for n, tile in enumerate(out)]
 
 
 def load_rows(faces, omega_ref):
@@ -337,16 +339,18 @@
             if 0 < i < 7:
                 bottom = bottom + square
                 top = top + x * part_ref[i, 8 * b : 8 * b + 8, :] * share[b]
-    rows = [sublane_sum(norm), sublane_sum(energy)] + zero_rows(6)
-    rows += load_rows(face_tiles(tiles), omega_ref)
-    rows += [sublane_sum(top), sublane_sum(bottom)] + zero_rows(94)
-    sums = lane_sums(jnp.concatenate(rows, axis=0))
-    lane = lane_ids()
-    over, under = sums[:, 32:33], sums[:, 33:34]
+    rows = [sublane_sum(top), sublane_sum(norm), sublane_sum(bottom)] + zero_rows(1)
+    rows += [sublane_sum(energy)] + zero_rows(3) + load_rows(face_tiles(tiles), omega_ref)
+    sums = lane_sums(jnp.concatenate(rows, axis=0), 0)
+    lane = lane_ids(1)
+    over, norm, under, energy = sums[:, 0:1], sums[:, 1:2], sums[:, 2:3], sums[:, 4:5]
     usable = under > 1e-30
     quotient = jnp.where(usable, over / jnp.where(usable, under, 1.0), 0.0)
-    quotient = jnp.broadcast_to(jnp.clip(quotient, 0.0, 1e6), (8, 128))
-    pre_ref[...] = jnp.where(lane == 2, quotient, jnp.where(lane < 32, sums, 0.0))
+    quotient = jnp.clip(quotient, 0.0, 1e6)
+    row = jnp.where(lane >= 8, sums, 0.0)
+    for n, value in ((M, norm), (Q, energy), (S, quotient)):
+        row = jnp.where(lane == n, value, row)
+    pre_ref[...] = jnp.broadcast_to(row, (8, 128))
 
 
 def image_sums(
@@ -354,7 +358,8 @@
     v1_ref, out_ref, field,
 ):
     share, layers = share_maps()
-    quotient = jnp.broadcast_to(pre_ref[:, 2:3], (8, 128))
+    low, high = in_order(low_ref[...], high_ref[...], "D" in SWAPS)
+    quotient = jnp.broadcast_to(pre_ref[:, S : S + 1], (8, 128))
     v1 = [[None] * 2 for _ in range(8)]
     u = [[None] * 2 for _ in range(8)]
     norm = cross_norm = energy = cross_energy = jnp.zeros((8, 128), F32)
@@ -363,9 +368,9 @@
             rows = slice(8 * b, 8 * b + 8)
             tile = part_ref[i, rows, :]
             if i == 0:
-                tile = tile + low_ref[rows, :]
+                tile = tile + low[rows, :]
             if i == 7:
-                tile = tile + high_ref[rows, :]
+                tile = tile + high[rows, :]
             v1[i][b] = tile
             v1_ref[i, rows, :] = tile
             x = v0_ref[i, rows, :]
@@ -388,94 +393,167 @@
             at = slice(16 * i + 8 * b, 16 * i + 8 * b + 8)
             inner = f1 * along_j[at, :] + f2 * along_k[at, :] + f3 * u[i][b]
             energy = energy + u[i][b] * (f0 * along_i + float(WEIGHTS[i]) * inner)
-    rows = zero_rows(3) + [sublane_sum(a) for a in (norm, cross_norm, energy, cross_energy)] + zero_rows(25)
-    rows += load_rows(face_tiles(v1), omega_ref) + zero_rows(72)
-    sums = lane_sums(jnp.concatenate(rows, axis=0)) + pre_ref[...]
-    out_ref[...] = jnp.broadcast_to(sums[0:1, :][None], (32, 1, 128))
-
-
-def merged(parts, last):
-    m, q, s, uu, g, ulu, t = [parts[:, n : n + 1] for n in range(7)]
-
-    def add(a):
-        return jnp.sum(a, axis=0, keepdims=True)
-
-    m_all, q_all = add(m), add(q)
-    if last:
-        common = q_all / m_all
-    else:
-        usable = m_all > 0.0
-        common = jnp.where(usable, add(m * s) / jnp.where(usable, m_all, 1.0), 0.0)
-    e = s - common
-    uu_all = add(uu + e * (2.0 * g + e * m))
-    g_all = add(g + e * m)
-    ulu_all = add(ulu + e * (2.0 * t + e * q))
-    t_all = add(t + e * q)
-    return m_all, q_all, common, uu_all, g_all, ulu_all, t_all, add(parts)
+    rows = [sublane_sum(a) for a in (norm, 2.0 * cross_norm)] + zero_rows(1)
+    rows += [sublane_sum(a) for a in (energy, 2.0 * cross_energy)] + zero_rows(3)
+    row = lane_sums(jnp.concatenate(rows, axis=0), 0)
+    row = row + lane_sums(jnp.concatenate(load_rows(face_tiles(v1), omega_ref), axis=0), 32)
+    out_ref[...] = jnp.broadcast_to(row + pre_ref[0:1, :], (32, 128))
+
+
+def merged(parts):
+    n = parts.shape[0]
+    lane = lane_ids(n)
+    common = parts[0:1, S : S + 1]
+    e = parts[:, S : S + 1] - common
+    once = jnp.where((lane == UU) | (lane == ULU), 1.0, jnp.where((lane == G2) | (lane == T2), 2.0, 0.0))
+    twice = jnp.where((lane == UU) | (lane == ULU), 1.0, 0.0)
+    rows = parts + e * (once * pltpu.roll(parts, 127, 1) + e * (twice * pltpu.roll(parts, 126, 1)))
+    total = jnp.sum(rows, axis=0, keepdims=True)
+    return jnp.where(lane_ids(1) == S, common, total)
 
 
 def group_sums(parts_ref, out_ref):
-    parts = parts_ref[...].reshape(parts_ref.shape[0], 128)
-    values = merged(parts, False)
-    row = values[7]
-    lane = lane_ids(1)
-    for n in range(7):
-        row = jnp.where(lane == n, values[n], row)
-    out_ref[...] = jnp.broadcast_to(row[None], out_ref.shape)
-
-
-def finish(parts_ref, v0_ref, v1_ref, arm_ref, store_ref, motion_ref, p_ref, velocity_ref):
-    parts = parts_ref[...].reshape(parts_ref.shape[0], 128)
-    m, q, _, uu, _, ulu, _, sums = merged(parts, True)
+    out_ref[...] = jnp.broadcast_to(merged(parts_ref[...]), out_ref.shape)
+
+
+def finish(
+    parts_ref, v0_ref, v1_ref, arm_ref, store_ref, motion_ref, p_out, velocity_out, p_ref, velocity_ref, sems
+):
+    total = merged(parts_ref[...])
+    uu, g2, m, ulu, t2, q, s = [total[:, n : n + 1] for n in range(7)]
     alpha = m / q
-    beta = alpha * alpha * uu / m
-    new = alpha * alpha * uu
-    curve = alpha * alpha * ulu - beta * beta * q
-    alpha_next = new / curve
+    e = s - q / m
+    uu = uu + e * (g2 + e * m)
+    ulu = ulu + e * (t2 + e * q)
+    square = alpha * alpha
+    beta = square * uu / m
+    curve = square * ulu - beta * beta * q
+    alpha_next = square * uu / curve
     c0 = alpha + alpha_next * (1.0 + beta)
     c1 = -alpha_next * alpha
-    for i in range(8):
-        p_ref[i] = c0 * v0_ref[i] + c1 * v1_ref[i]
-    loads = c0 * sums + c1 * pltpu.roll(sums, 104, 1)
+    wide0 = jnp.broadcast_to(c0, (16, 128))
+    wide1 = jnp.broadcast_to(c1, (16, 128))
+    for i in range(8):
+        p_ref[i] = wide0 * v0_ref[i] + wide1 * v1_ref[i]
+    p_copy = pltpu.make_async_copy(p_ref, p_out, sems.at[0])
+    p_copy.start()
+    loads = c0 * total + c1 * pltpu.roll(total, 104, 1)
     state = motion_ref[0:1, :] + motion_ref[1:2, :] * loads
     stores = store_ref[...]
-    zero = jnp.zeros((32, 128), F32)
     maps = []
     for c in range(6):
-        total = zero
+        value = jnp.zeros((32, 128), F32)
         for store in range(4):
             at = 8 + 4 * c + store
-            total = jnp.where(stores == store, state[:, at : at + 1], total)
-        maps.append(total)
+            value = jnp.where(stores == store, state[:, at : at + 1], value)
+        maps.append(value)
     arms = [arm_ref[c] for c in range(3)]
     for c in range(3):
         a, b = (c + 1) % 3, (c + 2) % 3
-        value = maps[c] + (maps[3 + a] * arms[b] - maps[3 + b] * arms[a])
-        for r in range(32):
-            velocity_ref[0, c : c + 1, 128 * r : 128 * r + 128] = value[r : r + 1, :]
-
-
-def wall_weights(elem_ref, face_ref, store_ref, node_ref, spread_ref, omega_ref, spread):
-    spread[...] = dot(node_ref[...], spread_ref[...])
-    omega_ref[...] = jnp.zeros(omega_ref.shape, F32)
-    lane = lane_ids() // 8
-
-    def add(n, carry):
-        elem, face, store = elem_ref[0, n], face_ref[0, n], store_ref[0, n]
-        tile = (2 * face + elem // 16) * 5 + store
-        here = lane == elem % 16
-        for q in range(3):
-            at = pl.multiple_of((q * 64 + n) * 8, 8)
-            omega_ref[tile * 3 + q] += jnp.where(here, spread[pl.ds(at, 8), :], 0.0)
+        velocity_ref[c] = maps[c] + (maps[3 + a] * arms[b] - maps[3 + b] * arms[a])
+    velocity_copy = pltpu.make_async_copy(velocity_ref, velocity_out, sems.at[1])
+    velocity_copy.start()
+    p_copy.wait()
+    velocity_copy.wait()
+
+
+def spread_geometry(geo_ref, out_ref):
+    element = lax.broadcasted_iota(jnp.int32, (16, 128), 0)
+    out_ref[...] = dot(geo_ref[...], jnp.where((lane_ids(16) >> 3) == element, 1.0, 0.0))
+
+
+def wall_table(
+    elem_ref, face_ref, stores_ref, motion_ref, inverse_ref, weight_ref, arm_ref,
+    table_ref, code_ref, store_out, motion_out,
+):
+    weight = weight_ref[...]
+    nodes = jnp.concatenate([weight] + [weight * arm_ref[c] for c in range(3)], axis=0)
+    a = lax.broadcasted_iota(jnp.int32, (128, 128), 0)
+    b = lax.broadcasted_iota(jnp.int32, (128, 128), 1)
+    slot, outer, inner = a & 64, (a >> 3) & 7, a & 7
+    table_ref[0:128, :] = dot(nodes, jnp.where(b == slot + (7 - outer) * 8 + inner, 1.0, 0.0))
+    table_ref[128:256, :] = dot(nodes, jnp.where(b == slot + (7 - inner) * 8 + outer, 1.0, 0.0))
+
+    elem, face, stores = elem_ref[...], face_ref[...], stores_ref[...]
+    n = lax.broadcasted_iota(jnp.int32, (1, 64), 1)
+    direction = face >> 1
+    first = jnp.where(direction == 2, 128, 0) + (n >> 1)
+    column = elem & 15
+    code_ref[0:1, :] = ((2 * face + (elem >> 4)) * 5 + stores) * 3
+    code_ref[1:2, :] = column
+    code_ref[2:3, :] = (8 * column + 64 * (n & 1) + 72) & 127
+    code_ref[3:4, :] = first
+    code_ref[4:5, :] = first + jnp.where(direction == 2, 64, 96)
+    code_ref[5:6, :] = first + jnp.where(direction == 0, 64, 32)
+    code_ref[6:8, :] = jnp.zeros((2, 64), jnp.int32)
+
+    numbers = stores.astype(F32)
+    row = lax.broadcasted_iota(jnp.int32, (32, 64), 0)
+    column = lax.broadcasted_iota(jnp.int32, (32, 64), 1)
+    even = jnp.sum(jnp.where(column == 2 * row, numbers, 0.0), axis=1, keepdims=True)
+    odd = jnp.sum(jnp.where(column == 2 * row + 1, numbers, 0.0), axis=1, keepdims=True)
+    store_out[...] = jnp.where(lane_ids(32) < 64, even, odd)
+
+    load = lane_ids(8) - 8
+    inside = (load >= 0) & (load < 24)
+    component, store = load >> 2, load & 3
+    row = row_ids()
+    motion = dot(motion_ref[...], jnp.where(inside & (component == row), 1.0, 0.0)[0:6, :])
+    motion_out[0:1, :] = jnp.sum(jnp.where((store == row)[0:4, :], motion, 0.0), axis=0, keepdims=True)
+    scale = dot(inverse_ref[...], jnp.where(inside & (store == row), 1.0, 0.0)[0:4, :])
+    taken = jnp.maximum(component - 2, 0) == row
+    motion_out[1:2, :] = jnp.sum(jnp.where(taken[0:4, :], scale, 0.0), axis=0, keepdims=True)
+
+
+def wall_weights(begin, end, code_ref, table_ref, *rest):
+    omega_ref = rest[-1]
+    if begin == 0:
+        omega_ref[...] = jnp.zeros(omega_ref.shape, F32)
+    lane = lane_ids() >> 3
+
+    def add(step, carry):
+        tiles = []
+        for k in range(8):
+            n = begin + 8 * step + k
+            here = lane == code_ref[1, n]
+            for q in range(3):
+                nodes = jnp.broadcast_to(table_ref[pl.ds(code_ref[3 + q, n], 1), :], (8, 128))
+                nodes = pltpu.roll(pltpu.roll(nodes, 0, 1, stride=8, stride_axis=0), code_ref[2, n], 1)
+                tiles.append(jnp.where(here, nodes, 0.0))
+        for k in range(8):
+            at = code_ref[0, begin + 8 * step + k]
+            for q in range(3):
+                omega_ref[at + q] += tiles[3 * k + q]
         return carry
 
-    lax.fori_loop(0, 64, add, 0)
+    lax.fori_loop(0, (end - begin) // 8, add, 0)
 
 
 def shifted(x, axis, step, ring=False):
     count = lax.axis_size(axis)
     pairs = [(i, (i + step) % count) for i in range(count) if ring or 0 <= i + step < count]
     return lax.ppermute(x, axis, pairs)
+
+
+def swapped(x, axis, first):
+    pairs = [(i, i + 1) for i in range(first, lax.axis_size(axis) - 1, 2)]
+    return lax.ppermute(x, axis, pairs + [(b, a) for a, b in pairs])
+
+
+SWAPS = "A"
+
+
+def stream_exchange(one, two, swap):
+    if swap:
+        return swapped(one, "stream", 0), swapped(two, "stream", 1)
+    return shifted(one, "stream", 1), shifted(two, "stream", -1)
+
+
+def in_order(first, second, swap):
+    if not swap:
+        return first, second
+    even = lax.axis_index("stream") % 2 == 0
+    return jnp.where(even, second, first), jnp.where(even, first, second)
 
 
 def per_device(
@@ -483,59 +561,54 @@
 ):
     lane_k, lane_i, rows, node_w = [jnp.asarray(a) for a in constants()]
     field = (8, 16, 128)
-
-    low = shifted(forcing[7], "stream", 1)
-    high = shifted(forcing[0], "stream", -1)
-
-    geo = jnp.repeat(geometry.reshape(8, 16), 8, axis=1)
-    face = wall_face[0]
-    sign = (1 - 2 * (face % 2)).astype(F32)[:, None]
-    weight = wall_weight[0].reshape(64, 64) * sign
-    arms = wall_arm[0].reshape(3, 64, 64)
-    direction = (face // 2)[:, None]
-    first = jnp.where(direction == 2, arms[1], arms[2])
-    second = jnp.where(direction == 0, arms[1], arms[0])
-    nodes = jnp.stack([weight, weight * first, weight * second]).reshape(3, 64, 8, 8)
-    nodes = jnp.where((direction == 2)[None, :, :, None], jnp.swapaxes(nodes, 2, 3), nodes)
-    spread = jnp.asarray(np.kron(np.ones((1, 16)), np.eye(8)).astype(np.float32))
-    omega = call(wall_weights, [(180, 8, 128)], cost=4000, scratch_shapes=[pltpu.VMEM((1536, 128), F32)])(
-        wall_elem, wall_face, wall_store, nodes.reshape(1536, 8), spread, smem=3
-    )[0]
-    arm_rows = wall_arm[0].reshape(3, 32, 128)
-    store_rows = jnp.repeat(wall_store[0], 64).reshape(32, 128)
-    zeros8, zeros96 = jnp.zeros((8,), F32), jnp.zeros((96,), F32)
-    scale = jnp.concatenate([store_inverse[0:1]] * 3 + [store_inverse[1:4]], axis=0)
-    motion = jnp.stack(
-        [
-            jnp.concatenate([zeros8, store_motion.reshape(24), zeros96]),
-            jnp.concatenate([zeros8, scale.reshape(24), zeros96]),
-        ]
-    )
-
+    tie = lax.optimization_barrier
+
+    if "A" in SWAPS:
+        odd = lax.axis_index("stream") % 2
+        top, bottom = [lax.dynamic_index_in_dim(forcing, at, 0, False) for at in (7 - 7 * odd, 7 * odd)]
+    else:
+        top, bottom = forcing[7], forcing[0]
+    low, high = stream_exchange(top, bottom, "A" in SWAPS)
+    geo = call(spread_geometry, [(8, 128)])(geometry.reshape(8, 16))[0]
     x, up, down = call(stream_added, [field, (72, 128), (72, 128)])(forcing, low, high, geo)
+
+    up, down, weight, arms = tie((up, down, wall_weight.reshape(32, 128), wall_arm.reshape(3, 32, 128)))
     low = shifted(up, "vert", 1, ring=True)
     high = shifted(down, "vert", -1, ring=True)
+    table, codes, store_rows, motion = call(
+        wall_table, [(256, 128), ((8, 64), jnp.int32), (32, 128), (2, 128)]
+    )(wall_elem, wall_face, wall_store, store_motion.T, store_inverse, weight, arms)
+    low, high, table, codes = tie((low, high, table, codes))
     wide, geo_wide, right, left = call(vert_added, [(8, 32, 128), (16, 128), (48, 128), (48, 128)])(
         x, low, high, geo
     )
+
+    right, left, table, codes = tie((right, left, table, codes))
     low = shifted(right, "span", 1)
     high = shifted(left, "span", -1)
+    omega = call(functools.partial(wall_weights, 0, 64), [(180, 8, 128)])(codes, table, smem=1)[0]
+    low, high, omega = tie((low, high, omega))
     v0, local, part, top, bottom, maps = call(
         span_added,
         [field, field, field, (16, 128), (16, 128), (4, 16, 128)],
         scratch_shapes=[pltpu.VMEM((288, 128), F32)],
     )(wide, geo_wide, right, left, low, high, lane_k, lane_i, rows, node_w)
-    low = shifted(top, "stream", 1)
-    high = shifted(bottom, "stream", -1)
+
+    low, high = stream_exchange(top, bottom, "D" in SWAPS)
     pre = call(before_image, [(8, 128)])(v0, local, part, omega)[0]
-    v1, sums = call(image_sums, [field, (32, 1, 128)], scratch_shapes=[pltpu.VMEM((128, 128), F32)])(
+    v1, sums = call(image_sums, [field, (32, 128)], scratch_shapes=[pltpu.VMEM((128, 128), F32)])(
         v0, local, part, low, high, maps, omega, pre, lane_k, rows
     )
-    sums = lax.all_to_all(sums, ("vert", "span"), 0, 0)
-    sums = call(group_sums, [(16, 1, 128)])(sums)[0]
-    sums = lax.all_to_all(sums, "stream", 0, 0)
-    pressure, velocity = call(finish, [field, (1, 3, 4096)])(sums, v0, v1, arm_rows, store_rows, motion)
-    return pressure, velocity
+    sums = lax.all_to_all(sums.reshape(32, 1, 128), ("vert", "span"), 0, 0)
+    sums = call(group_sums, [(16, 128)])(sums.reshape(32, 128))[0]
+    sums = lax.all_to_all(sums.reshape(16, 1, 128), "stream", 0, 0)
+    pressure, velocity = call(
+        finish,
+        [field, (3, 32, 128)],
+        out_space=pltpu.HBM,
+        scratch_shapes=[pltpu.VMEM(field, F32), pltpu.VMEM((3, 32, 128), F32), pltpu.SemaphoreType.DMA((2,))],
+    )(sums.reshape(16, 128), v0, v1, arms, store_rows, motion)
+    return pressure, velocity.reshape(1, 3, 4096)
 
 
 def solution(mesh):

time: 83.6 us -> 76.8 us (0.919)
  blocking collectives: 0 us -> 39.3 us
  starting transfers between devices: 45.2 us -> 21.7 us
  waiting for transfers between devices: 21 us -> 7.65 us
  local copies, waits for them, and re-layouts: 6.82 us -> 0.82 us
  other arithmetic: 2.02 us -> 0 us
    all_to_all x0 -> x2, blocking collectives: none -> 39.3 us  [the longest x1 24.3 us: per_device(): sums = lax.all_to_all(sums.reshape(16, 1, 128), 'stream', 0, 0)]
    all_to_all x2 -> x0, starting transfers between devices: 25.5 us -> none  [the longest x1 17.6 us: per_device(): sums = lax.all_to_all(sums, 'stream', 0, 0)]
    all_to_all x2 -> x0, waiting for transfers between devices: 16.5 us -> none  [the longest x1 9.73 us: per_device(): sums = lax.all_to_all(sums, 'stream', 0, 0)]
    ppermute x0 -> x2, starting transfers between devices: none -> 8.04 us  [swapped(): return lax.ppermute(x, axis, pairs + [(b, a) for a, b in pairs])]
    ppermute x8 -> x6, starting transfers between devices: 19.7 us -> 13.6 us  [shifted(): return lax.ppermute(x, axis, pairs)]
    unnamed x31 -> x26, local copies, waits for them, and re-layouts: 3.06 us -> 0.07 us
    ppermute x8 -> x6, waiting for transfers between devices: 4.48 us -> 6.76 us  [shifted(): return lax.ppermute(x, axis, pairs)]
    unnamed x2 -> x0, other arithmetic: 1.35 us -> none
  transfers between devices with their start and end apart: 10 -> 8, of which waited for: 5 -> 5; matrix products, arithmetic and copies ran while one was open for 7% -> 0% of each run, Pallas kernels for 3% -> 4%
where the time goes in v2:
time: 76.8 us; the launch traced here: 76.5 us
  blocking collectives  39.3 us (51%)
  starting transfers between devices  21.7 us (28%)
  waiting for transfers between devices  7.65 us (10%)
  Pallas kernels  6.15 us (8%)
  between operations  0.86 us (1%)
  local copies, waits for them, and re-layouts  0.82 us (1%)
    all_to_all x1, blocking collectives, per_device(): sums = lax.all_to_all(sums.reshape(16, 1, 128), 'stream', 0, 0)  24.3 us
    all_to_all x1, blocking collectives, per_device(): sums = lax.all_to_all(sums.reshape(32, 1, 128), ('vert', 'span'), 0, 0)  15 us
    ppermute x6, starting transfers between devices, shifted(): return lax.ppermute(x, axis, pairs)  13.6 us
    ppermute x2, starting transfers between devices, swapped(): return lax.ppermute(x, axis, pairs + [(b, a) for a, b in pairs])  8.04 us
    ppermute x6, waiting for transfers between devices, shifted(): return lax.ppermute(x, axis, pairs)  6.76 us
    pallas_call x10, Pallas kernels, run(): pl.pallas_call(body, out_shape=[jax.ShapeDtypeStruct(*s) for s in shapes]...  6.15 us
  transfers between devices with their start and end apart: 8, of which 5 were waited for; matrix products, arithmetic and copies ran while one was open for 0% of the time, Pallas kernels for 4%

profile of v2, /device:TPU:1, one launch (start us, length us, event | category | flops | bytes accessed | tf_op | source)
XLA Modules:
  0.0 76.5 jit_solution(16923656165762442673)
XLA Ops:
  0.6 0.0 copy-start.3
  0.7 0.7 dynamic-slice_bitcast_fusion
  1.4 0.0 copy-start.7
  1.4 0.8 %collective-permute-start.1 = (f32[16,128]{1,0:T(8,128)S(1)}, f32[16,128]{1,0:T(8,128)S(1)}, u32[]{:S(2)}, u32[]{:S(2)}) collective-permute-start(f32[16,128]{1,0:T(8,128)S(1)} %get-tuple-element.80), channel_id=1, source_target_pairs={{32,64},{96,128},{160,192},{224,256},{288,320},{352,384},{416,448}... | collective-permute-start | bytes 24584 | tf_op jit(solution)/shard_map/ppermute | solution.py:540
  2.2 7.3 %collective-permute-start = (f32[16,128]{1,0:T(8,128)S(1)}, f32[16,128]{1,0:T(8,128)S(1)}, u32[]{:S(2)}, u32[]{:S(2)}) collective-permute-start(f32[16,128]{1,0:T(8,128)S(1)} %get-tuple-element.81), channel_id=1, source_target_pairs={{0,32},{64,96},{128,160},{192,224},{256,288},{320,352},{384,416},{... | collective-permute-start | bytes 24584 | tf_op jit(solution)/shard_map/ppermute | solution.py:540
  9.5 0.0 copy-done.7
  9.5 0.1 shard_map.140.geo_ref
  9.6 0.0 copy-start.2
  9.6 0.0 collective-permute-done.1.high_ref
  9.6 0.9 %collective-permute-done.low_ref = f32[16,128]{1,0:T(8,128)S(1)} collective-permute-done((f32[16,128]{1,0:T(8,128)S(1)}, f32[16,128]{1,0:T(8,128)S(1)}, u32[]{:S(2)}, u32[]{:S(2)}) %collective-permute-start) | collective-permute-done | bytes 8224 | tf_op jit(solution)/shard_map/ppermute | solution.py:540
  10.5 0.0 copy-done.3
  10.5 0.0 copy-start.5
  10.5 0.0 copy-start.9
  10.5 0.0 copy-start.8
  10.5 0.0 copy-start.10
  10.6 0.0 copy-start.11
  10.6 0.0 copy-start.12
  10.6 3.0 %collective-permute-start.2 = (f32[72,128]{1,0:T(8,128)S(1)}, f32[72,128]{1,0:T(8,128)S(1)}, u32[]{:S(2)}, u32[]{:S(2)}) collective-permute-start(f32[72,128]{1,0:T(8,128)S(1)} %get-tuple-element.41), channel_id=1, source_target_pairs={{0,4},{4,8},{8,12},{12,16},{16,20},{20,24},{24,28},{28,0},{1,5},{5... | collective-permute-start | bytes 110600 | tf_op jit(solution)/shard_map/ppermute | solution.py:535
  13.6 1.1 %collective-permute-start.3 = (f32[72,128]{1,0:T(8,128)S(1)}, f32[72,128]{1,0:T(8,128)S(1)}, u32[]{:S(2)}, u32[]{:S(2)}) collective-permute-start(f32[72,128]{1,0:T(8,128)S(1)} %get-tuple-element.42), channel_id=1, source_target_pairs={{0,28},{4,0},{8,4},{12,8},{16,12},{20,16},{24,20},{28,24},{1,29},{... | collective-permute-start | bytes 110600 | tf_op jit(solution)/shard_map/ppermute | solution.py:535
  14.7 0.0 copy-done.2
  14.8 0.0 copy-done.5
  14.8 0.0 copy-done.9
  14.8 0.0 copy-done.8
  14.8 0.0 copy-done.10
  14.8 0.0 copy-done.11
  14.8 0.0 copy-done.12
  14.8 0.3 shard_map.142
  15.1 0.3 collective-permute-done.2.low_ref
  15.4 1.6 %collective-permute-done.3.high_ref = f32[72,128]{1,0:T(8,128)S(1)} collective-permute-done((f32[72,128]{1,0:T(8,128)S(1)}, f32[72,128]{1,0:T(8,128)S(1)}, u32[]{:S(2)}, u32[]{:S(2)}) %collective-permute-start.3) | collective-permute-done | bytes 36896 | tf_op jit(solution)/shard_map/ppermute | solution.py:535
  17.0 0.3 shard_map.143
  17.3 0.0 copy-start
  17.3 0.0 copy-start.1
  17.3 0.0 copy-start.4
  17.3 3.2 %collective-permute-start.4 = (f32[48,128]{1,0:T(8,128)S(1)}, f32[48,128]{1,0:T(8,128)S(1)}, u32[]{:S(2)}, u32[]{:S(2)}) collective-permute-start(f32[48,128]{1,0:T(8,128)S(1)} %get-tuple-element.55.right_ref), channel_id=1, source_target_pairs={{0,1},{1,2},{2,3},{4,5},{5,6},{6,7},{8,9},{9,10},{10,11},{12,13},{... | collective-permute-start | bytes 73736 | tf_op jit(solution)/shard_map/ppermute | solution.py:535
  20.6 1.3 %collective-permute-start.5 = (f32[48,128]{1,0:T(8,128)S(1)}, f32[48,128]{1,0:T(8,128)S(1)}, u32[]{:S(2)}, u32[]{:S(2)}) collective-permute-start(f32[48,128]{1,0:T(8,128)S(1)} %get-tuple-element.56.left_ref), channel_id=1, source_target_pairs={{1,0},{2,1},{3,2},{5,4},{6,5},{7,6},{9,8},{10,9},{11,10},{13,12},{... | collective-permute-start | bytes 73736 | tf_op jit(solution)/shard_map/ppermute | solution.py:535
  21.9 0.0 copy-start.6
  21.9 2.3 %shard_map.144.omega_ref = f32[180,8,128]{2,1,0:T(8,128)S(1)} custom-call(s32[8,64]{1,0:T(8,128)S(1)} %get-tuple-element.57.code_ref, f32[256,128]{1,0:T(8,128)S(1)} %get-tuple-element.58.table_ref), custom_call_target="tpu_custom_call" | custom-call | flops 2000000 | bytes 200000 | tf_op jit(solution)/shard_map/pallas_call | solution.py:115
  24.2 0.0 collective-permute-done.4.low_ref
  24.2 0.9 %collective-permute-done.5.high_ref = f32[48,128]{1,0:T(8,128)S(1)} collective-permute-done((f32[48,128]{1,0:T(8,128)S(1)}, f32[48,128]{1,0:T(8,128)S(1)}, u32[]{:S(2)}, u32[]{:S(2)}) %collective-permute-start.5) | collective-permute-done | bytes 24608 | tf_op jit(solution)/shard_map/ppermute | solution.py:535
  25.1 0.0 copy-done
  25.1 0.0 copy-done.1
  25.1 0.0 copy-done.4
  25.2 0.0 copy-done.6
  25.2 0.8 shard_map.145
  25.9 3.6 %collective-permute-start.6 = (f32[16,128]{1,0:T(8,128)S(1)}, f32[16,128]{1,0:T(8,128)S(1)}, u32[]{:S(2)}, u32[]{:S(2)}) collective-permute-start(f32[16,128]{1,0:T(8,128)S(1)} %get-tuple-element.64), channel_id=1, source_target_pairs={{0,32},{32,64},{64,96},{96,128},{128,160},{160,192},{192,224},{224... | collective-permute-start | bytes 24584 | tf_op jit(solution)/shard_map/ppermute | solution.py:535
  29.6 1.3 %collective-permute-start.7 = (f32[16,128]{1,0:T(8,128)S(1)}, f32[16,128]{1,0:T(8,128)S(1)}, u32[]{:S(2)}, u32[]{:S(2)}) collective-permute-start(f32[16,128]{1,0:T(8,128)S(1)} %get-tuple-element.65), channel_id=1, source_target_pairs={{32,0},{64,32},{96,64},{128,96},{160,128},{192,160},{224,192},{256... | collective-permute-start | bytes 24584 | tf_op jit(solution)/shard_map/ppermute | solution.py:535
  30.9 0.4 shard_map.146.pre_ref
  31.3 0.0 collective-permute-done.6.low_ref
  31.3 4.0 %collective-permute-done.7.high_ref = f32[16,128]{1,0:T(8,128)S(1)} collective-permute-done((f32[16,128]{1,0:T(8,128)S(1)}, f32[16,128]{1,0:T(8,128)S(1)}, u32[]{:S(2)}, u32[]{:S(2)}) %collective-permute-start.7) | collective-permute-done | bytes 8224 | tf_op jit(solution)/shard_map/ppermute | solution.py:535
  35.3 0.4 shard_map.147
  35.7 15.0 %all_to_all.10 = f32[32,1,128]{2,1,0:T(1,128)S(1)} all-to-all(f32[32,1,128]{2,1,0:T(1,128)S(1)} %bitcast.23), channel_id=1, replica_groups=mesh['stream'=16,'vert'=8,'span'=4] {'vert','span'}, dimensions={0} | all-to-all | bytes 32768 | tf_op jit(solution)/shard_map/all_to_all | solution.py:602
  50.7 0.1 shard_map.148
  50.8 24.3 %all_to_all.11 = f32[16,1,128]{2,1,0:T(1,128)S(1)} all-to-all(f32[16,1,128]{2,1,0:T(1,128)S(1)} %bitcast.21), channel_id=1, replica_groups=mesh['stream'=16,'vert'=8,'span'=4] {'stream'}, dimensions={0} | all-to-all | bytes 16384 | tf_op jit(solution)/shard_map/all_to_all | solution.py:604
  75.1 1.4 %shard_map.149 = (f32[8,16,128]{2,1,0:T(8,128)}, f32[3,32,128]{2,1,0:T(8,128)}) custom-call(f32[16,128]{1,0:T(8,128)S(1)} %bitcast.20, f32[8,16,128]{2,1,0:T(8,128)S(1)} %get-tuple-element.61.v0_ref, f32[8,16,128]{2,1,0:T(8,128)S(1)} %get-tuple-element.69.v1_ref, f32[3,32,128]{2,1,0:T(8,128)S(1)} %bitcast.18, f32[32,128]{1,0:T(8,128)S(1)} %get-tuple-element.70.store_ref, ...), custom_call_target="tpu_custom_call" | custom-call | flops 2000000 | bytes 200000 | tf_op jit(solution)/shard_map/pallas_call | solution.py:115
  (1 shorter events, 0.0 us)
Async XLA Ops:
  0.6 9.9 %copy-start.3 = (f32[8,16,128]{2,1,0:T(8,128)S(1)}, f32[8,16,128]{2,1,0:T(8,128)}, u32[]{:S(2)}) copy-start(f32[8,16,128]{2,1,0:T(8,128)} %f_ref.1) | copy-start | bytes 196612
  1.4 8.1 %copy-start.7 = (f32[4,1,2,16]{3,2,1,0:T(2,128)S(1)}, f32[4,1,2,16]{3,2,1,0:T(2,128)}, u32[]{:S(2)}) copy-start(f32[4,1,2,16]{3,2,1,0:T(2,128)} %param.14) | copy-start | bytes 1540
  1.4 8.2 %collective-permute-start.1 = (f32[16,128]{1,0:T(8,128)S(1)}, f32[16,128]{1,0:T(8,128)S(1)}, u32[]{:S(2)}, u32[]{:S(2)}) collective-permute-start(f32[16,128]{1,0:T(8,128)S(1)} %get-tuple-element.80), channel_id=1, source_target_pairs={{32,64},{96,128},{160,192},{224,256},{288,320},{352,384},{416,448}... | collective-permute-start | bytes 24584 | tf_op jit(solution)/shard_map/ppermute | solution.py:540
  2.2 8.3 %collective-permute-start = (f32[16,128]{1,0:T(8,128)S(1)}, f32[16,128]{1,0:T(8,128)S(1)}, u32[]{:S(2)}, u32[]{:S(2)}) collective-permute-start(f32[16,128]{1,0:T(8,128)S(1)} %get-tuple-element.81), channel_id=1, source_target_pairs={{0,32},{64,96},{128,160},{192,224},{256,288},{320,352},{384,416},{... | collective-permute-start | bytes 24584 | tf_op jit(solution)/shard_map/ppermute | solution.py:540
  9.6 5.2 %copy-start.2 = (f32[1,3,4096]{2,0,1:T(1,128)S(1)}, f32[1,3,4096]{2,0,1:T(1,128)}, u32[]{:S(2)}) copy-start(f32[1,3,4096]{2,0,1:T(1,128)} %param.19) | copy-start | bytes 147460
  10.5 4.3 %copy-start.5 = (f32[1,4096]{1,0:T(1,128)S(1)}, f32[1,4096]{1,0:T(1,128)}, u32[]{:S(2)}) copy-start(f32[1,4096]{1,0:T(1,128)} %param.18) | copy-start | bytes 49156
  10.5 4.2 %copy-start.9 = (f32[4,4]{1,0:T(4,128)S(1)}, f32[4,4]{1,0:T(4,128)}, u32[]{:S(2)}) copy-start(f32[4,4]{1,0:T(4,128)} %inverse_ref.1) | copy-start | bytes 196
  10.5 4.2 %copy-start.8 = (f32[6,4]{0,1:T(4,128)S(1)}, f32[6,4]{0,1:T(4,128)}, u32[]{:S(2)}) copy-start(f32[6,4]{0,1:T(4,128)} %param.20) | copy-start | bytes 292
  10.5 4.2 %copy-start.10 = (s32[1,64]{1,0:T(1,128)S(1)}, s32[1,64]{1,0:T(1,128)}, u32[]{:S(2)}) copy-start(s32[1,64]{1,0:T(1,128)} %elem_ref.1) | copy-start | bytes 772
  10.6 4.2 %copy-start.11 = (s32[1,64]{1,0:T(1,128)S(1)}, s32[1,64]{1,0:T(1,128)}, u32[]{:S(2)}) copy-start(s32[1,64]{1,0:T(1,128)} %face_ref.1) | copy-start | bytes 772
  10.6 4.2 %copy-start.12 = (s32[1,64]{1,0:T(1,128)S(1)}, s32[1,64]{1,0:T(1,128)}, u32[]{:S(2)}) copy-start(s32[1,64]{1,0:T(1,128)} %stores_ref.1) | copy-start | bytes 772
  10.6 4.9 %collective-permute-start.2 = (f32[72,128]{1,0:T(8,128)S(1)}, f32[72,128]{1,0:T(8,128)S(1)}, u32[]{:S(2)}, u32[]{:S(2)}) collective-permute-start(f32[72,128]{1,0:T(8,128)S(1)} %get-tuple-element.41), channel_id=1, source_target_pairs={{0,4},{4,8},{8,12},{12,16},{16,20},{20,24},{24,28},{28,0},{1,5},{5... | collective-permute-start | bytes 110600 | tf_op jit(solution)/shard_map/ppermute | solution.py:535
  13.6 3.4 %collective-permute-start.3 = (f32[72,128]{1,0:T(8,128)S(1)}, f32[72,128]{1,0:T(8,128)S(1)}, u32[]{:S(2)}, u32[]{:S(2)}) collective-permute-start(f32[72,128]{1,0:T(8,128)S(1)} %get-tuple-element.42), channel_id=1, source_target_pairs={{0,28},{4,0},{8,4},{12,8},{16,12},{20,16},{24,20},{28,24},{1,29},{... | collective-permute-start | bytes 110600 | tf_op jit(solution)/shard_map/ppermute | solution.py:535
  17.3 7.9 %copy-start = (f32[256,256]{1,0:T(8,128)S(1)}, f32[256,256]{1,0:T(8,128)}, u32[]{:S(2)}) copy-start(f32[256,256]{1,0:T(8,128)} %constant.40.clone.kr_ref) | copy-start | bytes 786436
  17.3 7.9 %copy-start.1 = (f32[128,128]{1,0:T(8,128)S(1)}, f32[128,128]{1,0:T(8,128)}, u32[]{:S(2)}) copy-start(f32[128,128]{1,0:T(8,128)} %constant.38.clone.kk_ref) | copy-start | bytes 196612
  17.3 7.8 %copy-start.4 = (f32[128,128]{1,0:T(8,128)S(1)}, f32[128,128]{1,0:T(8,128)}, u32[]{:S(2)}) copy-start(f32[128,128]{1,0:T(8,128)} %constant.39.clone.ki_ref) | copy-start | bytes 196612
  17.3 6.9 %collective-permute-start.4 = (f32[48,128]{1,0:T(8,128)S(1)}, f32[48,128]{1,0:T(8,128)S(1)}, u32[]{:S(2)}, u32[]{:S(2)}) collective-permute-start(f32[48,128]{1,0:T(8,128)S(1)} %get-tuple-element.55.right_ref), channel_id=1, source_target_pairs={{0,1},{1,2},{2,3},{4,5},{5,6},{6,7},{8,9},{9,10},{10,11},{12,13},{... | collective-permute-start | bytes 73736 | tf_op jit(solution)/shard_map/ppermute | solution.py:535
  20.6 4.6 %collective-permute-start.5 = (f32[48,128]{1,0:T(8,128)S(1)}, f32[48,128]{1,0:T(8,128)S(1)}, u32[]{:S(2)}, u32[]{:S(2)}) collective-permute-start(f32[48,128]{1,0:T(8,128)S(1)} %get-tuple-element.56.left_ref), channel_id=1, source_target_pairs={{1,0},{2,1},{3,2},{5,4},{6,5},{7,6},{9,8},{10,9},{11,10},{13,12},{... | collective-permute-start | bytes 73736 | tf_op jit(solution)/shard_map/ppermute | solution.py:535
  21.9 3.3 %copy-start.6 = (f32[24,128]{1,0:T(8,128)S(1)}, f32[24,128]{1,0:T(8,128)}, u32[]{:S(2)}) copy-start(f32[24,128]{1,0:T(8,128)} %constant.41.clone.w_ref) | copy-start | bytes 36868
  25.9 5.4 %collective-permute-start.6 = (f32[16,128]{1,0:T(8,128)S(1)}, f32[16,128]{1,0:T(8,128)S(1)}, u32[]{:S(2)}, u32[]{:S(2)}) collective-permute-start(f32[16,128]{1,0:T(8,128)S(1)} %get-tuple-element.64), channel_id=1, source_target_pairs={{0,32},{32,64},{64,96},{96,128},{128,160},{160,192},{192,224},{224... | collective-permute-start | bytes 24584 | tf_op jit(solution)/shard_map/ppermute | solution.py:535
  29.6 5.7 %collective-permute-start.7 = (f32[16,128]{1,0:T(8,128)S(1)}, f32[16,128]{1,0:T(8,128)S(1)}, u32[]{:S(2)}, u32[]{:S(2)}) collective-permute-start(f32[16,128]{1,0:T(8,128)S(1)} %get-tuple-element.65), channel_id=1, source_target_pairs={{32,0},{64,32},{96,64},{128,96},{160,128},{192,160},{224,192},{256... | collective-permute-start | bytes 24584 | tf_op jit(solution)/shard_map/ppermute | solution.py:535

commit v3 on v2

--- a/solution.py
+++ b/solution.py
@@ -126,7 +126,7 @@
 
 
 def stream_added(f_ref, low_ref, high_ref, geo_ref, x_ref, up_ref, down_ref):
-    low, high = in_order(low_ref[...], high_ref[...], "A" in SWAPS)
+    low, high = in_order(low_ref[...], high_ref[...], "stream", "A" in SWAPS)
     for i in range(8):
         a = f_ref[i, 0:8, :]
         b = f_ref[i, 8:16, :]
@@ -145,7 +145,7 @@
     up_ref[64:72, :] = geo_ref[...]
 
 
-def vert_added(x_ref, low_ref, high_ref, geo_ref, v_ref, g_ref, right_ref, left_ref):
+def vert_added(x_ref, low_ref, high_ref, geo_ref, v_ref, g_ref, right_ref, left_ref, one_ref, two_ref):
     v = lax.axis_index("vert")
     has_low = jnp.where(v > 0, 1.0, 0.0)
     has_high = jnp.where(v < 7, 1.0, 0.0)
@@ -181,6 +181,7 @@
     first = jnp.broadcast_to(extended[:, 0:1], (16, 128))
     right_ref[32:48, :] = jnp.where(wide < 64, last, 0.0)
     left_ref[32:48, :] = jnp.where(wide >= 64, first, 0.0)
+    one_ref[...], two_ref[...] = sent_in_order(right_ref[...], left_ref[...], "span", "C" in SWAPS)
 
 
 def node_rows(geo, d, t):
@@ -264,7 +265,7 @@
             if i in (0, 7):
                 outer[i].append(tile)
     top, bottom = [jnp.concatenate(outer[i], axis=0) for i in (7, 0)]
-    bottom_ref[...], top_ref[...] = in_order(bottom, top, "D" in SWAPS)
+    top_ref[...], bottom_ref[...] = sent_in_order(top, bottom, "stream", "D" in SWAPS)
 
 
 def share_maps():
@@ -358,7 +359,7 @@
     v1_ref, out_ref, field,
 ):
     share, layers = share_maps()
-    low, high = in_order(low_ref[...], high_ref[...], "D" in SWAPS)
+    low, high = in_order(low_ref[...], high_ref[...], "stream", "D" in SWAPS)
     quotient = jnp.broadcast_to(pre_ref[:, S : S + 1], (8, 128))
     v1 = [[None] * 2 for _ in range(8)]
     u = [[None] * 2 for _ in range(8)]
@@ -397,7 +398,7 @@
     rows += [sublane_sum(a) for a in (energy, 2.0 * cross_energy)] + zero_rows(3)
     row = lane_sums(jnp.concatenate(rows, axis=0), 0)
     row = row + lane_sums(jnp.concatenate(load_rows(face_tiles(v1), omega_ref), axis=0), 32)
-    out_ref[...] = jnp.broadcast_to(row + pre_ref[0:1, :], (32, 128))
+    out_ref[...] = jnp.broadcast_to(row + pre_ref[0:1, :], out_ref.shape)
 
 
 def merged(parts):
@@ -540,20 +541,41 @@
     return lax.ppermute(x, axis, pairs + [(b, a) for a, b in pairs])
 
 
-SWAPS = "A"
-
-
-def stream_exchange(one, two, swap):
+SWAPS = "AC"
+HEAD = 8
+LEAD = 22
+FIRST = 32
+SPLIT = 32
+
+
+def reduced(sums):
+    for axes, count, first in ((("vert", "span"), 32, LEAD), ("stream", 16, HEAD)):
+        lists = [[(first + n) % count for n in range(count)]]
+        sums = lax.all_to_all(sums.reshape(count, 1, 128), axes, 0, 0, axis_index_groups=lists).reshape(count, 128)
+        if count == 32:
+            sums = call(group_sums, [(16, 128)])(sums)[0]
+    return sums
+
+
+def exchange(one, two, axis, swap):
     if swap:
-        return swapped(one, "stream", 0), swapped(two, "stream", 1)
-    return shifted(one, "stream", 1), shifted(two, "stream", -1)
-
-
-def in_order(first, second, swap):
+        later = swapped(two, axis, 1)
+        return swapped(one, axis, 0), later
+    return shifted(one, axis, 1), shifted(two, axis, -1)
+
+
+def in_order(first, second, axis, swap):
     if not swap:
         return first, second
-    even = lax.axis_index("stream") % 2 == 0
+    even = lax.axis_index(axis) % 2 == 0
     return jnp.where(even, second, first), jnp.where(even, first, second)
+
+
+def sent_in_order(up, down, axis, swap):
+    if not swap:
+        return up, down
+    even = lax.axis_index(axis) % 2 == 0
+    return jnp.where(even, up, down), jnp.where(even, down, up)
 
 
 def per_device(
@@ -568,7 +590,7 @@
         top, bottom = [lax.dynamic_index_in_dim(forcing, at, 0, False) for at in (7 - 7 * odd, 7 * odd)]
     else:
         top, bottom = forcing[7], forcing[0]
-    low, high = stream_exchange(top, bottom, "A" in SWAPS)
+    low, high = exchange(top, bottom, "stream", "A" in SWAPS)
     geo = call(spread_geometry, [(8, 128)])(geometry.reshape(8, 16))[0]
     x, up, down = call(stream_added, [field, (72, 128), (72, 128)])(forcing, low, high, geo)
 
@@ -578,15 +600,17 @@
     table, codes, store_rows, motion = call(
         wall_table, [(256, 128), ((8, 64), jnp.int32), (32, 128), (2, 128)]
     )(wall_elem, wall_face, wall_store, store_motion.T, store_inverse, weight, arms)
-    low, high, table, codes = tie((low, high, table, codes))
-    wide, geo_wide, right, left = call(vert_added, [(8, 32, 128), (16, 128), (48, 128), (48, 128)])(
+    omega = call(functools.partial(wall_weights, 0, SPLIT), [(180, 8, 128)])(codes, table, smem=1)[0]
+    low, high, table, codes, omega = tie((low, high, table, codes, omega))
+    wide, geo_wide, right, left, to_one, to_two = call(vert_added, [(8, 32, 128), (16, 128)] + [(48, 128)] * 4)(
         x, low, high, geo
     )
 
-    right, left, table, codes = tie((right, left, table, codes))
-    low = shifted(right, "span", 1)
-    high = shifted(left, "span", -1)
-    omega = call(functools.partial(wall_weights, 0, 64), [(180, 8, 128)])(codes, table, smem=1)[0]
+    to_one, to_two, table, codes, omega = tie((to_one, to_two, table, codes, omega))
+    low, high = exchange(to_one, to_two, "span", "C" in SWAPS)
+    omega = call(functools.partial(wall_weights, SPLIT, 64), [(180, 8, 128)], input_output_aliases={2: 0})(
+        codes, table, omega, smem=1
+    )[0]
     low, high, omega = tie((low, high, omega))
     v0, local, part, top, bottom, maps = call(
         span_added,
@@ -594,20 +618,18 @@
         scratch_shapes=[pltpu.VMEM((288, 128), F32)],
     )(wide, geo_wide, right, left, low, high, lane_k, lane_i, rows, node_w)
 
-    low, high = stream_exchange(top, bottom, "D" in SWAPS)
+    low, high = exchange(top, bottom, "stream", "D" in SWAPS)
     pre = call(before_image, [(8, 128)])(v0, local, part, omega)[0]
-    v1, sums = call(image_sums, [field, (32, 128)], scratch_shapes=[pltpu.VMEM((128, 128), F32)])(
+    v1, sums = call(image_sums, [field, (FIRST, 128)], scratch_shapes=[pltpu.VMEM((128, 128), F32)])(
         v0, local, part, low, high, maps, omega, pre, lane_k, rows
     )
-    sums = lax.all_to_all(sums.reshape(32, 1, 128), ("vert", "span"), 0, 0)
-    sums = call(group_sums, [(16, 128)])(sums.reshape(32, 128))[0]
-    sums = lax.all_to_all(sums.reshape(16, 1, 128), "stream", 0, 0)
+    sums = reduced(sums)
     pressure, velocity = call(
         finish,
         [field, (3, 32, 128)],
         out_space=pltpu.HBM,
         scratch_shapes=[pltpu.VMEM(field, F32), pltpu.VMEM((3, 32, 128), F32), pltpu.SemaphoreType.DMA((2,))],
-    )(sums.reshape(16, 128), v0, v1, arms, store_rows, motion)
+    )(sums, v0, v1, arms, store_rows, motion)
     return pressure, velocity.reshape(1, 3, 4096)
 
 

time: 76.8 us -> 66.6 us (0.87)
  blocking collectives: 39.3 us -> 30.9 us
  waiting for transfers between devices: 7.65 us -> 5.24 us
    all_to_all x2, blocking collectives: 39.3 us -> 30.9 us  [reduced(): lax.all_to_all(sums.reshape(count, 1, 128), axes, 0, 0, axis_index_groups...]
    ppermute x6 -> x4, starting transfers between devices: 13.6 us -> 9.1 us  [shifted(): return lax.ppermute(x, axis, pairs)]
    ppermute x2 -> x4, starting transfers between devices: 8.04 us -> 12 us  [swapped(): return lax.ppermute(x, axis, pairs + [(b, a) for a, b in pairs])]
    ppermute x6 -> x4, waiting for transfers between devices: 6.76 us -> 4.35 us  [shifted(): return lax.ppermute(x, axis, pairs)]
    pallas_call x10 -> x11, Pallas kernels: 6.15 us -> 6.76 us  [run(): pl.pallas_call(body, out_shape=[jax.ShapeDtypeStruct(*s) for s in shapes]...]
  transfers between devices with their start and end apart: 8 -> 8, of which waited for: 5 -> 3; matrix products, arithmetic and copies ran while one was open for 0% -> 0% of each run, Pallas kernels for 4% -> 6%
where the time goes in v3:
time: 66.6 us; the launch traced here: 65.6 us
  blocking collectives  30.9 us (46%)
  starting transfers between devices  21.1 us (32%)
  Pallas kernels  6.76 us (10%)
  waiting for transfers between devices  5.24 us (8%)
  between operations  0.88 us (1%)
  local copies, waits for them, and re-layouts  0.82 us (1%)
    all_to_all x2, blocking collectives, reduced(): lax.all_to_all(sums.reshape(count, 1, 128), axes, 0, 0, axis_index_groups...  30.9 us
    ppermute x4, starting transfers between devices, swapped(): return lax.ppermute(x, axis, pairs + [(b, a) for a, b in pairs])  12 us
    ppermute x4, starting transfers between devices, shifted(): return lax.ppermute(x, axis, pairs)  9.1 us
    pallas_call x11, Pallas kernels, run(): pl.pallas_call(body, out_shape=[jax.ShapeDtypeStruct(*s) for s in shapes]...  6.76 us
    ppermute x4, waiting for transfers between devices, shifted(): return lax.ppermute(x, axis, pairs)  4.35 us
  transfers between devices with their start and end apart: 8, of which 3 were waited for; matrix products, arithmetic and copies ran while one was open for 0% of the time, Pallas kernels for 6%

profile of v3, /device:TPU:1, one launch (start us, length us, event | category | flops | bytes accessed | tf_op | source)
XLA Modules:
  0.0 65.6 jit_solution(12265815296034762328)
XLA Ops:
  0.6 0.0 copy-start.3
  0.7 0.7 %dynamic-slice_bitcast_fusion = (f32[16,128]{1,0:T(8,128)S(1)}, f32[16,128]{1,0:T(8,128)S(1)}) fusion(f32[8,16,128]{2,1,0:T(8,128)} %f_ref.1, s32[]{:T(128)S(6)} %select_n.16, s32[]{:T(128)S(6)} %select_n.15), kind=kLoop, calls=%fused_computation | loop fusion | bytes 32776 | tf_op jit(solution)/shard_map/jit(dynamic_index_in_dim)/squeeze | solution.py:590
  1.4 0.0 copy-start.7
  1.4 0.8 %collective-permute-start.1 = (f32[16,128]{1,0:T(8,128)S(1)}, f32[16,128]{1,0:T(8,128)S(1)}, u32[]{:S(2)}, u32[]{:S(2)}) collective-permute-start(f32[16,128]{1,0:T(8,128)S(1)} %get-tuple-element.88), channel_id=1, source_target_pairs={{32,64},{96,128},{160,192},{224,256},{288,320},{352,384},{416,448}... | collective-permute-start | bytes 24584 | tf_op jit(solution)/shard_map/ppermute | solution.py:541
  2.2 7.3 %collective-permute-start = (f32[16,128]{1,0:T(8,128)S(1)}, f32[16,128]{1,0:T(8,128)S(1)}, u32[]{:S(2)}, u32[]{:S(2)}) collective-permute-start(f32[16,128]{1,0:T(8,128)S(1)} %get-tuple-element.89), channel_id=1, source_target_pairs={{0,32},{64,96},{128,160},{192,224},{256,288},{320,352},{384,416},{... | collective-permute-start | bytes 24584 | tf_op jit(solution)/shard_map/ppermute | solution.py:541
  9.5 0.0 copy-done.7
  9.5 0.1 shard_map.140.geo_ref
  9.6 0.0 copy-start.2
  9.6 0.0 collective-permute-done.1.high_ref
  9.6 0.9 %collective-permute-done.low_ref = f32[16,128]{1,0:T(8,128)S(1)} collective-permute-done((f32[16,128]{1,0:T(8,128)S(1)}, f32[16,128]{1,0:T(8,128)S(1)}, u32[]{:S(2)}, u32[]{:S(2)}) %collective-permute-start) | collective-permute-done | bytes 8224 | tf_op jit(solution)/shard_map/ppermute | solution.py:541
  10.5 0.0 copy-done.3
  10.5 0.0 copy-start.5
  10.5 0.0 copy-start.9
  10.5 0.0 copy-start.8
  10.5 0.0 copy-start.10
  10.6 0.0 copy-start.11
  10.6 0.0 copy-start.12
  10.6 3.0 %collective-permute-start.2 = (f32[72,128]{1,0:T(8,128)S(1)}, f32[72,128]{1,0:T(8,128)S(1)}, u32[]{:S(2)}, u32[]{:S(2)}) collective-permute-start(f32[72,128]{1,0:T(8,128)S(1)} %get-tuple-element.45), channel_id=1, source_target_pairs={{0,4},{4,8},{8,12},{12,16},{16,20},{20,24},{24,28},{28,0},{1,5},{5... | collective-permute-start | bytes 110600 | tf_op jit(solution)/shard_map/ppermute | solution.py:536
  13.6 1.1 %collective-permute-start.3 = (f32[72,128]{1,0:T(8,128)S(1)}, f32[72,128]{1,0:T(8,128)S(1)}, u32[]{:S(2)}, u32[]{:S(2)}) collective-permute-start(f32[72,128]{1,0:T(8,128)S(1)} %get-tuple-element.46), channel_id=1, source_target_pairs={{0,28},{4,0},{8,4},{12,8},{16,12},{20,16},{24,20},{28,24},{1,29},{... | collective-permute-start | bytes 110600 | tf_op jit(solution)/shard_map/ppermute | solution.py:536
  14.7 0.0 copy-done.2
  14.8 0.0 copy-done.5
  14.8 0.0 copy-done.9
  14.8 0.0 copy-done.8
  14.8 0.0 copy-done.10
  14.8 0.0 copy-done.11
  14.8 0.0 copy-done.12
  14.8 0.3 shard_map.142
  15.1 1.5 %shard_map.143.rest_0_ = f32[180,8,128]{2,1,0:T(8,128)S(1)} custom-call(s32[8,64]{1,0:T(8,128)S(1)} %get-tuple-element.64.code_ref, f32[256,128]{1,0:T(8,128)S(1)} %get-tuple-element.65.table_ref), custom_call_target="tpu_custom_call" | custom-call | flops 2000000 | bytes 200000 | tf_op jit(solution)/shard_map/pallas_call | solution.py:115
  16.6 0.0 collective-permute-done.2.low_ref
  16.6 0.4 collective-permute-done.3.high_ref
  17.0 0.3 shard_map.144
  17.3 0.0 copy-start
  17.3 0.0 copy-start.1
  17.3 0.0 copy-start.4
  17.3 3.3 %collective-permute-start.4 = (f32[48,128]{1,0:T(8,128)S(1)}, f32[48,128]{1,0:T(8,128)S(1)}, u32[]{:S(2)}, u32[]{:S(2)}) collective-permute-start(f32[48,128]{1,0:T(8,128)S(1)} %get-tuple-element.62), channel_id=1, source_target_pairs={{0,1},{2,3},{1,0},{3,2},{4,5},{6,7},{5,4},{7,6},{8,9},{10,11},{9,8... | collective-permute-start | bytes 73736 | tf_op jit(solution)/shard_map/ppermute | solution.py:541
  20.6 0.7 %collective-permute-start.5 = (f32[48,128]{1,0:T(8,128)S(1)}, f32[48,128]{1,0:T(8,128)S(1)}, u32[]{:S(2)}, u32[]{:S(2)}) collective-permute-start(f32[48,128]{1,0:T(8,128)S(1)} %get-tuple-element.63), channel_id=1, source_target_pairs={{1,2},{2,1},{5,6},{6,5},{9,10},{10,9},{13,14},{14,13},{17,18},{18,... | collective-permute-start | bytes 73736 | tf_op jit(solution)/shard_map/ppermute | solution.py:541
  21.2 0.0 copy-start.6
  21.3 1.5 %shard_map.145.omega_ref = f32[180,8,128]{2,1,0:T(8,128)S(1)} custom-call(s32[8,64]{1,0:T(8,128)S(1)} %get-tuple-element.64.code_ref, f32[256,128]{1,0:T(8,128)S(1)} %get-tuple-element.65.table_ref, f32[180,8,128]{2,1,0:T(8,128)S(1)} %shard_map.143.rest_0_), custom_call_target="tpu_custom_call", output_to_operand_aliasing={{}: (2, {})} | custom-call | flops 2000000 | bytes 200000 | tf_op jit(solution)/shard_map/pallas_call | solution.py:115
  22.7 0.0 collective-permute-done.4.low_ref
  22.7 0.0 collective-permute-done.5.high_ref
  22.7 0.0 copy-done
  22.7 0.0 copy-done.1
  22.7 0.0 copy-done.4
  22.7 0.0 copy-done.6
  22.8 0.8 %shard_map.146 = (f32[8,16,128]{2,1,0:T(8,128)S(1)}, f32[8,16,128]{2,1,0:T(8,128)S(1)}, f32[8,16,128]{2,1,0:T(8,128)S(1)}, f32[16,128]{1,0:T(8,128)S(1)}, f32[16...) custom-call(f32[8,32,128]{2,1,0:T(8,128)S(1)} %get-tuple-element.53.v_ref, f32[16,128]{1,0:T(8,128)S(1)} %get-tuple-element.54.g_ref, ...), custom_call_target="tpu_custom_call" | custom-call | flops 2000000 | bytes 200000 | tf_op jit(solution)/shard_map/pallas_call | solution.py:115
  23.5 3.6 %collective-permute-start.6 = (f32[16,128]{1,0:T(8,128)S(1)}, f32[16,128]{1,0:T(8,128)S(1)}, u32[]{:S(2)}, u32[]{:S(2)}) collective-permute-start(f32[16,128]{1,0:T(8,128)S(1)} %get-tuple-element.72), channel_id=1, source_target_pairs={{0,32},{32,64},{64,96},{96,128},{128,160},{160,192},{192,224},{224... | collective-permute-start | bytes 24584 | tf_op jit(solution)/shard_map/ppermute | solution.py:536
  27.2 1.3 %collective-permute-start.7 = (f32[16,128]{1,0:T(8,128)S(1)}, f32[16,128]{1,0:T(8,128)S(1)}, u32[]{:S(2)}, u32[]{:S(2)}) collective-permute-start(f32[16,128]{1,0:T(8,128)S(1)} %get-tuple-element.73), channel_id=1, source_target_pairs={{32,0},{64,32},{96,64},{128,96},{160,128},{192,160},{224,192},{256... | collective-permute-start | bytes 24584 | tf_op jit(solution)/shard_map/ppermute | solution.py:536
  28.5 0.4 shard_map.147.pre_ref
  28.9 0.0 collective-permute-done.6.low_ref
  28.9 4.0 %collective-permute-done.7.high_ref = f32[16,128]{1,0:T(8,128)S(1)} collective-permute-done((f32[16,128]{1,0:T(8,128)S(1)}, f32[16,128]{1,0:T(8,128)S(1)}, u32[]{:S(2)}, u32[]{:S(2)}) %collective-permute-start.7) | collective-permute-done | bytes 8224 | tf_op jit(solution)/shard_map/ppermute | solution.py:536
  32.9 0.4 shard_map.148
  33.3 13.5 %all_to_all.10 = f32[32,1,128]{2,1,0:T(1,128)S(1)} all-to-all(f32[32,1,128]{2,1,0:T(1,128)S(1)} %bitcast.23), channel_id=1, replica_groups={{22,23,24,25,26,27,28,29,30,31,0,1,2,3,4,5,6,7,8,9,10,11,12,13,14,15,16..., dimensions={0} | all-to-all | bytes 32768 | tf_op jit(solution)/shard_map/all_to_all | solution.py:554
  46.8 0.1 shard_map.149
  46.9 17.4 %all_to_all.11 = f32[16,1,128]{2,1,0:T(1,128)S(1)} all-to-all(f32[16,1,128]{2,1,0:T(1,128)S(1)} %bitcast.21), channel_id=1, replica_groups={{256,288,320,352,384,416,448,480,0,32,64,96,128,160,192,224},{257,289,3..., dimensions={0} | all-to-all | bytes 16384 | tf_op jit(solution)/shard_map/all_to_all | solution.py:554
  64.3 1.4 %shard_map.150 = (f32[8,16,128]{2,1,0:T(8,128)}, f32[3,32,128]{2,1,0:T(8,128)}) custom-call(f32[16,128]{1,0:T(8,128)S(1)} %bitcast.20, f32[8,16,128]{2,1,0:T(8,128)S(1)} %get-tuple-element.69.v0_ref, f32[8,16,128]{2,1,0:T(8,128)S(1)} %get-tuple-element.77.v1_ref, f32[3,32,128]{2,1,0:T(8,128)S(1)} %bitcast.18, f32[32,128]{1,0:T(8,128)S(1)} %get-tuple-element.78.store_ref, ...), custom_call_target="tpu_custom_call" | custom-call | flops 2000000 | bytes 200000 | tf_op jit(solution)/shard_map/pallas_call | solution.py:115
  (1 shorter events, 0.0 us)
Async XLA Ops:
  0.6 9.9 %copy-start.3 = (f32[8,16,128]{2,1,0:T(8,128)S(1)}, f32[8,16,128]{2,1,0:T(8,128)}, u32[]{:S(2)}) copy-start(f32[8,16,128]{2,1,0:T(8,128)} %f_ref.1) | copy-start | bytes 196612
  1.4 8.1 %copy-start.7 = (f32[4,1,2,16]{3,2,1,0:T(2,128)S(1)}, f32[4,1,2,16]{3,2,1,0:T(2,128)}, u32[]{:S(2)}) copy-start(f32[4,1,2,16]{3,2,1,0:T(2,128)} %param.14) | copy-start | bytes 1540
  1.4 8.2 %collective-permute-start.1 = (f32[16,128]{1,0:T(8,128)S(1)}, f32[16,128]{1,0:T(8,128)S(1)}, u32[]{:S(2)}, u32[]{:S(2)}) collective-permute-start(f32[16,128]{1,0:T(8,128)S(1)} %get-tuple-element.88), channel_id=1, source_target_pairs={{32,64},{96,128},{160,192},{224,256},{288,320},{352,384},{416,448}... | collective-permute-start | bytes 24584 | tf_op jit(solution)/shard_map/ppermute | solution.py:541
  2.2 8.3 %collective-permute-start = (f32[16,128]{1,0:T(8,128)S(1)}, f32[16,128]{1,0:T(8,128)S(1)}, u32[]{:S(2)}, u32[]{:S(2)}) collective-permute-start(f32[16,128]{1,0:T(8,128)S(1)} %get-tuple-element.89), channel_id=1, source_target_pairs={{0,32},{64,96},{128,160},{192,224},{256,288},{320,352},{384,416},{... | collective-permute-start | bytes 24584 | tf_op jit(solution)/shard_map/ppermute | solution.py:541
  9.6 5.2 %copy-start.2 = (f32[1,3,4096]{2,0,1:T(1,128)S(1)}, f32[1,3,4096]{2,0,1:T(1,128)}, u32[]{:S(2)}) copy-start(f32[1,3,4096]{2,0,1:T(1,128)} %param.19) | copy-start | bytes 147460
  10.5 4.3 %copy-start.5 = (f32[1,4096]{1,0:T(1,128)S(1)}, f32[1,4096]{1,0:T(1,128)}, u32[]{:S(2)}) copy-start(f32[1,4096]{1,0:T(1,128)} %param.18) | copy-start | bytes 49156
  10.5 4.2 %copy-start.9 = (f32[4,4]{1,0:T(4,128)S(1)}, f32[4,4]{1,0:T(4,128)}, u32[]{:S(2)}) copy-start(f32[4,4]{1,0:T(4,128)} %inverse_ref.1) | copy-start | bytes 196
  10.5 4.2 %copy-start.8 = (f32[6,4]{0,1:T(4,128)S(1)}, f32[6,4]{0,1:T(4,128)}, u32[]{:S(2)}) copy-start(f32[6,4]{0,1:T(4,128)} %param.20) | copy-start | bytes 292
  10.5 4.2 %copy-start.10 = (s32[1,64]{1,0:T(1,128)S(1)}, s32[1,64]{1,0:T(1,128)}, u32[]{:S(2)}) copy-start(s32[1,64]{1,0:T(1,128)} %elem_ref.1) | copy-start | bytes 772
  10.6 4.2 %copy-start.11 = (s32[1,64]{1,0:T(1,128)S(1)}, s32[1,64]{1,0:T(1,128)}, u32[]{:S(2)}) copy-start(s32[1,64]{1,0:T(1,128)} %face_ref.1) | copy-start | bytes 772
  10.6 4.2 %copy-start.12 = (s32[1,64]{1,0:T(1,128)S(1)}, s32[1,64]{1,0:T(1,128)}, u32[]{:S(2)}) copy-start(s32[1,64]{1,0:T(1,128)} %stores_ref.1) | copy-start | bytes 772
  10.6 6.0 %collective-permute-start.2 = (f32[72,128]{1,0:T(8,128)S(1)}, f32[72,128]{1,0:T(8,128)S(1)}, u32[]{:S(2)}, u32[]{:S(2)}) collective-permute-start(f32[72,128]{1,0:T(8,128)S(1)} %get-tuple-element.45), channel_id=1, source_target_pairs={{0,4},{4,8},{8,12},{12,16},{16,20},{20,24},{24,28},{28,0},{1,5},{5... | collective-permute-start | bytes 110600 | tf_op jit(solution)/shard_map/ppermute | solution.py:536
  13.6 3.4 %collective-permute-start.3 = (f32[72,128]{1,0:T(8,128)S(1)}, f32[72,128]{1,0:T(8,128)S(1)}, u32[]{:S(2)}, u32[]{:S(2)}) collective-permute-start(f32[72,128]{1,0:T(8,128)S(1)} %get-tuple-element.46), channel_id=1, source_target_pairs={{0,28},{4,0},{8,4},{12,8},{16,12},{20,16},{24,20},{28,24},{1,29},{... | collective-permute-start | bytes 110600 | tf_op jit(solution)/shard_map/ppermute | solution.py:536
  17.3 5.4 %copy-start = (f32[256,256]{1,0:T(8,128)S(1)}, f32[256,256]{1,0:T(8,128)}, u32[]{:S(2)}) copy-start(f32[256,256]{1,0:T(8,128)} %constant.40.clone.kr_ref) | copy-start | bytes 786436
  17.3 5.4 %copy-start.1 = (f32[128,128]{1,0:T(8,128)S(1)}, f32[128,128]{1,0:T(8,128)}, u32[]{:S(2)}) copy-start(f32[128,128]{1,0:T(8,128)} %constant.38.clone.kk_ref) | copy-start | bytes 196612
  17.3 5.4 %copy-start.4 = (f32[128,128]{1,0:T(8,128)S(1)}, f32[128,128]{1,0:T(8,128)}, u32[]{:S(2)}) copy-start(f32[128,128]{1,0:T(8,128)} %constant.39.clone.ki_ref) | copy-start | bytes 196612
  17.3 5.4 %collective-permute-start.4 = (f32[48,128]{1,0:T(8,128)S(1)}, f32[48,128]{1,0:T(8,128)S(1)}, u32[]{:S(2)}, u32[]{:S(2)}) collective-permute-start(f32[48,128]{1,0:T(8,128)S(1)} %get-tuple-element.62), channel_id=1, source_target_pairs={{0,1},{2,3},{1,0},{3,2},{4,5},{6,7},{5,4},{7,6},{8,9},{10,11},{9,8... | collective-permute-start | bytes 73736 | tf_op jit(solution)/shard_map/ppermute | solution.py:541
  20.6 2.1 %collective-permute-start.5 = (f32[48,128]{1,0:T(8,128)S(1)}, f32[48,128]{1,0:T(8,128)S(1)}, u32[]{:S(2)}, u32[]{:S(2)}) collective-permute-start(f32[48,128]{1,0:T(8,128)S(1)} %get-tuple-element.63), channel_id=1, source_target_pairs={{1,2},{2,1},{5,6},{6,5},{9,10},{10,9},{13,14},{14,13},{17,18},{18,... | collective-permute-start | bytes 73736 | tf_op jit(solution)/shard_map/ppermute | solution.py:541
  21.2 1.5 %copy-start.6 = (f32[24,128]{1,0:T(8,128)S(1)}, f32[24,128]{1,0:T(8,128)}, u32[]{:S(2)}) copy-start(f32[24,128]{1,0:T(8,128)} %constant.41.clone.w_ref) | copy-start | bytes 36868
  23.5 5.4 %collective-permute-start.6 = (f32[16,128]{1,0:T(8,128)S(1)}, f32[16,128]{1,0:T(8,128)S(1)}, u32[]{:S(2)}, u32[]{:S(2)}) collective-permute-start(f32[16,128]{1,0:T(8,128)S(1)} %get-tuple-element.72), channel_id=1, source_target_pairs={{0,32},{32,64},{64,96},{96,128},{128,160},{160,192},{192,224},{224... | collective-permute-start | bytes 24584 | tf_op jit(solution)/shard_map/ppermute | solution.py:536
  27.2 5.7 %collective-permute-start.7 = (f32[16,128]{1,0:T(8,128)S(1)}, f32[16,128]{1,0:T(8,128)S(1)}, u32[]{:S(2)}, u32[]{:S(2)}) collective-permute-start(f32[16,128]{1,0:T(8,128)S(1)} %get-tuple-element.73), channel_id=1, source_target_pairs={{32,0},{64,32},{96,64},{128,96},{160,128},{192,160},{224,192},{256... | collective-permute-start | bytes 24584 | tf_op jit(solution)/shard_map/ppermute | solution.py:536

commit v4 on v3

--- a/solution.py
+++ b/solution.py
@@ -126,7 +126,7 @@
 
 
 def stream_added(f_ref, low_ref, high_ref, geo_ref, x_ref, up_ref, down_ref):
-    low, high = in_order(low_ref[...], high_ref[...], "stream", "A" in SWAPS)
+    low, high = in_order(low_ref[...], high_ref[...], "A")
     for i in range(8):
         a = f_ref[i, 0:8, :]
         b = f_ref[i, 8:16, :]
@@ -139,8 +139,9 @@
         a, b = join_rows(a, b)
         x_ref[i, 0:8, :] = a
         x_ref[i, 8:16, :] = b
-        down_ref[8 * i : 8 * i + 8, :] = a
-        up_ref[8 * i : 8 * i + 8, :] = b
+        one, two = sent_in_order(b, a, "B")
+        up_ref[8 * i : 8 * i + 8, :] = one
+        down_ref[8 * i : 8 * i + 8, :] = two
     down_ref[64:72, :] = geo_ref[...]
     up_ref[64:72, :] = geo_ref[...]
 
@@ -154,8 +155,9 @@
     left = [jnp.zeros((8, 128), F32) for _ in range(4)]
     for i in range(8):
         rows = slice(8 * i, 8 * i + 8)
-        low, a = join_rows(low_ref[rows, :] * has_low, x_ref[i, 0:8, :])
-        b, high = join_rows(x_ref[i, 8:16, :], high_ref[rows, :] * has_high)
+        low, high = in_order(low_ref[rows, :], high_ref[rows, :], "B")
+        low, a = join_rows(low * has_low, x_ref[i, 0:8, :])
+        b, high = join_rows(x_ref[i, 8:16, :], high * has_high)
         for t, tile in enumerate((low, a, b, high)):
             tile = join_lanes(tile)
             v_ref[i, 8 * t : 8 * t + 8, :] = tile
@@ -167,8 +169,8 @@
         right_ref[8 * t : 8 * t + 8, :] = right[t]
         left_ref[8 * t : 8 * t + 8, :] = left[t]
     geo = geo_ref[...]
-    geo_low = low_ref[64:72, :] * has_low
-    geo_high = high_ref[64:72, :] * has_high
+    geo_low, geo_high = in_order(low_ref[64:72, :], high_ref[64:72, :], "B")
+    geo_low, geo_high = geo_low * has_low, geo_high * has_high
     rows = []
     for d in range(4):
         rows.append(geo_low[2 * d + 1 : 2 * d + 2, :])
@@ -181,7 +183,7 @@
     first = jnp.broadcast_to(extended[:, 0:1], (16, 128))
     right_ref[32:48, :] = jnp.where(wide < 64, last, 0.0)
     left_ref[32:48, :] = jnp.where(wide >= 64, first, 0.0)
-    one_ref[...], two_ref[...] = sent_in_order(right_ref[...], left_ref[...], "span", "C" in SWAPS)
+    one_ref[...], two_ref[...] = sent_in_order(right_ref[...], left_ref[...], "C")
 
 
 def node_rows(geo, d, t):
@@ -265,7 +267,7 @@
             if i in (0, 7):
                 outer[i].append(tile)
     top, bottom = [jnp.concatenate(outer[i], axis=0) for i in (7, 0)]
-    top_ref[...], bottom_ref[...] = sent_in_order(top, bottom, "stream", "D" in SWAPS)
+    top_ref[...], bottom_ref[...] = sent_in_order(top, bottom, "D")
 
 
 def share_maps():
@@ -359,7 +361,7 @@
     v1_ref, out_ref, field,
 ):
     share, layers = share_maps()
-    low, high = in_order(low_ref[...], high_ref[...], "stream", "D" in SWAPS)
+    low, high = in_order(low_ref[...], high_ref[...], "D")
     quotient = jnp.broadcast_to(pre_ref[:, S : S + 1], (8, 128))
     v1 = [[None] * 2 for _ in range(8)]
     u = [[None] * 2 for _ in range(8)]
@@ -541,40 +543,49 @@
     return lax.ppermute(x, axis, pairs + [(b, a) for a, b in pairs])
 
 
-SWAPS = "AC"
-HEAD = 8
-LEAD = 22
-FIRST = 32
+SWAPS = "ACD"
 SPLIT = 32
 
 
+STAGES = ((("vert", "span"), 32, 22), ("stream", 16, 8))
+
+
 def reduced(sums):
-    for axes, count, first in ((("vert", "span"), 32, LEAD), ("stream", 16, HEAD)):
+    for at, (axes, count, first) in enumerate(STAGES):
         lists = [[(first + n) % count for n in range(count)]]
         sums = lax.all_to_all(sums.reshape(count, 1, 128), axes, 0, 0, axis_index_groups=lists).reshape(count, 128)
-        if count == 32:
-            sums = call(group_sums, [(16, 128)])(sums)[0]
+        if at == 0:
+            sums = call(group_sums, [(STAGES[1][1], 128)])(sums)[0]
     return sums
 
 
-def exchange(one, two, axis, swap):
-    if swap:
-        later = swapped(two, axis, 1)
-        return swapped(one, axis, 0), later
-    return shifted(one, axis, 1), shifted(two, axis, -1)
-
-
-def in_order(first, second, axis, swap):
-    if not swap:
+AXIS = {"A": "stream", "B": "vert", "C": "span", "D": "stream"}
+FLIPS = "D"
+
+
+def swaps_at(stage):
+    return int(stage in FLIPS)
+
+
+def exchange(one, two, stage):
+    axis = AXIS[stage]
+    if stage in SWAPS:
+        first = swaps_at(stage)
+        return swapped(one, axis, first), swapped(two, axis, 1 - first)
+    return shifted(one, axis, 1, stage == "B"), shifted(two, axis, -1, stage == "B")
+
+
+def in_order(first, second, stage):
+    if stage not in SWAPS:
         return first, second
-    even = lax.axis_index(axis) % 2 == 0
+    even = lax.axis_index(AXIS[stage]) % 2 == swaps_at(stage)
     return jnp.where(even, second, first), jnp.where(even, first, second)
 
 
-def sent_in_order(up, down, axis, swap):
-    if not swap:
+def sent_in_order(up, down, stage):
+    if stage not in SWAPS:
         return up, down
-    even = lax.axis_index(axis) % 2 == 0
+    even = lax.axis_index(AXIS[stage]) % 2 == swaps_at(stage)
     return jnp.where(even, up, down), jnp.where(even, down, up)
 
 
@@ -586,17 +597,16 @@
     tie = lax.optimization_barrier
 
     if "A" in SWAPS:
-        odd = lax.axis_index("stream") % 2
+        odd = (lax.axis_index("stream") + swaps_at("A")) % 2
         top, bottom = [lax.dynamic_index_in_dim(forcing, at, 0, False) for at in (7 - 7 * odd, 7 * odd)]
     else:
         top, bottom = forcing[7], forcing[0]
-    low, high = exchange(top, bottom, "stream", "A" in SWAPS)
+    low, high = exchange(top, bottom, "A")
     geo = call(spread_geometry, [(8, 128)])(geometry.reshape(8, 16))[0]
     x, up, down = call(stream_added, [field, (72, 128), (72, 128)])(forcing, low, high, geo)
 
     up, down, weight, arms = tie((up, down, wall_weight.reshape(32, 128), wall_arm.reshape(3, 32, 128)))
-    low = shifted(up, "vert", 1, ring=True)
-    high = shifted(down, "vert", -1, ring=True)
+    low, high = exchange(up, down, "B")
     table, codes, store_rows, motion = call(
         wall_table, [(256, 128), ((8, 64), jnp.int32), (32, 128), (2, 128)]
     )(wall_elem, wall_face, wall_store, store_motion.T, store_inverse, weight, arms)
@@ -607,7 +617,7 @@
     )
 
     to_one, to_two, table, codes, omega = tie((to_one, to_two, table, codes, omega))
-    low, high = exchange(to_one, to_two, "span", "C" in SWAPS)
+    low, high = exchange(to_one, to_two, "C")
     omega = call(functools.partial(wall_weights, SPLIT, 64), [(180, 8, 128)], input_output_aliases={2: 0})(
         codes, table, omega, smem=1
     )[0]
@@ -618,9 +628,9 @@
         scratch_shapes=[pltpu.VMEM((288, 128), F32)],
     )(wide, geo_wide, right, left, low, high, lane_k, lane_i, rows, node_w)
 
-    low, high = exchange(top, bottom, "stream", "D" in SWAPS)
+    low, high = exchange(top, bottom, "D")
     pre = call(before_image, [(8, 128)])(v0, local, part, omega)[0]
-    v1, sums = call(image_sums, [field, (FIRST, 128)], scratch_shapes=[pltpu.VMEM((128, 128), F32)])(
+    v1, sums = call(image_sums, [field, (STAGES[0][1], 128)], scratch_shapes=[pltpu.VMEM((128, 128), F32)])(
         v0, local, part, low, high, maps, omega, pre, lane_k, rows
     )
     sums = reduced(sums)

time: 66.6 us -> 65.9 us (0.989)
  waiting for transfers between devices: 5.24 us -> 1.87 us
  starting transfers between devices: 21.1 us -> 24.4 us
  blocking collectives: 30.9 us -> 30.1 us
    ppermute x4 -> x6, starting transfers between devices: 12 us -> 20.3 us  [swapped(): return lax.ppermute(x, axis, pairs + [(b, a) for a, b in pairs])]
    ppermute x4 -> x2, starting transfers between devices: 9.1 us -> 4.17 us  [shifted(): return lax.ppermute(x, axis, pairs)]
    ppermute x4 -> x2, waiting for transfers between devices: 4.35 us -> 0.37 us  [shifted(): return lax.ppermute(x, axis, pairs)]
    all_to_all x2, blocking collectives: 30.9 us -> 30.1 us  [reduced(): lax.all_to_all(sums.reshape(count, 1, 128), axes, 0, 0, axis_index_groups...]
    ppermute x4 -> x6, waiting for transfers between devices: 0.89 us -> 1.49 us  [swapped(): return lax.ppermute(x, axis, pairs + [(b, a) for a, b in pairs])]
where the time goes in v4:
time: 65.9 us; the launch traced here: 64.9 us
  blocking collectives  30.1 us (46%)
  starting transfers between devices  24.4 us (37%)
  Pallas kernels  6.76 us (10%)
  waiting for transfers between devices  1.87 us (3%)
  between operations  0.88 us (1%)
  local copies, waits for them, and re-layouts  0.82 us (1%)
    all_to_all x2, blocking collectives, reduced(): lax.all_to_all(sums.reshape(count, 1, 128), axes, 0, 0, axis_index_groups...  30.1 us
    ppermute x6, starting transfers between devices, swapped(): return lax.ppermute(x, axis, pairs + [(b, a) for a, b in pairs])  20.3 us
    pallas_call x11, Pallas kernels, run(): pl.pallas_call(body, out_shape=[jax.ShapeDtypeStruct(*s) for s in shapes]...  6.76 us
    ppermute x2, starting transfers between devices, shifted(): return lax.ppermute(x, axis, pairs)  4.17 us
    ppermute x6, waiting for transfers between devices, swapped(): return lax.ppermute(x, axis, pairs + [(b, a) for a, b in pairs])  1.49 us
  transfers between devices with their start and end apart: 8, of which 3 were waited for; matrix products, arithmetic and copies ran while one was open for 0% of the time, Pallas kernels for 6%

profile of v4, /device:TPU:1, one launch (start us, length us, event | category | flops | bytes accessed | tf_op | source)
XLA Modules:
  0.0 64.9 jit_solution(2805633770400209608)
XLA Ops:
  0.6 0.0 copy-start.3
  0.7 0.7 %dynamic-slice_bitcast_fusion = (f32[16,128]{1,0:T(8,128)S(1)}, f32[16,128]{1,0:T(8,128)S(1)}) fusion(f32[8,16,128]{2,1,0:T(8,128)} %f_ref.1, s32[]{:T(128)S(6)} %select_n.16, s32[]{:T(128)S(6)} %select_n.15), kind=kLoop, calls=%fused_computation | loop fusion | bytes 32776 | tf_op jit(solution)/shard_map/jit(dynamic_index_in_dim)/squeeze | solution.py:601
  1.4 0.0 copy-start.7
  1.4 0.8 %collective-permute-start.1 = (f32[16,128]{1,0:T(8,128)S(1)}, f32[16,128]{1,0:T(8,128)S(1)}, u32[]{:S(2)}, u32[]{:S(2)}) collective-permute-start(f32[16,128]{1,0:T(8,128)S(1)} %get-tuple-element.88), channel_id=1, source_target_pairs={{32,64},{96,128},{160,192},{224,256},{288,320},{352,384},{416,448}... | collective-permute-start | bytes 24584 | tf_op jit(solution)/shard_map/ppermute | solution.py:543
  2.2 7.3 %collective-permute-start = (f32[16,128]{1,0:T(8,128)S(1)}, f32[16,128]{1,0:T(8,128)S(1)}, u32[]{:S(2)}, u32[]{:S(2)}) collective-permute-start(f32[16,128]{1,0:T(8,128)S(1)} %get-tuple-element.89), channel_id=1, source_target_pairs={{0,32},{64,96},{128,160},{192,224},{256,288},{320,352},{384,416},{... | collective-permute-start | bytes 24584 | tf_op jit(solution)/shard_map/ppermute | solution.py:543
  9.5 0.0 copy-done.7
  9.5 0.1 shard_map.140.geo_ref
  9.6 0.0 copy-start.2
  9.6 0.0 collective-permute-done.1.high_ref
  9.6 0.9 %collective-permute-done.low_ref = f32[16,128]{1,0:T(8,128)S(1)} collective-permute-done((f32[16,128]{1,0:T(8,128)S(1)}, f32[16,128]{1,0:T(8,128)S(1)}, u32[]{:S(2)}, u32[]{:S(2)}) %collective-permute-start) | collective-permute-done | bytes 8224 | tf_op jit(solution)/shard_map/ppermute | solution.py:543
  10.5 0.0 copy-done.3
  10.5 0.0 copy-start.5
  10.5 0.0 copy-start.9
  10.5 0.0 copy-start.8
  10.5 0.0 copy-start.10
  10.6 0.0 copy-start.11
  10.6 0.0 copy-start.12
  10.6 3.0 %collective-permute-start.2 = (f32[72,128]{1,0:T(8,128)S(1)}, f32[72,128]{1,0:T(8,128)S(1)}, u32[]{:S(2)}, u32[]{:S(2)}) collective-permute-start(f32[72,128]{1,0:T(8,128)S(1)} %get-tuple-element.45), channel_id=1, source_target_pairs={{0,4},{4,8},{8,12},{12,16},{16,20},{20,24},{24,28},{28,0},{1,5},{5... | collective-permute-start | bytes 110600 | tf_op jit(solution)/shard_map/ppermute | solution.py:538
  13.6 1.1 %collective-permute-start.3 = (f32[72,128]{1,0:T(8,128)S(1)}, f32[72,128]{1,0:T(8,128)S(1)}, u32[]{:S(2)}, u32[]{:S(2)}) collective-permute-start(f32[72,128]{1,0:T(8,128)S(1)} %get-tuple-element.46), channel_id=1, source_target_pairs={{0,28},{4,0},{8,4},{12,8},{16,12},{20,16},{24,20},{28,24},{1,29},{... | collective-permute-start | bytes 110600 | tf_op jit(solution)/shard_map/ppermute | solution.py:538
  14.7 0.0 copy-done.2
  14.8 0.0 copy-done.5
  14.8 0.0 copy-done.9
  14.8 0.0 copy-done.8
  14.8 0.0 copy-done.10
  14.8 0.0 copy-done.11
  14.8 0.0 copy-done.12
  14.8 0.3 shard_map.142
  15.1 1.5 %shard_map.143.rest_0_ = f32[180,8,128]{2,1,0:T(8,128)S(1)} custom-call(s32[8,64]{1,0:T(8,128)S(1)} %get-tuple-element.64.code_ref, f32[256,128]{1,0:T(8,128)S(1)} %get-tuple-element.65.table_ref), custom_call_target="tpu_custom_call" | custom-call | flops 2000000 | bytes 200000 | tf_op jit(solution)/shard_map/pallas_call | solution.py:115
  16.6 0.0 collective-permute-done.2.low_ref
  16.6 0.4 collective-permute-done.3.high_ref
  17.0 0.3 shard_map.144
  17.3 0.0 copy-start
  17.3 0.0 copy-start.1
  17.3 0.0 copy-start.4
  17.3 3.3 %collective-permute-start.4 = (f32[48,128]{1,0:T(8,128)S(1)}, f32[48,128]{1,0:T(8,128)S(1)}, u32[]{:S(2)}, u32[]{:S(2)}) collective-permute-start(f32[48,128]{1,0:T(8,128)S(1)} %get-tuple-element.62), channel_id=1, source_target_pairs={{0,1},{2,3},{1,0},{3,2},{4,5},{6,7},{5,4},{7,6},{8,9},{10,11},{9,8... | collective-permute-start | bytes 73736 | tf_op jit(solution)/shard_map/ppermute | solution.py:543
  20.6 0.7 %collective-permute-start.5 = (f32[48,128]{1,0:T(8,128)S(1)}, f32[48,128]{1,0:T(8,128)S(1)}, u32[]{:S(2)}, u32[]{:S(2)}) collective-permute-start(f32[48,128]{1,0:T(8,128)S(1)} %get-tuple-element.63), channel_id=1, source_target_pairs={{1,2},{2,1},{5,6},{6,5},{9,10},{10,9},{13,14},{14,13},{17,18},{18,... | collective-permute-start | bytes 73736 | tf_op jit(solution)/shard_map/ppermute | solution.py:543
  21.2 0.0 copy-start.6
  21.3 1.5 %shard_map.145.omega_ref = f32[180,8,128]{2,1,0:T(8,128)S(1)} custom-call(s32[8,64]{1,0:T(8,128)S(1)} %get-tuple-element.64.code_ref, f32[256,128]{1,0:T(8,128)S(1)} %get-tuple-element.65.table_ref, f32[180,8,128]{2,1,0:T(8,128)S(1)} %shard_map.143.rest_0_), custom_call_target="tpu_custom_call", output_to_operand_aliasing={{}: (2, {})} | custom-call | flops 2000000 | bytes 200000 | tf_op jit(solution)/shard_map/pallas_call | solution.py:115
  22.7 0.0 collective-permute-done.4.low_ref
  22.7 0.0 collective-permute-done.5.high_ref
  22.7 0.0 copy-done
  22.7 0.0 copy-done.1
  22.7 0.0 copy-done.4
  22.7 0.0 copy-done.6
  22.8 0.8 %shard_map.146 = (f32[8,16,128]{2,1,0:T(8,128)S(1)}, f32[8,16,128]{2,1,0:T(8,128)S(1)}, f32[8,16,128]{2,1,0:T(8,128)S(1)}, f32[16,128]{1,0:T(8,128)S(1)}, f32[16...) custom-call(f32[8,32,128]{2,1,0:T(8,128)S(1)} %get-tuple-element.53.v_ref, f32[16,128]{1,0:T(8,128)S(1)} %get-tuple-element.54.g_ref, ...), custom_call_target="tpu_custom_call" | custom-call | flops 2000000 | bytes 200000 | tf_op jit(solution)/shard_map/pallas_call | solution.py:115
  23.5 0.7 %collective-permute-start.6 = (f32[16,128]{1,0:T(8,128)S(1)}, f32[16,128]{1,0:T(8,128)S(1)}, u32[]{:S(2)}, u32[]{:S(2)}) collective-permute-start(f32[16,128]{1,0:T(8,128)S(1)} %get-tuple-element.72), channel_id=1, source_target_pairs={{32,64},{96,128},{160,192},{224,256},{288,320},{352,384},{416,448}... | collective-permute-start | bytes 24584 | tf_op jit(solution)/shard_map/ppermute | solution.py:543
  24.2 7.6 %collective-permute-start.7 = (f32[16,128]{1,0:T(8,128)S(1)}, f32[16,128]{1,0:T(8,128)S(1)}, u32[]{:S(2)}, u32[]{:S(2)}) collective-permute-start(f32[16,128]{1,0:T(8,128)S(1)} %get-tuple-element.73), channel_id=1, source_target_pairs={{0,32},{64,96},{128,160},{192,224},{256,288},{320,352},{384,416},{... | collective-permute-start | bytes 24584 | tf_op jit(solution)/shard_map/ppermute | solution.py:543
  31.8 0.4 shard_map.147.pre_ref
  32.3 0.0 collective-permute-done.6.low_ref
  32.3 0.6 collective-permute-done.7.high_ref
  32.9 0.4 shard_map.148
  33.3 13.5 %all_to_all.10 = f32[32,1,128]{2,1,0:T(1,128)S(1)} all-to-all(f32[32,1,128]{2,1,0:T(1,128)S(1)} %bitcast.23), channel_id=1, replica_groups={{22,23,24,25,26,27,28,29,30,31,0,1,2,3,4,5,6,7,8,9,10,11,12,13,14,15,16..., dimensions={0} | all-to-all | bytes 32768 | tf_op jit(solution)/shard_map/all_to_all | solution.py:556
  46.8 0.1 shard_map.149
  46.9 16.7 %all_to_all.11 = f32[16,1,128]{2,1,0:T(1,128)S(1)} all-to-all(f32[16,1,128]{2,1,0:T(1,128)S(1)} %bitcast.21), channel_id=1, replica_groups={{256,288,320,352,384,416,448,480,0,32,64,96,128,160,192,224},{257,289,3..., dimensions={0} | all-to-all | bytes 16384 | tf_op jit(solution)/shard_map/all_to_all | solution.py:556
  63.5 1.4 %shard_map.150 = (f32[8,16,128]{2,1,0:T(8,128)}, f32[3,32,128]{2,1,0:T(8,128)}) custom-call(f32[16,128]{1,0:T(8,128)S(1)} %bitcast.20, f32[8,16,128]{2,1,0:T(8,128)S(1)} %get-tuple-element.69.v0_ref, f32[8,16,128]{2,1,0:T(8,128)S(1)} %get-tuple-element.77.v1_ref, f32[3,32,128]{2,1,0:T(8,128)S(1)} %bitcast.18, f32[32,128]{1,0:T(8,128)S(1)} %get-tuple-element.78.store_ref, ...), custom_call_target="tpu_custom_call" | custom-call | flops 2000000 | bytes 200000 | tf_op jit(solution)/shard_map/pallas_call | solution.py:115
  (1 shorter events, 0.0 us)
Async XLA Ops:
  0.6 9.9 %copy-start.3 = (f32[8,16,128]{2,1,0:T(8,128)S(1)}, f32[8,16,128]{2,1,0:T(8,128)}, u32[]{:S(2)}) copy-start(f32[8,16,128]{2,1,0:T(8,128)} %f_ref.1) | copy-start | bytes 196612
  1.4 8.1 %copy-start.7 = (f32[4,1,2,16]{3,2,1,0:T(2,128)S(1)}, f32[4,1,2,16]{3,2,1,0:T(2,128)}, u32[]{:S(2)}) copy-start(f32[4,1,2,16]{3,2,1,0:T(2,128)} %param.14) | copy-start | bytes 1540
  1.4 8.2 %collective-permute-start.1 = (f32[16,128]{1,0:T(8,128)S(1)}, f32[16,128]{1,0:T(8,128)S(1)}, u32[]{:S(2)}, u32[]{:S(2)}) collective-permute-start(f32[16,128]{1,0:T(8,128)S(1)} %get-tuple-element.88), channel_id=1, source_target_pairs={{32,64},{96,128},{160,192},{224,256},{288,320},{352,384},{416,448}... | collective-permute-start | bytes 24584 | tf_op jit(solution)/shard_map/ppermute | solution.py:543
  2.2 8.3 %collective-permute-start = (f32[16,128]{1,0:T(8,128)S(1)}, f32[16,128]{1,0:T(8,128)S(1)}, u32[]{:S(2)}, u32[]{:S(2)}) collective-permute-start(f32[16,128]{1,0:T(8,128)S(1)} %get-tuple-element.89), channel_id=1, source_target_pairs={{0,32},{64,96},{128,160},{192,224},{256,288},{320,352},{384,416},{... | collective-permute-start | bytes 24584 | tf_op jit(solution)/shard_map/ppermute | solution.py:543
  9.6 5.2 %copy-start.2 = (f32[1,3,4096]{2,0,1:T(1,128)S(1)}, f32[1,3,4096]{2,0,1:T(1,128)}, u32[]{:S(2)}) copy-start(f32[1,3,4096]{2,0,1:T(1,128)} %param.19) | copy-start | bytes 147460
  10.5 4.3 %copy-start.5 = (f32[1,4096]{1,0:T(1,128)S(1)}, f32[1,4096]{1,0:T(1,128)}, u32[]{:S(2)}) copy-start(f32[1,4096]{1,0:T(1,128)} %param.18) | copy-start | bytes 49156
  10.5 4.2 %copy-start.9 = (f32[4,4]{1,0:T(4,128)S(1)}, f32[4,4]{1,0:T(4,128)}, u32[]{:S(2)}) copy-start(f32[4,4]{1,0:T(4,128)} %inverse_ref.1) | copy-start | bytes 196
  10.5 4.2 %copy-start.8 = (f32[6,4]{0,1:T(4,128)S(1)}, f32[6,4]{0,1:T(4,128)}, u32[]{:S(2)}) copy-start(f32[6,4]{0,1:T(4,128)} %param.20) | copy-start | bytes 292
  10.5 4.2 %copy-start.10 = (s32[1,64]{1,0:T(1,128)S(1)}, s32[1,64]{1,0:T(1,128)}, u32[]{:S(2)}) copy-start(s32[1,64]{1,0:T(1,128)} %elem_ref.1) | copy-start | bytes 772
  10.6 4.2 %copy-start.11 = (s32[1,64]{1,0:T(1,128)S(1)}, s32[1,64]{1,0:T(1,128)}, u32[]{:S(2)}) copy-start(s32[1,64]{1,0:T(1,128)} %face_ref.1) | copy-start | bytes 772
  10.6 4.2 %copy-start.12 = (s32[1,64]{1,0:T(1,128)S(1)}, s32[1,64]{1,0:T(1,128)}, u32[]{:S(2)}) copy-start(s32[1,64]{1,0:T(1,128)} %stores_ref.1) | copy-start | bytes 772
  10.6 6.0 %collective-permute-start.2 = (f32[72,128]{1,0:T(8,128)S(1)}, f32[72,128]{1,0:T(8,128)S(1)}, u32[]{:S(2)}, u32[]{:S(2)}) collective-permute-start(f32[72,128]{1,0:T(8,128)S(1)} %get-tuple-element.45), channel_id=1, source_target_pairs={{0,4},{4,8},{8,12},{12,16},{16,20},{20,24},{24,28},{28,0},{1,5},{5... | collective-permute-start | bytes 110600 | tf_op jit(solution)/shard_map/ppermute | solution.py:538
  13.6 3.4 %collective-permute-start.3 = (f32[72,128]{1,0:T(8,128)S(1)}, f32[72,128]{1,0:T(8,128)S(1)}, u32[]{:S(2)}, u32[]{:S(2)}) collective-permute-start(f32[72,128]{1,0:T(8,128)S(1)} %get-tuple-element.46), channel_id=1, source_target_pairs={{0,28},{4,0},{8,4},{12,8},{16,12},{20,16},{24,20},{28,24},{1,29},{... | collective-permute-start | bytes 110600 | tf_op jit(solution)/shard_map/ppermute | solution.py:538
  17.3 5.4 %copy-start = (f32[256,256]{1,0:T(8,128)S(1)}, f32[256,256]{1,0:T(8,128)}, u32[]{:S(2)}) copy-start(f32[256,256]{1,0:T(8,128)} %constant.40.clone.kr_ref) | copy-start | bytes 786436
  17.3 5.4 %copy-start.1 = (f32[128,128]{1,0:T(8,128)S(1)}, f32[128,128]{1,0:T(8,128)}, u32[]{:S(2)}) copy-start(f32[128,128]{1,0:T(8,128)} %constant.38.clone.kk_ref) | copy-start | bytes 196612
  17.3 5.4 %copy-start.4 = (f32[128,128]{1,0:T(8,128)S(1)}, f32[128,128]{1,0:T(8,128)}, u32[]{:S(2)}) copy-start(f32[128,128]{1,0:T(8,128)} %constant.39.clone.ki_ref) | copy-start | bytes 196612
  17.3 5.4 %collective-permute-start.4 = (f32[48,128]{1,0:T(8,128)S(1)}, f32[48,128]{1,0:T(8,128)S(1)}, u32[]{:S(2)}, u32[]{:S(2)}) collective-permute-start(f32[48,128]{1,0:T(8,128)S(1)} %get-tuple-element.62), channel_id=1, source_target_pairs={{0,1},{2,3},{1,0},{3,2},{4,5},{6,7},{5,4},{7,6},{8,9},{10,11},{9,8... | collective-permute-start | bytes 73736 | tf_op jit(solution)/shard_map/ppermute | solution.py:543
  20.6 2.1 %collective-permute-start.5 = (f32[48,128]{1,0:T(8,128)S(1)}, f32[48,128]{1,0:T(8,128)S(1)}, u32[]{:S(2)}, u32[]{:S(2)}) collective-permute-start(f32[48,128]{1,0:T(8,128)S(1)} %get-tuple-element.63), channel_id=1, source_target_pairs={{1,2},{2,1},{5,6},{6,5},{9,10},{10,9},{13,14},{14,13},{17,18},{18,... | collective-permute-start | bytes 73736 | tf_op jit(solution)/shard_map/ppermute | solution.py:543
  21.2 1.5 %copy-start.6 = (f32[24,128]{1,0:T(8,128)S(1)}, f32[24,128]{1,0:T(8,128)}, u32[]{:S(2)}) copy-start(f32[24,128]{1,0:T(8,128)} %constant.41.clone.w_ref) | copy-start | bytes 36868
  23.5 8.7 %collective-permute-start.6 = (f32[16,128]{1,0:T(8,128)S(1)}, f32[16,128]{1,0:T(8,128)S(1)}, u32[]{:S(2)}, u32[]{:S(2)}) collective-permute-start(f32[16,128]{1,0:T(8,128)S(1)} %get-tuple-element.72), channel_id=1, source_target_pairs={{32,64},{96,128},{160,192},{224,256},{288,320},{352,384},{416,448}... | collective-permute-start | bytes 24584 | tf_op jit(solution)/shard_map/ppermute | solution.py:543
  24.2 8.7 %collective-permute-start.7 = (f32[16,128]{1,0:T(8,128)S(1)}, f32[16,128]{1,0:T(8,128)S(1)}, u32[]{:S(2)}, u32[]{:S(2)}) collective-permute-start(f32[16,128]{1,0:T(8,128)S(1)} %get-tuple-element.73), channel_id=1, source_target_pairs={{0,32},{64,96},{128,160},{192,224},{256,288},{320,352},{384,416},{... | collective-permute-start | bytes 24584 | tf_op jit(solution)/shard_map/ppermute | solution.py:543

commit v5 on v4

--- a/solution.py
+++ b/solution.py
@@ -419,6 +419,11 @@
     out_ref[...] = jnp.broadcast_to(merged(parts_ref[...]), out_ref.shape)
 
 
+def load_column(row, first):
+    place = lax.broadcasted_iota(jnp.int32, (24, 128), 0) + first
+    return jnp.sum(jnp.where(lane_ids(24) == place, row, 0.0), axis=1, keepdims=True)
+
+
 def finish(
     parts_ref, v0_ref, v1_ref, arm_ref, store_ref, motion_ref, p_out, velocity_out, p_ref, velocity_ref, sems
 ):
@@ -440,15 +445,15 @@
         p_ref[i] = wide0 * v0_ref[i] + wide1 * v1_ref[i]
     p_copy = pltpu.make_async_copy(p_ref, p_out, sems.at[0])
     p_copy.start()
-    loads = c0 * total + c1 * pltpu.roll(total, 104, 1)
-    state = motion_ref[0:1, :] + motion_ref[1:2, :] * loads
+    loads = c0 * load_column(total, 8) + c1 * load_column(total, 32)
+    state = motion_ref[0:24, :] + motion_ref[24:48, :] * loads
     stores = store_ref[...]
     maps = []
     for c in range(6):
         value = jnp.zeros((32, 128), F32)
         for store in range(4):
-            at = 8 + 4 * c + store
-            value = jnp.where(stores == store, state[:, at : at + 1], value)
+            at = 4 * c + store
+            value = jnp.where(stores == store, state[at : at + 1, :], value)
         maps.append(value)
     arms = [arm_ref[c] for c in range(3)]
     for c in range(3):
@@ -502,10 +507,12 @@
     component, store = load >> 2, load & 3
     row = row_ids()
     motion = dot(motion_ref[...], jnp.where(inside & (component == row), 1.0, 0.0)[0:6, :])
-    motion_out[0:1, :] = jnp.sum(jnp.where((store == row)[0:4, :], motion, 0.0), axis=0, keepdims=True)
+    motion = jnp.sum(jnp.where((store == row)[0:4, :], motion, 0.0), axis=0, keepdims=True)
+    motion_out[0:24, :] = jnp.broadcast_to(load_column(motion, 8), (24, 128))
     scale = dot(inverse_ref[...], jnp.where(inside & (store == row), 1.0, 0.0)[0:4, :])
     taken = jnp.maximum(component - 2, 0) == row
-    motion_out[1:2, :] = jnp.sum(jnp.where(taken[0:4, :], scale, 0.0), axis=0, keepdims=True)
+    scale = jnp.sum(jnp.where(taken[0:4, :], scale, 0.0), axis=0, keepdims=True)
+    motion_out[24:48, :] = jnp.broadcast_to(load_column(scale, 8), (24, 128))
 
 
 def wall_weights(begin, end, code_ref, table_ref, *rest):
@@ -544,7 +551,7 @@
 
 
 SWAPS = "ACD"
-SPLIT = 32
+SPLIT = 16
 
 
 STAGES = ((("vert", "span"), 32, 22), ("stream", 16, 8))
@@ -608,7 +615,7 @@
     up, down, weight, arms = tie((up, down, wall_weight.reshape(32, 128), wall_arm.reshape(3, 32, 128)))
     low, high = exchange(up, down, "B")
     table, codes, store_rows, motion = call(
-        wall_table, [(256, 128), ((8, 64), jnp.int32), (32, 128), (2, 128)]
+        wall_table, [(256, 128), ((8, 64), jnp.int32), (32, 128), (48, 128)]
     )(wall_elem, wall_face, wall_store, store_motion.T, store_inverse, weight, arms)
     omega = call(functools.partial(wall_weights, 0, SPLIT), [(180, 8, 128)])(codes, table, smem=1)[0]
     low, high, table, codes, omega = tie((low, high, table, codes, omega))

time: 65.9 us -> 65.6 us (level)
    all_to_all x2, blocking collectives: 30.1 us -> 29.5 us  [reduced(): lax.all_to_all(sums.reshape(count, 1, 128), axes, 0, 0, axis_index_groups...]
where the time goes in v5:
time: 65.6 us; the launch traced here: 64.6 us
  blocking collectives  29.5 us (45%)
  starting transfers between devices  24.4 us (37%)
  Pallas kernels  6.78 us (10%)
  waiting for transfers between devices  2.21 us (3%)
  between operations  0.88 us (1%)
  local copies, waits for them, and re-layouts  0.82 us (1%)
    all_to_all x2, blocking collectives, reduced(): lax.all_to_all(sums.reshape(count, 1, 128), axes, 0, 0, axis_index_groups...  29.5 us
    ppermute x6, starting transfers between devices, swapped(): return lax.ppermute(x, axis, pairs + [(b, a) for a, b in pairs])  20.3 us
    pallas_call x11, Pallas kernels, run(): pl.pallas_call(body, out_shape=[jax.ShapeDtypeStruct(*s) for s in shapes]...  6.78 us
    ppermute x2, starting transfers between devices, shifted(): return lax.ppermute(x, axis, pairs)  4.17 us
    ppermute x6, waiting for transfers between devices, swapped(): return lax.ppermute(x, axis, pairs + [(b, a) for a, b in pairs])  1.49 us
  transfers between devices with their start and end apart: 8, of which 3 were waited for; matrix products, arithmetic and copies ran while one was open for 0% of the time, Pallas kernels for 6%

profile of v5, /device:TPU:1, one launch (start us, length us, event | category | flops | bytes accessed | tf_op | source)
XLA Modules:
  0.0 64.6 jit_solution(17895941551429822169)
XLA Ops:
  0.6 0.0 copy-start.3
  0.7 0.7 %dynamic-slice_bitcast_fusion = (f32[16,128]{1,0:T(8,128)S(1)}, f32[16,128]{1,0:T(8,128)S(1)}) fusion(f32[8,16,128]{2,1,0:T(8,128)} %f_ref.1, s32[]{:T(128)S(6)} %select_n.16, s32[]{:T(128)S(6)} %select_n.15), kind=kLoop, calls=%fused_computation | loop fusion | bytes 32776 | tf_op jit(solution)/shard_map/jit(dynamic_index_in_dim)/squeeze | solution.py:608
  1.4 0.0 copy-start.7
  1.4 0.8 %collective-permute-start.1 = (f32[16,128]{1,0:T(8,128)S(1)}, f32[16,128]{1,0:T(8,128)S(1)}, u32[]{:S(2)}, u32[]{:S(2)}) collective-permute-start(f32[16,128]{1,0:T(8,128)S(1)} %get-tuple-element.88), channel_id=1, source_target_pairs={{32,64},{96,128},{160,192},{224,256},{288,320},{352,384},{416,448}... | collective-permute-start | bytes 24584 | tf_op jit(solution)/shard_map/ppermute | solution.py:550
  2.2 7.3 %collective-permute-start = (f32[16,128]{1,0:T(8,128)S(1)}, f32[16,128]{1,0:T(8,128)S(1)}, u32[]{:S(2)}, u32[]{:S(2)}) collective-permute-start(f32[16,128]{1,0:T(8,128)S(1)} %get-tuple-element.89), channel_id=1, source_target_pairs={{0,32},{64,96},{128,160},{192,224},{256,288},{320,352},{384,416},{... | collective-permute-start | bytes 24584 | tf_op jit(solution)/shard_map/ppermute | solution.py:550
  9.5 0.0 copy-done.7
  9.5 0.1 shard_map.140.geo_ref
  9.6 0.0 copy-start.2
  9.6 0.0 collective-permute-done.1.high_ref
  9.6 0.9 %collective-permute-done.low_ref = f32[16,128]{1,0:T(8,128)S(1)} collective-permute-done((f32[16,128]{1,0:T(8,128)S(1)}, f32[16,128]{1,0:T(8,128)S(1)}, u32[]{:S(2)}, u32[]{:S(2)}) %collective-permute-start) | collective-permute-done | bytes 8224 | tf_op jit(solution)/shard_map/ppermute | solution.py:550
  10.5 0.0 copy-done.3
  10.5 0.0 copy-start.5
  10.5 0.0 copy-start.9
  10.5 0.0 copy-start.8
  10.5 0.0 copy-start.10
  10.6 0.0 copy-start.11
  10.6 0.0 copy-start.12
  10.6 3.0 %collective-permute-start.2 = (f32[72,128]{1,0:T(8,128)S(1)}, f32[72,128]{1,0:T(8,128)S(1)}, u32[]{:S(2)}, u32[]{:S(2)}) collective-permute-start(f32[72,128]{1,0:T(8,128)S(1)} %get-tuple-element.45), channel_id=1, source_target_pairs={{0,4},{4,8},{8,12},{12,16},{16,20},{20,24},{24,28},{28,0},{1,5},{5... | collective-permute-start | bytes 110600 | tf_op jit(solution)/shard_map/ppermute | solution.py:545
  13.6 1.1 %collective-permute-start.3 = (f32[72,128]{1,0:T(8,128)S(1)}, f32[72,128]{1,0:T(8,128)S(1)}, u32[]{:S(2)}, u32[]{:S(2)}) collective-permute-start(f32[72,128]{1,0:T(8,128)S(1)} %get-tuple-element.46), channel_id=1, source_target_pairs={{0,28},{4,0},{8,4},{12,8},{16,12},{20,16},{24,20},{28,24},{1,29},{... | collective-permute-start | bytes 110600 | tf_op jit(solution)/shard_map/ppermute | solution.py:545
  14.7 0.0 copy-done.2
  14.8 0.0 copy-done.5
  14.8 0.0 copy-done.9
  14.8 0.0 copy-done.8
  14.8 0.0 copy-done.10
  14.8 0.0 copy-done.11
  14.8 0.0 copy-done.12
  14.8 0.4 shard_map.142
  15.2 1.1 %shard_map.143.rest_0_ = f32[180,8,128]{2,1,0:T(8,128)S(1)} custom-call(s32[8,64]{1,0:T(8,128)S(1)} %get-tuple-element.64.code_ref, f32[256,128]{1,0:T(8,128)S(1)} %get-tuple-element.65.table_ref), custom_call_target="tpu_custom_call" | custom-call | flops 2000000 | bytes 200000 | tf_op jit(solution)/shard_map/pallas_call | solution.py:115
  16.3 0.0 collective-permute-done.2.low_ref
  16.3 0.7 %collective-permute-done.3.high_ref = f32[72,128]{1,0:T(8,128)S(1)} collective-permute-done((f32[72,128]{1,0:T(8,128)S(1)}, f32[72,128]{1,0:T(8,128)S(1)}, u32[]{:S(2)}, u32[]{:S(2)}) %collective-permute-start.3) | collective-permute-done | bytes 36896 | tf_op jit(solution)/shard_map/ppermute | solution.py:545
  17.0 0.3 shard_map.144
  17.3 0.0 copy-start
  17.3 0.0 copy-start.1
  17.3 0.0 copy-start.4
  17.3 3.3 %collective-permute-start.4 = (f32[48,128]{1,0:T(8,128)S(1)}, f32[48,128]{1,0:T(8,128)S(1)}, u32[]{:S(2)}, u32[]{:S(2)}) collective-permute-start(f32[48,128]{1,0:T(8,128)S(1)} %get-tuple-element.62), channel_id=1, source_target_pairs={{0,1},{2,3},{1,0},{3,2},{4,5},{6,7},{5,4},{7,6},{8,9},{10,11},{9,8... | collective-permute-start | bytes 73736 | tf_op jit(solution)/shard_map/ppermute | solution.py:550
  20.6 0.7 %collective-permute-start.5 = (f32[48,128]{1,0:T(8,128)S(1)}, f32[48,128]{1,0:T(8,128)S(1)}, u32[]{:S(2)}, u32[]{:S(2)}) collective-permute-start(f32[48,128]{1,0:T(8,128)S(1)} %get-tuple-element.63), channel_id=1, source_target_pairs={{1,2},{2,1},{5,6},{6,5},{9,10},{10,9},{13,14},{14,13},{17,18},{18,... | collective-permute-start | bytes 73736 | tf_op jit(solution)/shard_map/ppermute | solution.py:550
  21.2 0.0 copy-start.6
  21.3 1.9 %shard_map.145.omega_ref = f32[180,8,128]{2,1,0:T(8,128)S(1)} custom-call(s32[8,64]{1,0:T(8,128)S(1)} %get-tuple-element.64.code_ref, f32[256,128]{1,0:T(8,128)S(1)} %get-tuple-element.65.table_ref, f32[180,8,128]{2,1,0:T(8,128)S(1)} %shard_map.143.rest_0_), custom_call_target="tpu_custom_call", output_to_operand_aliasing={{}: (2, {})} | custom-call | flops 2000000 | bytes 200000 | tf_op jit(solution)/shard_map/pallas_call | solution.py:115
  23.1 0.0 collective-permute-done.4.low_ref
  23.1 0.0 collective-permute-done.5.high_ref
  23.1 0.0 copy-done
  23.2 0.0 copy-done.1
  23.2 0.0 copy-done.4
  23.2 0.0 copy-done.6
  23.2 0.8 %shard_map.146 = (f32[8,16,128]{2,1,0:T(8,128)S(1)}, f32[8,16,128]{2,1,0:T(8,128)S(1)}, f32[8,16,128]{2,1,0:T(8,128)S(1)}, f32[16,128]{1,0:T(8,128)S(1)}, f32[16...) custom-call(f32[8,32,128]{2,1,0:T(8,128)S(1)} %get-tuple-element.53.v_ref, f32[16,128]{1,0:T(8,128)S(1)} %get-tuple-element.54.g_ref, ...), custom_call_target="tpu_custom_call" | custom-call | flops 2000000 | bytes 200000 | tf_op jit(solution)/shard_map/pallas_call | solution.py:115
  23.9 0.7 %collective-permute-start.6 = (f32[16,128]{1,0:T(8,128)S(1)}, f32[16,128]{1,0:T(8,128)S(1)}, u32[]{:S(2)}, u32[]{:S(2)}) collective-permute-start(f32[16,128]{1,0:T(8,128)S(1)} %get-tuple-element.72), channel_id=1, source_target_pairs={{32,64},{96,128},{160,192},{224,256},{288,320},{352,384},{416,448}... | collective-permute-start | bytes 24584 | tf_op jit(solution)/shard_map/ppermute | solution.py:550
  24.6 7.6 %collective-permute-start.7 = (f32[16,128]{1,0:T(8,128)S(1)}, f32[16,128]{1,0:T(8,128)S(1)}, u32[]{:S(2)}, u32[]{:S(2)}) collective-permute-start(f32[16,128]{1,0:T(8,128)S(1)} %get-tuple-element.73), channel_id=1, source_target_pairs={{0,32},{64,96},{128,160},{192,224},{256,288},{320,352},{384,416},{... | collective-permute-start | bytes 24584 | tf_op jit(solution)/shard_map/ppermute | solution.py:550
  32.3 0.4 shard_map.147.pre_ref
  32.7 0.0 collective-permute-done.6.low_ref
  32.7 0.6 collective-permute-done.7.high_ref
  33.3 0.4 shard_map.148
  33.7 12.8 %all_to_all.10 = f32[32,1,128]{2,1,0:T(1,128)S(1)} all-to-all(f32[32,1,128]{2,1,0:T(1,128)S(1)} %bitcast.23), channel_id=1, replica_groups={{22,23,24,25,26,27,28,29,30,31,0,1,2,3,4,5,6,7,8,9,10,11,12,13,14,15,16..., dimensions={0} | all-to-all | bytes 32768 | tf_op jit(solution)/shard_map/all_to_all | solution.py:563
  46.5 0.1 shard_map.149
  46.6 16.7 %all_to_all.11 = f32[16,1,128]{2,1,0:T(1,128)S(1)} all-to-all(f32[16,1,128]{2,1,0:T(1,128)S(1)} %bitcast.21), channel_id=1, replica_groups={{256,288,320,352,384,416,448,480,0,32,64,96,128,160,192,224},{257,289,3..., dimensions={0} | all-to-all | bytes 16384 | tf_op jit(solution)/shard_map/all_to_all | solution.py:563
  63.3 1.3 %shard_map.150 = (f32[8,16,128]{2,1,0:T(8,128)}, f32[3,32,128]{2,1,0:T(8,128)}) custom-call(f32[16,128]{1,0:T(8,128)S(1)} %bitcast.20, f32[8,16,128]{2,1,0:T(8,128)S(1)} %get-tuple-element.69.v0_ref, f32[8,16,128]{2,1,0:T(8,128)S(1)} %get-tuple-element.77.v1_ref, f32[3,32,128]{2,1,0:T(8,128)S(1)} %bitcast.18, f32[32,128]{1,0:T(8,128)S(1)} %get-tuple-element.78.store_ref, ...), custom_call_target="tpu_custom_call" | custom-call | flops 2000000 | bytes 200000 | tf_op jit(solution)/shard_map/pallas_call | solution.py:115
  (1 shorter events, 0.0 us)
Async XLA Ops:
  0.6 9.9 %copy-start.3 = (f32[8,16,128]{2,1,0:T(8,128)S(1)}, f32[8,16,128]{2,1,0:T(8,128)}, u32[]{:S(2)}) copy-start(f32[8,16,128]{2,1,0:T(8,128)} %f_ref.1) | copy-start | bytes 196612
  1.4 8.1 %copy-start.7 = (f32[4,1,2,16]{3,2,1,0:T(2,128)S(1)}, f32[4,1,2,16]{3,2,1,0:T(2,128)}, u32[]{:S(2)}) copy-start(f32[4,1,2,16]{3,2,1,0:T(2,128)} %param.14) | copy-start | bytes 1540
  1.4 8.2 %collective-permute-start.1 = (f32[16,128]{1,0:T(8,128)S(1)}, f32[16,128]{1,0:T(8,128)S(1)}, u32[]{:S(2)}, u32[]{:S(2)}) collective-permute-start(f32[16,128]{1,0:T(8,128)S(1)} %get-tuple-element.88), channel_id=1, source_target_pairs={{32,64},{96,128},{160,192},{224,256},{288,320},{352,384},{416,448}... | collective-permute-start | bytes 24584 | tf_op jit(solution)/shard_map/ppermute | solution.py:550
  2.2 8.3 %collective-permute-start = (f32[16,128]{1,0:T(8,128)S(1)}, f32[16,128]{1,0:T(8,128)S(1)}, u32[]{:S(2)}, u32[]{:S(2)}) collective-permute-start(f32[16,128]{1,0:T(8,128)S(1)} %get-tuple-element.89), channel_id=1, source_target_pairs={{0,32},{64,96},{128,160},{192,224},{256,288},{320,352},{384,416},{... | collective-permute-start | bytes 24584 | tf_op jit(solution)/shard_map/ppermute | solution.py:550
  9.6 5.2 %copy-start.2 = (f32[1,3,4096]{2,0,1:T(1,128)S(1)}, f32[1,3,4096]{2,0,1:T(1,128)}, u32[]{:S(2)}) copy-start(f32[1,3,4096]{2,0,1:T(1,128)} %param.19) | copy-start | bytes 147460
  10.5 4.3 %copy-start.5 = (f32[1,4096]{1,0:T(1,128)S(1)}, f32[1,4096]{1,0:T(1,128)}, u32[]{:S(2)}) copy-start(f32[1,4096]{1,0:T(1,128)} %param.18) | copy-start | bytes 49156
  10.5 4.2 %copy-start.9 = (f32[4,4]{1,0:T(4,128)S(1)}, f32[4,4]{1,0:T(4,128)}, u32[]{:S(2)}) copy-start(f32[4,4]{1,0:T(4,128)} %inverse_ref.1) | copy-start | bytes 196
  10.5 4.2 %copy-start.8 = (f32[6,4]{0,1:T(4,128)S(1)}, f32[6,4]{0,1:T(4,128)}, u32[]{:S(2)}) copy-start(f32[6,4]{0,1:T(4,128)} %param.20) | copy-start | bytes 292
  10.5 4.2 %copy-start.10 = (s32[1,64]{1,0:T(1,128)S(1)}, s32[1,64]{1,0:T(1,128)}, u32[]{:S(2)}) copy-start(s32[1,64]{1,0:T(1,128)} %elem_ref.1) | copy-start | bytes 772
  10.6 4.2 %copy-start.11 = (s32[1,64]{1,0:T(1,128)S(1)}, s32[1,64]{1,0:T(1,128)}, u32[]{:S(2)}) copy-start(s32[1,64]{1,0:T(1,128)} %face_ref.1) | copy-start | bytes 772
  10.6 4.2 %copy-start.12 = (s32[1,64]{1,0:T(1,128)S(1)}, s32[1,64]{1,0:T(1,128)}, u32[]{:S(2)}) copy-start(s32[1,64]{1,0:T(1,128)} %stores_ref.1) | copy-start | bytes 772
  10.6 5.7 %collective-permute-start.2 = (f32[72,128]{1,0:T(8,128)S(1)}, f32[72,128]{1,0:T(8,128)S(1)}, u32[]{:S(2)}, u32[]{:S(2)}) collective-permute-start(f32[72,128]{1,0:T(8,128)S(1)} %get-tuple-element.45), channel_id=1, source_target_pairs={{0,4},{4,8},{8,12},{12,16},{16,20},{20,24},{24,28},{28,0},{1,5},{5... | collective-permute-start | bytes 110600 | tf_op jit(solution)/shard_map/ppermute | solution.py:545
  13.6 3.4 %collective-permute-start.3 = (f32[72,128]{1,0:T(8,128)S(1)}, f32[72,128]{1,0:T(8,128)S(1)}, u32[]{:S(2)}, u32[]{:S(2)}) collective-permute-start(f32[72,128]{1,0:T(8,128)S(1)} %get-tuple-element.46), channel_id=1, source_target_pairs={{0,28},{4,0},{8,4},{12,8},{16,12},{20,16},{24,20},{28,24},{1,29},{... | collective-permute-start | bytes 110600 | tf_op jit(solution)/shard_map/ppermute | solution.py:545
  17.3 5.9 %copy-start = (f32[256,256]{1,0:T(8,128)S(1)}, f32[256,256]{1,0:T(8,128)}, u32[]{:S(2)}) copy-start(f32[256,256]{1,0:T(8,128)} %constant.40.clone.kr_ref) | copy-start | bytes 786436
  17.3 5.9 %copy-start.1 = (f32[128,128]{1,0:T(8,128)S(1)}, f32[128,128]{1,0:T(8,128)}, u32[]{:S(2)}) copy-start(f32[128,128]{1,0:T(8,128)} %constant.38.clone.kk_ref) | copy-start | bytes 196612
  17.3 5.9 %copy-start.4 = (f32[128,128]{1,0:T(8,128)S(1)}, f32[128,128]{1,0:T(8,128)}, u32[]{:S(2)}) copy-start(f32[128,128]{1,0:T(8,128)} %constant.39.clone.ki_ref) | copy-start | bytes 196612
  17.3 5.8 %collective-permute-start.4 = (f32[48,128]{1,0:T(8,128)S(1)}, f32[48,128]{1,0:T(8,128)S(1)}, u32[]{:S(2)}, u32[]{:S(2)}) collective-permute-start(f32[48,128]{1,0:T(8,128)S(1)} %get-tuple-element.62), channel_id=1, source_target_pairs={{0,1},{2,3},{1,0},{3,2},{4,5},{6,7},{5,4},{7,6},{8,9},{10,11},{9,8... | collective-permute-start | bytes 73736 | tf_op jit(solution)/shard_map/ppermute | solution.py:550
  20.6 2.6 %collective-permute-start.5 = (f32[48,128]{1,0:T(8,128)S(1)}, f32[48,128]{1,0:T(8,128)S(1)}, u32[]{:S(2)}, u32[]{:S(2)}) collective-permute-start(f32[48,128]{1,0:T(8,128)S(1)} %get-tuple-element.63), channel_id=1, source_target_pairs={{1,2},{2,1},{5,6},{6,5},{9,10},{10,9},{13,14},{14,13},{17,18},{18,... | collective-permute-start | bytes 73736 | tf_op jit(solution)/shard_map/ppermute | solution.py:550
  21.2 1.9 %copy-start.6 = (f32[24,128]{1,0:T(8,128)S(1)}, f32[24,128]{1,0:T(8,128)}, u32[]{:S(2)}) copy-start(f32[24,128]{1,0:T(8,128)} %constant.41.clone.w_ref) | copy-start | bytes 36868
  23.9 8.7 %collective-permute-start.6 = (f32[16,128]{1,0:T(8,128)S(1)}, f32[16,128]{1,0:T(8,128)S(1)}, u32[]{:S(2)}, u32[]{:S(2)}) collective-permute-start(f32[16,128]{1,0:T(8,128)S(1)} %get-tuple-element.72), channel_id=1, source_target_pairs={{32,64},{96,128},{160,192},{224,256},{288,320},{352,384},{416,448}... | collective-permute-start | bytes 24584 | tf_op jit(solution)/shard_map/ppermute | solution.py:550
  24.6 8.7 %collective-permute-start.7 = (f32[16,128]{1,0:T(8,128)S(1)}, f32[16,128]{1,0:T(8,128)S(1)}, u32[]{:S(2)}, u32[]{:S(2)}) collective-permute-start(f32[16,128]{1,0:T(8,128)S(1)} %get-tuple-element.73), channel_id=1, source_target_pairs={{0,32},{64,96},{128,160},{192,224},{256,288},{320,352},{384,416},{... | collective-permute-start | bytes 24584 | tf_op jit(solution)/shard_map/ppermute | solution.py:550

commit v6 on v5

--- a/solution.py
+++ b/solution.py
@@ -551,7 +551,7 @@
 
 
 SWAPS = "ACD"
-SPLIT = 16
+SPLIT = 8
 
 
 STAGES = ((("vert", "span"), 32, 22), ("stream", 16, 8))

time: 65.6 us -> 65.6 us (level)
  no operation moved by 1% of the time
where the time goes in v6:
time: 65.6 us; the launch traced here: 64.6 us
  blocking collectives  29.3 us (45%)
  starting transfers between devices  24.4 us (37%)
  Pallas kernels  6.72 us (10%)
  waiting for transfers between devices  2.47 us (4%)
  between operations  0.88 us (1%)
  local copies, waits for them, and re-layouts  0.82 us (1%)
    all_to_all x2, blocking collectives, reduced(): lax.all_to_all(sums.reshape(count, 1, 128), axes, 0, 0, axis_index_groups...  29.3 us
    ppermute x6, starting transfers between devices, swapped(): return lax.ppermute(x, axis, pairs + [(b, a) for a, b in pairs])  20.3 us
    pallas_call x11, Pallas kernels, run(): pl.pallas_call(body, out_shape=[jax.ShapeDtypeStruct(*s) for s in shapes]...  6.72 us
    ppermute x2, starting transfers between devices, shifted(): return lax.ppermute(x, axis, pairs)  4.17 us
    ppermute x6, waiting for transfers between devices, swapped(): return lax.ppermute(x, axis, pairs + [(b, a) for a, b in pairs])  1.49 us
  transfers between devices with their start and end apart: 8, of which 3 were waited for; matrix products, arithmetic and copies ran while one was open for 0% of the time, Pallas kernels for 6%

profile of v6, /device:TPU:1, one launch (start us, length us, event | category | flops | bytes accessed | tf_op | source)
XLA Modules:
  0.0 64.6 jit_solution(1716560928290762517)
XLA Ops:
  0.6 0.0 copy-start.3
  0.7 0.7 %dynamic-slice_bitcast_fusion = (f32[16,128]{1,0:T(8,128)S(1)}, f32[16,128]{1,0:T(8,128)S(1)}) fusion(f32[8,16,128]{2,1,0:T(8,128)} %f_ref.1, s32[]{:T(128)S(6)} %select_n.16, s32[]{:T(128)S(6)} %select_n.15), kind=kLoop, calls=%fused_computation | loop fusion | bytes 32776 | tf_op jit(solution)/shard_map/jit(dynamic_index_in_dim)/squeeze | solution.py:608
  1.4 0.0 copy-start.7
  1.4 0.8 %collective-permute-start.1 = (f32[16,128]{1,0:T(8,128)S(1)}, f32[16,128]{1,0:T(8,128)S(1)}, u32[]{:S(2)}, u32[]{:S(2)}) collective-permute-start(f32[16,128]{1,0:T(8,128)S(1)} %get-tuple-element.88), channel_id=1, source_target_pairs={{32,64},{96,128},{160,192},{224,256},{288,320},{352,384},{416,448}... | collective-permute-start | bytes 24584 | tf_op jit(solution)/shard_map/ppermute | solution.py:550
  2.2 7.3 %collective-permute-start = (f32[16,128]{1,0:T(8,128)S(1)}, f32[16,128]{1,0:T(8,128)S(1)}, u32[]{:S(2)}, u32[]{:S(2)}) collective-permute-start(f32[16,128]{1,0:T(8,128)S(1)} %get-tuple-element.89), channel_id=1, source_target_pairs={{0,32},{64,96},{128,160},{192,224},{256,288},{320,352},{384,416},{... | collective-permute-start | bytes 24584 | tf_op jit(solution)/shard_map/ppermute | solution.py:550
  9.5 0.0 copy-done.7
  9.5 0.1 shard_map.140.geo_ref
  9.6 0.0 copy-start.2
  9.6 0.0 collective-permute-done.1.high_ref
  9.6 0.9 %collective-permute-done.low_ref = f32[16,128]{1,0:T(8,128)S(1)} collective-permute-done((f32[16,128]{1,0:T(8,128)S(1)}, f32[16,128]{1,0:T(8,128)S(1)}, u32[]{:S(2)}, u32[]{:S(2)}) %collective-permute-start) | collective-permute-done | bytes 8224 | tf_op jit(solution)/shard_map/ppermute | solution.py:550
  10.5 0.0 copy-done.3
  10.5 0.0 copy-start.5
  10.5 0.0 copy-start.9
  10.5 0.0 copy-start.8
  10.5 0.0 copy-start.10
  10.6 0.0 copy-start.11
  10.6 0.0 copy-start.12
  10.6 3.0 %collective-permute-start.2 = (f32[72,128]{1,0:T(8,128)S(1)}, f32[72,128]{1,0:T(8,128)S(1)}, u32[]{:S(2)}, u32[]{:S(2)}) collective-permute-start(f32[72,128]{1,0:T(8,128)S(1)} %get-tuple-element.45), channel_id=1, source_target_pairs={{0,4},{4,8},{8,12},{12,16},{16,20},{20,24},{24,28},{28,0},{1,5},{5... | collective-permute-start | bytes 110600 | tf_op jit(solution)/shard_map/ppermute | solution.py:545
  13.6 1.1 %collective-permute-start.3 = (f32[72,128]{1,0:T(8,128)S(1)}, f32[72,128]{1,0:T(8,128)S(1)}, u32[]{:S(2)}, u32[]{:S(2)}) collective-permute-start(f32[72,128]{1,0:T(8,128)S(1)} %get-tuple-element.46), channel_id=1, source_target_pairs={{0,28},{4,0},{8,4},{12,8},{16,12},{20,16},{24,20},{28,24},{1,29},{... | collective-permute-start | bytes 110600 | tf_op jit(solution)/shard_map/ppermute | solution.py:545
  14.7 0.0 copy-done.2
  14.8 0.0 copy-done.5
  14.8 0.0 copy-done.9
  14.8 0.0 copy-done.8
  14.8 0.0 copy-done.10
  14.8 0.0 copy-done.11
  14.8 0.0 copy-done.12
  14.8 0.4 shard_map.142
  15.2 0.8 %shard_map.143.rest_0_ = f32[180,8,128]{2,1,0:T(8,128)S(1)} custom-call(s32[8,64]{1,0:T(8,128)S(1)} %get-tuple-element.64.code_ref, f32[256,128]{1,0:T(8,128)S(1)} %get-tuple-element.65.table_ref), custom_call_target="tpu_custom_call" | custom-call | flops 2000000 | bytes 200000 | tf_op jit(solution)/shard_map/pallas_call | solution.py:115
  16.0 0.0 collective-permute-done.2.low_ref
  16.0 1.0 %collective-permute-done.3.high_ref = f32[72,128]{1,0:T(8,128)S(1)} collective-permute-done((f32[72,128]{1,0:T(8,128)S(1)}, f32[72,128]{1,0:T(8,128)S(1)}, u32[]{:S(2)}, u32[]{:S(2)}) %collective-permute-start.3) | collective-permute-done | bytes 36896 | tf_op jit(solution)/shard_map/ppermute | solution.py:545
  17.0 0.3 shard_map.144
  17.3 0.0 copy-start
  17.3 0.0 copy-start.1
  17.3 0.0 copy-start.4
  17.3 3.3 %collective-permute-start.4 = (f32[48,128]{1,0:T(8,128)S(1)}, f32[48,128]{1,0:T(8,128)S(1)}, u32[]{:S(2)}, u32[]{:S(2)}) collective-permute-start(f32[48,128]{1,0:T(8,128)S(1)} %get-tuple-element.62), channel_id=1, source_target_pairs={{0,1},{2,3},{1,0},{3,2},{4,5},{6,7},{5,4},{7,6},{8,9},{10,11},{9,8... | collective-permute-start | bytes 73736 | tf_op jit(solution)/shard_map/ppermute | solution.py:550
  20.6 0.7 %collective-permute-start.5 = (f32[48,128]{1,0:T(8,128)S(1)}, f32[48,128]{1,0:T(8,128)S(1)}, u32[]{:S(2)}, u32[]{:S(2)}) collective-permute-start(f32[48,128]{1,0:T(8,128)S(1)} %get-tuple-element.63), channel_id=1, source_target_pairs={{1,2},{2,1},{5,6},{6,5},{9,10},{10,9},{13,14},{14,13},{17,18},{18,... | collective-permute-start | bytes 73736 | tf_op jit(solution)/shard_map/ppermute | solution.py:550
  21.2 0.0 copy-start.6
  21.3 2.1 %shard_map.145.omega_ref = f32[180,8,128]{2,1,0:T(8,128)S(1)} custom-call(s32[8,64]{1,0:T(8,128)S(1)} %get-tuple-element.64.code_ref, f32[256,128]{1,0:T(8,128)S(1)} %get-tuple-element.65.table_ref, f32[180,8,128]{2,1,0:T(8,128)S(1)} %shard_map.143.rest_0_), custom_call_target="tpu_custom_call", output_to_operand_aliasing={{}: (2, {})} | custom-call | flops 2000000 | bytes 200000 | tf_op jit(solution)/shard_map/pallas_call | solution.py:115
  23.3 0.0 collective-permute-done.4.low_ref
  23.3 0.0 collective-permute-done.5.high_ref
  23.4 0.0 copy-done
  23.4 0.0 copy-done.1
  23.4 0.0 copy-done.4
  23.4 0.0 copy-done.6
  23.4 0.8 %shard_map.146 = (f32[8,16,128]{2,1,0:T(8,128)S(1)}, f32[8,16,128]{2,1,0:T(8,128)S(1)}, f32[8,16,128]{2,1,0:T(8,128)S(1)}, f32[16,128]{1,0:T(8,128)S(1)}, f32[16...) custom-call(f32[8,32,128]{2,1,0:T(8,128)S(1)} %get-tuple-element.53.v_ref, f32[16,128]{1,0:T(8,128)S(1)} %get-tuple-element.54.g_ref, ...), custom_call_target="tpu_custom_call" | custom-call | flops 2000000 | bytes 200000 | tf_op jit(solution)/shard_map/pallas_call | solution.py:115
  24.2 0.7 %collective-permute-start.6 = (f32[16,128]{1,0:T(8,128)S(1)}, f32[16,128]{1,0:T(8,128)S(1)}, u32[]{:S(2)}, u32[]{:S(2)}) collective-permute-start(f32[16,128]{1,0:T(8,128)S(1)} %get-tuple-element.72), channel_id=1, source_target_pairs={{32,64},{96,128},{160,192},{224,256},{288,320},{352,384},{416,448}... | collective-permute-start | bytes 24584 | tf_op jit(solution)/shard_map/ppermute | solution.py:550
  24.8 7.6 %collective-permute-start.7 = (f32[16,128]{1,0:T(8,128)S(1)}, f32[16,128]{1,0:T(8,128)S(1)}, u32[]{:S(2)}, u32[]{:S(2)}) collective-permute-start(f32[16,128]{1,0:T(8,128)S(1)} %get-tuple-element.73), channel_id=1, source_target_pairs={{0,32},{64,96},{128,160},{192,224},{256,288},{320,352},{384,416},{... | collective-permute-start | bytes 24584 | tf_op jit(solution)/shard_map/ppermute | solution.py:550
  32.5 0.4 shard_map.147.pre_ref
  32.9 0.0 collective-permute-done.6.low_ref
  32.9 0.6 collective-permute-done.7.high_ref
  33.5 0.4 shard_map.148
  33.9 12.6 %all_to_all.10 = f32[32,1,128]{2,1,0:T(1,128)S(1)} all-to-all(f32[32,1,128]{2,1,0:T(1,128)S(1)} %bitcast.23), channel_id=1, replica_groups={{22,23,24,25,26,27,28,29,30,31,0,1,2,3,4,5,6,7,8,9,10,11,12,13,14,15,16..., dimensions={0} | all-to-all | bytes 32768 | tf_op jit(solution)/shard_map/all_to_all | solution.py:563
  46.5 0.1 shard_map.149
  46.6 16.7 %all_to_all.11 = f32[16,1,128]{2,1,0:T(1,128)S(1)} all-to-all(f32[16,1,128]{2,1,0:T(1,128)S(1)} %bitcast.21), channel_id=1, replica_groups={{256,288,320,352,384,416,448,480,0,32,64,96,128,160,192,224},{257,289,3..., dimensions={0} | all-to-all | bytes 16384 | tf_op jit(solution)/shard_map/all_to_all | solution.py:563
  63.3 1.3 %shard_map.150 = (f32[8,16,128]{2,1,0:T(8,128)}, f32[3,32,128]{2,1,0:T(8,128)}) custom-call(f32[16,128]{1,0:T(8,128)S(1)} %bitcast.20, f32[8,16,128]{2,1,0:T(8,128)S(1)} %get-tuple-element.69.v0_ref, f32[8,16,128]{2,1,0:T(8,128)S(1)} %get-tuple-element.77.v1_ref, f32[3,32,128]{2,1,0:T(8,128)S(1)} %bitcast.18, f32[32,128]{1,0:T(8,128)S(1)} %get-tuple-element.78.store_ref, ...), custom_call_target="tpu_custom_call" | custom-call | flops 2000000 | bytes 200000 | tf_op jit(solution)/shard_map/pallas_call | solution.py:115
  (1 shorter events, 0.0 us)
Async XLA Ops:
  0.6 9.9 %copy-start.3 = (f32[8,16,128]{2,1,0:T(8,128)S(1)}, f32[8,16,128]{2,1,0:T(8,128)}, u32[]{:S(2)}) copy-start(f32[8,16,128]{2,1,0:T(8,128)} %f_ref.1) | copy-start | bytes 196612
  1.4 8.1 %copy-start.7 = (f32[4,1,2,16]{3,2,1,0:T(2,128)S(1)}, f32[4,1,2,16]{3,2,1,0:T(2,128)}, u32[]{:S(2)}) copy-start(f32[4,1,2,16]{3,2,1,0:T(2,128)} %param.14) | copy-start | bytes 1540
  1.4 8.2 %collective-permute-start.1 = (f32[16,128]{1,0:T(8,128)S(1)}, f32[16,128]{1,0:T(8,128)S(1)}, u32[]{:S(2)}, u32[]{:S(2)}) collective-permute-start(f32[16,128]{1,0:T(8,128)S(1)} %get-tuple-element.88), channel_id=1, source_target_pairs={{32,64},{96,128},{160,192},{224,256},{288,320},{352,384},{416,448}... | collective-permute-start | bytes 24584 | tf_op jit(solution)/shard_map/ppermute | solution.py:550
  2.2 8.3 %collective-permute-start = (f32[16,128]{1,0:T(8,128)S(1)}, f32[16,128]{1,0:T(8,128)S(1)}, u32[]{:S(2)}, u32[]{:S(2)}) collective-permute-start(f32[16,128]{1,0:T(8,128)S(1)} %get-tuple-element.89), channel_id=1, source_target_pairs={{0,32},{64,96},{128,160},{192,224},{256,288},{320,352},{384,416},{... | collective-permute-start | bytes 24584 | tf_op jit(solution)/shard_map/ppermute | solution.py:550
  9.6 5.2 %copy-start.2 = (f32[1,3,4096]{2,0,1:T(1,128)S(1)}, f32[1,3,4096]{2,0,1:T(1,128)}, u32[]{:S(2)}) copy-start(f32[1,3,4096]{2,0,1:T(1,128)} %param.19) | copy-start | bytes 147460
  10.5 4.3 %copy-start.5 = (f32[1,4096]{1,0:T(1,128)S(1)}, f32[1,4096]{1,0:T(1,128)}, u32[]{:S(2)}) copy-start(f32[1,4096]{1,0:T(1,128)} %param.18) | copy-start | bytes 49156
  10.5 4.2 %copy-start.9 = (f32[4,4]{1,0:T(4,128)S(1)}, f32[4,4]{1,0:T(4,128)}, u32[]{:S(2)}) copy-start(f32[4,4]{1,0:T(4,128)} %inverse_ref.1) | copy-start | bytes 196
  10.5 4.2 %copy-start.8 = (f32[6,4]{0,1:T(4,128)S(1)}, f32[6,4]{0,1:T(4,128)}, u32[]{:S(2)}) copy-start(f32[6,4]{0,1:T(4,128)} %param.20) | copy-start | bytes 292
  10.5 4.2 %copy-start.10 = (s32[1,64]{1,0:T(1,128)S(1)}, s32[1,64]{1,0:T(1,128)}, u32[]{:S(2)}) copy-start(s32[1,64]{1,0:T(1,128)} %elem_ref.1) | copy-start | bytes 772
  10.6 4.2 %copy-start.11 = (s32[1,64]{1,0:T(1,128)S(1)}, s32[1,64]{1,0:T(1,128)}, u32[]{:S(2)}) copy-start(s32[1,64]{1,0:T(1,128)} %face_ref.1) | copy-start | bytes 772
  10.6 4.2 %copy-start.12 = (s32[1,64]{1,0:T(1,128)S(1)}, s32[1,64]{1,0:T(1,128)}, u32[]{:S(2)}) copy-start(s32[1,64]{1,0:T(1,128)} %stores_ref.1) | copy-start | bytes 772
  10.6 5.4 %collective-permute-start.2 = (f32[72,128]{1,0:T(8,128)S(1)}, f32[72,128]{1,0:T(8,128)S(1)}, u32[]{:S(2)}, u32[]{:S(2)}) collective-permute-start(f32[72,128]{1,0:T(8,128)S(1)} %get-tuple-element.45), channel_id=1, source_target_pairs={{0,4},{4,8},{8,12},{12,16},{16,20},{20,24},{24,28},{28,0},{1,5},{5... | collective-permute-start | bytes 110600 | tf_op jit(solution)/shard_map/ppermute | solution.py:545
  13.6 3.4 %collective-permute-start.3 = (f32[72,128]{1,0:T(8,128)S(1)}, f32[72,128]{1,0:T(8,128)S(1)}, u32[]{:S(2)}, u32[]{:S(2)}) collective-permute-start(f32[72,128]{1,0:T(8,128)S(1)} %get-tuple-element.46), channel_id=1, source_target_pairs={{0,28},{4,0},{8,4},{12,8},{16,12},{20,16},{24,20},{28,24},{1,29},{... | collective-permute-start | bytes 110600 | tf_op jit(solution)/shard_map/ppermute | solution.py:545
  17.3 6.1 %copy-start = (f32[256,256]{1,0:T(8,128)S(1)}, f32[256,256]{1,0:T(8,128)}, u32[]{:S(2)}) copy-start(f32[256,256]{1,0:T(8,128)} %constant.40.clone.kr_ref) | copy-start | bytes 786436
  17.3 6.1 %copy-start.1 = (f32[128,128]{1,0:T(8,128)S(1)}, f32[128,128]{1,0:T(8,128)}, u32[]{:S(2)}) copy-start(f32[128,128]{1,0:T(8,128)} %constant.38.clone.kk_ref) | copy-start | bytes 196612
  17.3 6.1 %copy-start.4 = (f32[128,128]{1,0:T(8,128)S(1)}, f32[128,128]{1,0:T(8,128)}, u32[]{:S(2)}) copy-start(f32[128,128]{1,0:T(8,128)} %constant.39.clone.ki_ref) | copy-start | bytes 196612
  17.3 6.0 %collective-permute-start.4 = (f32[48,128]{1,0:T(8,128)S(1)}, f32[48,128]{1,0:T(8,128)S(1)}, u32[]{:S(2)}, u32[]{:S(2)}) collective-permute-start(f32[48,128]{1,0:T(8,128)S(1)} %get-tuple-element.62), channel_id=1, source_target_pairs={{0,1},{2,3},{1,0},{3,2},{4,5},{6,7},{5,4},{7,6},{8,9},{10,11},{9,8... | collective-permute-start | bytes 73736 | tf_op jit(solution)/shard_map/ppermute | solution.py:550
  20.6 2.8 %collective-permute-start.5 = (f32[48,128]{1,0:T(8,128)S(1)}, f32[48,128]{1,0:T(8,128)S(1)}, u32[]{:S(2)}, u32[]{:S(2)}) collective-permute-start(f32[48,128]{1,0:T(8,128)S(1)} %get-tuple-element.63), channel_id=1, source_target_pairs={{1,2},{2,1},{5,6},{6,5},{9,10},{10,9},{13,14},{14,13},{17,18},{18,... | collective-permute-start | bytes 73736 | tf_op jit(solution)/shard_map/ppermute | solution.py:550
  21.2 2.1 %copy-start.6 = (f32[24,128]{1,0:T(8,128)S(1)}, f32[24,128]{1,0:T(8,128)}, u32[]{:S(2)}) copy-start(f32[24,128]{1,0:T(8,128)} %constant.41.clone.w_ref) | copy-start | bytes 36868
  24.2 8.7 %collective-permute-start.6 = (f32[16,128]{1,0:T(8,128)S(1)}, f32[16,128]{1,0:T(8,128)S(1)}, u32[]{:S(2)}, u32[]{:S(2)}) collective-permute-start(f32[16,128]{1,0:T(8,128)S(1)} %get-tuple-element.72), channel_id=1, source_target_pairs={{32,64},{96,128},{160,192},{224,256},{288,320},{352,384},{416,448}... | collective-permute-start | bytes 24584 | tf_op jit(solution)/shard_map/ppermute | solution.py:550
  24.8 8.7 %collective-permute-start.7 = (f32[16,128]{1,0:T(8,128)S(1)}, f32[16,128]{1,0:T(8,128)S(1)}, u32[]{:S(2)}, u32[]{:S(2)}) collective-permute-start(f32[16,128]{1,0:T(8,128)S(1)} %get-tuple-element.73), channel_id=1, source_target_pairs={{0,32},{64,96},{128,160},{192,224},{256,288},{320,352},{384,416},{... | collective-permute-start | bytes 24584 | tf_op jit(solution)/shard_map/ppermute | solution.py:550
